TPU v7x, 32 devices: a whole 2x2x4 slice. The times are simulated.
32 devices in a mesh: seq: 8 (over z, y), chan: 4 (over x, core).
Axes of the slice: x: 2, y: 2, z: 4, core: 2. Of those that a mesh axis runs over, the one named last changes fastest.
Arguments:
- targets: int32 [8192], P('seq'), may hold values from 0 to 4
- resid: bfloat16 [8192, 2560], P('seq', 'chan'), may hold values from -6 to 6
- w_gate_in: bfloat16 [2560, 2560], P('seq', 'chan'), may hold values from -0.125 to 0.125
- w_x_in: bfloat16 [2560, 2560], P('seq', 'chan'), may hold values from -0.125 to 0.125
- conv_weight: float32 [4, 2560], P(None, 'chan'), may hold values from -3 to 3
- conv_bias: float32 [2560], P('chan'), may hold values from -3 to 3
- skip_d: float32 [40], P('chan'), may hold values from 0.5 to 2
- norm_gain: float32 [2560], P('chan'), may hold values from 0.1 to 1.9
- w_out: bfloat16 [2560, 2560], P('seq', 'chan'), may hold values from -0.125 to 0.125
- w_head: bfloat16 [2560, 16], P('chan'), may hold values from -0.375 to 0.375
Outputs:
- new_resid: bfloat16 [8192, 2560], P('seq', 'chan')
- grad_gate_in: float32 [2560, 2560], P('seq', 'chan')
- grad_x_in: float32 [2560, 2560], P('seq', 'chan')
- grad_out: float32 [2560, 2560], P('seq', 'chan')
- grad_head: float32 [2560, 16], P('chan')
- grad_conv_weight: float32 [4, 2560], P(None, 'chan')
- grad_conv_bias: float32 [2560], P('chan')
- grad_skip: float32 [40], P('chan')
- grad_gain: float32 [2560], P('chan')
All inputs are finite; a program needn't handle non-finite values.
Results may differ from a plain program's by a relative error of at most 0.035.
Values may be sent and summed in bfloat16 or wider, within the bound.
No kernel may reach another device: no remote copies, remote signals or barrier semaphores. Data moves between devices by JAX's collectives and lax.ppermute only.
A program may use at most 128 MiB of HBM per device.

v0:
```python
import functools

import jax
import jax.numpy as jnp
from jax import lax
from jax.experimental import pallas as pl
from jax.experimental.pallas import tpu as pltpu
from jax.sharding import PartitionSpec as P

HEADDIM = 64
KERNEL = 4
VOCAB = 16
INNER = 2560
f32 = jnp.float32
bf16 = jnp.bfloat16
HI = lax.Precision.HIGHEST
LIGHT = pl.CostEstimate(flops=1, bytes_accessed=1, transcendentals=0)
MIB = 1024 * 1024
PROJ_VMEM = 58 * MIB


def slope(value, sig):
    return sig * (1.0 + value * (1.0 - sig))


def after(value, *others):
    return lax.optimization_barrier((value,) + others)[0]


def flip(value, axis, bit):
    return lax.ppermute(value, axis, [(i, i ^ bit) for i in range(lax.axis_size(axis))])


def xor_sum(value, axis):
    bit = 1
    while bit < lax.axis_size(axis):
        value = value + flip(value, axis, bit)
        bit *= 2
    return value


def xor_gather(value, axis, least=1):
    size = lax.axis_size(axis)
    blocks = {0: value}
    bit = size // 2
    while bit >= least:
        for j in list(blocks):
            blocks[j | bit] = flip(blocks[j], axis, bit)
        bit //= 2
    return [blocks[j] for j in range(0, size, least)]


def seq_factors():
    slow = 4
    return slow, lax.axis_size("seq") // slow


def move_slow(value, by):
    slow, fast = seq_factors()
    pairs = [(a * fast + b, ((a + by) % slow) * fast + b) for a in range(slow) for b in range(fast)]
    return lax.ppermute(value, "seq", pairs)


def move_fast(value, by):
    slow, fast = seq_factors()
    pairs = [(a * fast + b, a * fast + (b + by) % fast) for a in range(slow) for b in range(fast)]
    return lax.ppermute(value, "seq", pairs)


def shifted(array, by):
    length = lax.axis_size("seq")
    return lax.ppermute(array, "seq", [(i, i + by) for i in range(length) if 0 <= i + by < length])


def sync(*groups):
    flat = lax.optimization_barrier(tuple(value for group in groups for value in group))
    out, at = [], 0
    for group in groups:
        out.append(list(flat[at : at + len(group)]))
        at += len(group)
    return out


def to_fast(block):
    return [move_fast(block, j) for j in range(1, seq_factors()[1])]


def slow_total(own, came):
    even, odd = own + came[1], came[0] + came[2]
    return even + odd


def gather_sources():
    slow, fast = seq_factors()
    me = lax.axis_index("seq")
    a, b = me // fast, me % fast
    return [((a - k) % slow) * fast + (b - j) % fast for k in range(slow) for j in range(fast)]


def picked(pieces, sources, wanted):
    return sum(jnp.where(source == wanted, piece, 0.0) for source, piece in zip(sources, pieces))


def turn_kernel(n_feat, *refs):
    for j in range(n_feat):
        refs[n_feat][j] = refs[j][...].T


def turned(feats):
    tok, depth = feats[0].shape
    n_feat = len(feats)
    tile = 256
    return pl.pallas_call(
        functools.partial(turn_kernel, n_feat),
        out_shape=jax.ShapeDtypeStruct((n_feat, depth, tok), bf16),
        grid=(tok // tile,),
        in_specs=[pl.BlockSpec((tile, depth), lambda i: (i, 0))] * n_feat,
        out_specs=pl.BlockSpec((n_feat, depth, tile), lambda i: (0, 0, i)),
        compiler_params=pltpu.CompilerParams(vmem_limit_bytes=PROJ_VMEM),
        cost_estimate=LIGHT,
    )(*feats)


def proj_kernel(n_feat, counts, idx, *refs):
    feats = refs[:n_feat]
    shards = refs[n_feat : n_feat + len(counts)]
    out = refs[n_feat + len(counts)]
    fbuf, wbuf, fsem, wsem = refs[n_feat + len(counts) + 1 :]
    rows = shards[0].shape[1]
    tok, depth = feats[0].shape
    joined = len(fbuf.shape) == 2
    n_tile = fsem.shape[1]
    tile = tok // n_tile

    def f_copy(j, t):
        at = pl.ds(t * tile, tile)
        to = fbuf.at[at, pl.ds(j * depth, depth)] if joined else fbuf.at[j, at]
        return pltpu.make_async_copy(feats[j].at[at], to, fsem.at[j, t])

    copies = []
    for shard, places in zip(shards, counts):
        for i, s in enumerate(places):
            place = pl.ds(pl.multiple_of(idx[n_feat + s] * rows, 16), rows)
            copies.append(pltpu.make_async_copy(shard.at[i], wbuf.at[place], wsem.at[s]))
    for copy in copies:
        copy.start()
    for t in range(n_tile):
        for j in range(n_feat):
            f_copy(j, t).start()
    for copy in copies:
        copy.wait()
    for t in range(n_tile):
        at = pl.ds(t * tile, tile)
        for j in range(n_feat):
            f_copy(j, t).wait()
        if joined:
            total = jnp.dot(fbuf[at, :], wbuf[...], preferred_element_type=f32)
        else:
            total = jnp.zeros((tile, wbuf.shape[1]), f32)
            for j in range(n_feat):
                part = wbuf[j * depth : (j + 1) * depth, :]
                total += jnp.dot(fbuf[j, at, :], part, preferred_element_type=f32)
        out[at, :] = total.astype(out.dtype)


def proj(feats, shards, counts, idx):
    tok, depth = feats[0].shape
    rows, cols = shards[0].shape[1:]
    n_feat, n_shard = len(feats), sum(len(places) for places in counts)
    any_spec = pl.BlockSpec(memory_space=pltpu.HBM)
    return pl.pallas_call(
        functools.partial(proj_kernel, n_feat, counts),
        out_shape=jax.ShapeDtypeStruct((tok, cols), bf16),
        in_specs=[pl.BlockSpec(memory_space=pltpu.SMEM)] + [any_spec] * (n_feat + len(shards)),
        out_specs=pl.BlockSpec(memory_space=pltpu.VMEM),
        scratch_shapes=[
            pltpu.VMEM((tok, n_feat * depth) if depth % 128 == 0 else (n_feat, tok, depth), bf16),
            pltpu.VMEM((n_shard * rows, cols), bf16),
            pltpu.SemaphoreType.DMA((n_feat, 2)),
            pltpu.SemaphoreType.DMA((n_shard,)),
        ],
        compiler_params=pltpu.CompilerParams(vmem_limit_bytes=PROJ_VMEM),
        cost_estimate=LIGHT,
    )(idx, *feats, *shards)


def group_kernel(n_feat, n_fast, n_use, first, ats, idx, *refs):
    part = None if first else refs[0]
    refs = refs if first else refs[1:]
    n_shard, n_block = n_fast * len(ats), n_use * len(ats)
    feats = refs[:n_feat]
    shards = refs[n_feat : n_feat + n_shard]
    outs = refs[n_feat + n_shard : -4]
    fbuf, wbuf, fsem, wsem = refs[-4:]
    count, rows = shards[0].shape[:2]
    depth = fbuf.shape[2]
    tile = outs[0].shape[-2]
    step = pl.program_id(0)

    def w_copy(i):
        at = ats[i // n_fast] + n_use + i % n_fast
        place = pl.multiple_of((i // n_fast * n_fast + idx[at]) * rows, 16)
        return pltpu.make_async_copy(shards[i], wbuf.at[:, pl.ds(place, rows)], wsem.at[i])

    @pl.when(step == 0)
    def _():
        for m in range(n_block):
            for j in range(n_feat):

                @pl.when(idx[ats[m // n_use] + m % n_use] == j)
                def _():
                    pltpu.make_async_copy(feats[j], fbuf.at[m], fsem.at[m]).start()

        for i in range(n_shard):
            w_copy(i).start()
        for i in range(n_shard):
            w_copy(i).wait()
        for m in range(n_block):
            pltpu.make_async_copy(feats[0], fbuf.at[m], fsem.at[m]).wait()

    here = pl.ds(pl.multiple_of(step * tile, tile), tile)
    for w in range(count):
        total = None if first else part[w]
        for m in range(n_block):
            rhs = wbuf[w, m * depth : (m + 1) * depth, :]
            term = jnp.dot(fbuf[m, here, :], rhs, preferred_element_type=f32)
            total = term if total is None else total + term
        if len(outs) == 1:
            outs[0][w] = total
        else:
            outs[w][...] = total.astype(bf16)


def add_groups(part, feats, shards, idx, ats, n_use, final):
    count, rows, cols = shards[0].shape
    tok, depth = feats[0].shape
    n_feat, n_shard, n_block = len(feats), len(shards), n_use * len(ats)
    tile = tok // 4
    any_spec = pl.BlockSpec(memory_space=pltpu.HBM)
    whole = pl.BlockSpec((count, tile, cols), lambda i, idx: (0, i, 0))
    if final:
        out_shape = [jax.ShapeDtypeStruct((tok, cols), bf16)] * count
        out_specs = [pl.BlockSpec((tile, cols), lambda i, idx: (i, 0))] * count
    else:
        out_shape = [jax.ShapeDtypeStruct((count, tok, cols), f32)]
        out_specs = [whole]
    parts = [] if part is None else [part]
    return pl.pallas_call(
        functools.partial(group_kernel, n_feat, n_shard // len(ats), n_use, part is None, ats),
        out_shape=out_shape,
        grid_spec=pltpu.PrefetchScalarGridSpec(
            num_scalar_prefetch=1,
            grid=(tok // tile,),
            in_specs=[whole] * len(parts) + [any_spec] * (n_feat + n_shard),
            out_specs=out_specs,
            scratch_shapes=[
                pltpu.VMEM((n_block, tok, depth), bf16),
                pltpu.VMEM((count, n_shard * rows, cols), bf16),
                pltpu.SemaphoreType.DMA((n_block,)),
                pltpu.SemaphoreType.DMA((n_shard,)),
            ],
        ),
        compiler_params=pltpu.CompilerParams(vmem_limit_bytes=PROJ_VMEM),
        cost_estimate=LIGHT,
    )(idx, *parts, *feats, *shards)


def blocks_kernel(sizes, idx, lhs, rhs, *outs):
    at = 0
    for out, size in zip(outs, sizes):
        for i in range(size):

            @pl.when(pl.program_id(0) == at)
            def _():
                total = jnp.dot(lhs[0], rhs[...], preferred_element_type=f32)
                out[i] = total.astype(bf16)

            at += 1


def block_grads(feat_t, rhs, places, begin, sizes, rows):
    tok = feat_t.shape[2]
    cols = rhs.shape[1]

    def place(i, idx):
        return (idx[2 * (begin + i)], idx[2 * (begin + i) + 1], 0)

    return pl.pallas_call(
        functools.partial(blocks_kernel, sizes),
        out_shape=[jax.ShapeDtypeStruct((size, rows, cols), bf16) for size in sizes],
        grid_spec=pltpu.PrefetchScalarGridSpec(
            num_scalar_prefetch=1,
            grid=(sum(sizes),),
            in_specs=[
                pl.BlockSpec((1, rows, tok), place),
                pl.BlockSpec((tok, cols), lambda i, idx: (0, 0)),
            ],
            out_specs=[
                pl.BlockSpec((size, rows, cols), lambda i, idx: (0, 0, 0)) for size in sizes
            ],
        ),
        compiler_params=pltpu.CompilerParams(vmem_limit_bytes=16 * MIB),
        cost_estimate=LIGHT,
    )(places, feat_t, rhs)


def dest_places(keys, rows, depth):
    slow, fast = seq_factors()
    me = lax.axis_index("seq")
    per_feat = depth // rows
    out = []
    for k, j in keys:
        dest = ((me // fast + k) % slow) * fast + (me % fast + j) % fast
        out += [(dest // per_feat) ^ lax.axis_index("chan"), dest % per_feat]
    return out


def slow_order():
    return [1, 3, 2, 0]


def per_device(
    targets, resid, w_gate_in, w_x_in, conv_weight, conv_bias, skip_d, norm_gain, w_out, w_head
):
    tok_rows = resid.shape[0]
    seq_count = lax.axis_size("seq")
    chan_count = lax.axis_size("chan")
    chan = lax.axis_index("chan")
    local_inner = w_gate_in.shape[1]
    w_rows = w_out.shape[0]
    halo = KERNEL - 1

    sources = gather_sources()
    slow, fast = seq_factors()
    order = slow_order()
    first, second = order[:2], order[2:]
    far = [(k, j) for pair in (first, second) for j in range(1, fast) for k in pair]
    near = [(k, 0) for k in order]
    per_feat = resid.shape[1] // w_rows
    idx = [chan ^ j for j in range(chan_count)]
    idx += [((i // per_feat) ^ chan) * per_feat + i % per_feat for i in sources]
    idx += dest_places(far + near, w_rows, resid.shape[1])
    n_idx = chan_count + seq_count
    n_use = fast // per_feat
    group_at = []
    for k in range(slow):
        group_at.append(len(idx))
        mine = sources[k * fast : (k + 1) * fast]
        idx += [(mine[0] // fast * n_use + m) ^ chan for m in range(n_use)]
        idx += [source % fast for source in mine]
    idx = jnp.concatenate([jnp.reshape(i, (1,)) for i in idx]).astype(jnp.int32)

    now = jnp.stack([w_gate_in, w_x_in])
    shards = []
    extra = [idx]
    for k in range(slow - 1):
        shards.append(now)
        came = [move_slow(now, 1)]
        came_fast = to_fast(now)
        if k == 0:
            feats = xor_gather(resid, "chan", 2)
        if k == 1:
            head_t = after(w_head.T, now)
            part_m = lax.dot_general(
                head_t, w_out, (((1,), (1,)), ((), ())), preferred_element_type=f32
            )
            part_r = lax.dot_general(
                head_t, resid, (((1,), (1,)), ((), ())), preferred_element_type=f32
            )
            early = jnp.concatenate([part_m, part_r], axis=1)
            early = early + flip(early, "chan", 1)
            extra = [early] + feats
        if k == 2:
            bit = 2
            while bit < chan_count:
                early = early + flip(early, "chan", bit)
                bit *= 2
            full = []
            for block in feats:
                full += [block, flip(block, "chan", 1)]
            feats = full
            feat_t = turned(feats)
            part = add_groups(
                None, feats, shards[: 2 * fast], idx, group_at[:2], n_use, False
            )[0]
            own_m, resid_logits = early[:, :w_rows], early[:, w_rows:]
            own_m = after(own_m, part)
            pair_m = jnp.concatenate([own_m] + to_fast(own_m), axis=1)
            extra = [pair_m, resid_logits, feat_t, part] + feats
        came, came_fast, extra = sync(came, came_fast, extra)
        now = came[0]
        shards += came_fast
        if k == 0:
            idx = extra[0]
        if k == 1:
            early, feats = extra[0], extra[1:]
    pair_m, resid_logits, feat_t, part = extra[:4]
    feats = extra[4:]
    shards.append(now)
    came_fast = to_fast(now)
    moved_m = [move_slow(pair_m, k) for k in range(1, slow)]
    out_first = after(w_out, now)
    out_pair = jnp.stack([out_first, move_slow(out_first, 1)])
    came_fast, moved_m, held = sync(came_fast, moved_m, [now, out_pair])
    now, out_pair = held
    out_pair_fast = to_fast(out_pair)
    out_far = [move_slow(out_pair[1], 1), move_slow(out_first, 3)]
    last = shards[2 * fast : 3 * fast] + [now] + came_fast
    gate_pre, x_pre = add_groups(part, feats, last, idx, group_at[2:], n_use, True)

    all_m = jnp.concatenate([pair_m] + moved_m, axis=1)
    per_chan = per_feat
    pieces = [all_m[:, i * w_rows : (i + 1) * w_rows] for i in range(seq_count)]
    m_loc = jnp.concatenate(
        [picked(pieces, sources, chan * per_chan + i) for i in range(per_chan)], axis=1
    )
    gain_m = m_loc * norm_gain[None, :]

    before = shifted(x_pre[tok_rows - halo :], 1)
    padded = jnp.concatenate([before, x_pre], axis=0).astype(f32)
    conv_out = jnp.zeros((tok_rows, local_inner), f32) + conv_bias
    for offset in range(KERNEL):
        conv_out = conv_out + conv_weight[offset] * padded[offset : offset + tok_rows]
    sig_conv = jax.nn.sigmoid(conv_out)
    active = conv_out * sig_conv
    gate_f32 = gate_pre.astype(f32)
    sig_gate = jax.nn.sigmoid(gate_f32)
    silu_gate = gate_f32 * sig_gate
    head_scale = jnp.repeat(skip_d, HEADDIM)
    gated = active * head_scale * silu_gate
    z_part = lax.dot_general(
        gain_m, gated, (((1,), (1,)), ((), ())), precision=HI, preferred_element_type=f32
    )
    sq_part = jnp.sum(gated * gated, axis=1)
    sums = jnp.concatenate([z_part, jnp.broadcast_to(sq_part[None], (8, tok_rows))])
    held, out_pair_fast, out_far = sync([sums], out_pair_fast, out_far)
    sums = xor_sum(held[0], "chan")
    out_far = jnp.stack(out_far)
    out_far_fast = to_fast(out_far)
    normed = (gated * norm_gain).astype(bf16)
    normed_x = xor_gather(after(normed, sums), "chan", 2)
    z_all = sums[:VOCAB]
    inverse = lax.rsqrt(sums[VOCAB] / INNER + 1e-05)
    raised = jnp.exp(resid_logits + inverse[None] * z_all)
    probs = raised / jnp.sum(raised, axis=0, keepdims=True)
    onehot = (targets[None, :] == jnp.arange(VOCAB, dtype=jnp.int32)[:, None]).astype(f32)
    loss_weight = 4.0 / jnp.sqrt(jnp.asarray(tok_rows * seq_count, f32))
    dlogit = (probs - onehot) * loss_weight
    dot_gn = jnp.sum(dlogit * z_all, axis=0)
    dnormed = lax.dot_general(
        dlogit, m_loc, (((0,), (0,)), ((), ())), precision=HI, preferred_element_type=f32
    )
    inv = inverse[:, None]
    dgated = inv * norm_gain * dnormed - gated * (inverse**3 * dot_gn / INNER)[:, None]
    gain_local = jnp.sum(dnormed * gated * inv, axis=0)
    skip_local = jnp.sum(dgated * active * silu_gate, axis=0)
    dgate = (dgated * active * head_scale * slope(gate_f32, sig_gate)).astype(bf16)
    dconv = dgated * head_scale * silu_gate * slope(conv_out, sig_conv)
    bias_local = jnp.sum(dconv, axis=0)
    taps_local = jnp.stack(
        [jnp.sum(dconv * padded[offset : offset + tok_rows], axis=0) for offset in range(KERNEL)]
    )
    future = shifted(dconv[:halo], -1)

    def far_grads(rhs):
        sizes = [2] * (2 * fast - 2)
        out = block_grads(feat_t, rhs, idx, n_idx // 2, sizes, w_rows)
        return out[: fast - 1], out[fast - 1 :]

    def near_grads(rhs):
        return block_grads(feat_t, rhs, idx, n_idx // 2 + len(far), [1] * slow, w_rows)

    def send_fast(blocks):
        return [move_fast(block, j) for j, block in enumerate(blocks, 1)]

    def total_of(own, came, i):
        return own[0].astype(f32) + sum(block[i].astype(f32) for block in came)

    def send_slow(own, came, i, k):
        return move_slow(total_of(own, came, i).astype(bf16), k)

    far_gate = far_grads(dgate)
    gate_first, gate_second, held, out_far_fast = sync(
        *far_gate, [future, dconv, dlogit, dgate], out_far_fast
    )
    future, dconv, dlogit, dgate = held

    came = send_fast(gate_first)
    dpadded = jnp.concatenate([dconv, future], axis=0)
    dx_sum = jnp.zeros((tok_rows, local_inner), f32)
    for offset in range(KERNEL):
        dx_sum = (
            dx_sum + conv_weight[offset] * dpadded[halo - offset : halo - offset + tok_rows]
        )
    dx_pre = dx_sum.astype(bf16)
    out_local = lax.dot_general(
        dlogit, gated * inv * norm_gain, (((1,), (0,)), ((), ())), precision=HI
    )
    mid = jnp.concatenate(
        [out_local, taps_local, bias_local[None], skip_local[None], gain_local[None]], 0
    )
    gate_own = near_grads(dgate)
    x_first, x_second = far_grads(dx_pre)
    mid = after(mid, x_first[0], gate_own[0])
    mid_came = [move_slow(mid, k) for k in range(1, slow)]
    gate_first, gate_second, x_first, x_second, gate_own, normed_x, mid_came, held = sync(
        came, gate_second, x_first, x_second, gate_own, normed_x, mid_came, [dx_pre, mid]
    )
    dx_pre, mid = held
    mid = slow_total(mid, mid_came)

    came = send_fast(gate_second)
    gate_slow = [send_slow(gate_own[i], gate_first, i, first[i]) for i in range(2)]
    normed_all = []
    for block in normed_x:
        normed_all += [block, flip(block, "chan", 1)]
    out_shards = [out_pair] + out_pair_fast + [out_far] + out_far_fast
    counts = [[k * fast + j for k in ks] for ks in ((0, 1), (2, 3)) for j in range(fast)]
    raw = proj(normed_all, out_shards, counts, idx)
    gate_second, gate_slow, x_first, x_second, held = sync(
        came, gate_slow, x_first, x_second, [raw, dx_pre]
    )
    raw, dx_pre = held

    came = send_fast(x_first)
    gate_slow.append(send_slow(gate_own[2], gate_second, 0, second[0]))
    x_own = near_grads(dx_pre)
    new_resid = (resid.astype(f32) + inv * raw.astype(f32)).astype(bf16)
    head_local = lax.dot_general(
        dlogit, new_resid.astype(f32), (((1,), (0,)), ((), ())), precision=HI
    )
    mid_came = to_fast(after(mid, x_own[0]))
    head_local = after(head_local, x_own[0])
    head_came = [move_slow(head_local, k) for k in range(1, slow)]
    x_first, x_second, x_own, gate_slow, mid_came, head_came, held = sync(
        came, x_second, x_own, gate_slow, mid_came, head_came, [mid, head_local]
    )
    mid, head_local = held
    mid = mid + sum(mid_came)
    head_local = slow_total(head_local, head_came)

    came = send_fast(x_second)
    x_terms = [total_of(x_own[i], x_first, i).astype(bf16) for i in range(2)]
    x_slow = [move_slow(x_terms[i], first[i]) for i in range(2)]
    head_came = to_fast(after(head_local, *x_terms))
    g_pieces = xor_gather(after(mid[:VOCAB], *x_terms), "chan")
    x_second, x_slow, head_came, g_pieces = sync(came, x_slow, head_came, g_pieces)

    x_slow.append(send_slow(x_own[2], x_second, 0, second[0]))
    head_local = head_local + sum(head_came)
    grad_gate_in = total_of(gate_own[3], gate_second, 1) + sum(
        block.astype(f32) for block in gate_slow
    )
    grad_x_in = total_of(x_own[3], x_second, 1) + sum(block.astype(f32) for block in x_slow)
    grad_head = head_local.T
    seq = lax.axis_index("seq")
    g_chan = picked(g_pieces, [chan ^ j for j in range(chan_count)], seq // per_chan)
    g_rows = lax.dynamic_slice_in_dim(g_chan, (seq % per_chan) * w_rows, w_rows, 1)
    grad_out = lax.dot_general(
        g_rows, w_head.T.astype(f32), (((0,), (0,)), ((), ())), precision=HI
    )
    tail = mid[VOCAB:]
    grad_skip = tail[KERNEL + 1].reshape(-1, HEADDIM).sum(axis=1)
    return (
        new_resid,
        grad_gate_in,
        grad_x_in,
        grad_out,
        grad_head,
        tail[:KERNEL],
        tail[KERNEL],
        grad_skip,
        tail[KERNEL + 2],
    )


def solution(mesh):
    return jax.shard_map(
        per_device,
        mesh=mesh,
        in_specs=(
            P("seq"),
            P("seq", "chan"),
            P("seq", "chan"),
            P("seq", "chan"),
            P(None, "chan"),
            P("chan"),
            P("chan"),
            P("chan"),
            P("seq", "chan"),
            P("chan", None),
        ),
        out_specs=(
            P("seq", "chan"),
            P("seq", "chan"),
            P("seq", "chan"),
            P("seq", "chan"),
            P("chan", None),
            P(None, "chan"),
            P("chan"),
            P("chan"),
            P("chan"),
        ),
        check_vma=False,
    )
```

profile of v0, /device:TPU:0, one launch (start us, length us, event | category | flops | bytes accessed | tf_op | source)
XLA Modules:
  0.0 264.4 jit_solution(13548603306927433147)
XLA Ops:
  0.7 1.3 pad_maximum_fusion.refs_4_
  2.0 3.1 %collective-permute-start = (bf16[2,320,640]{2,1,0:T(8,128)(2,1)S(1)}, bf16[2,320,640]{2,1,0:T(8,128)(2,1)}, u32[]{:S(2)}, u32[]{:S(2)}) collective-permute-start(bf16[2,320,640]{2,1,0:T(8,128)(2,1)S(1)} %pad_maximum_fusion.refs_4_), channel_id=1, source_target_pairs={{0,8},{4,12},{8,16},{12,20},{16,24},{20,28},{24,0},{28,4},{1,9},{5... | collective-permute-start | bytes 2457608 | tf_op jit(solution)/shard_map/ppermute | solution.py:61
  5.1 1.5 collective-permute-start.1
  6.6 1.5 collective-permute-start.5
  8.8 16.7 %collective-permute-done.refs_6_ = bf16[2,320,640]{2,1,0:T(8,128)(2,1)} collective-permute-done((bf16[2,320,640]{2,1,0:T(8,128)(2,1)S(1)}, bf16[2,320,640]{2,1,0:T(8,128)(2,1)}, u32[]{:S(2)}, u32[]{:S(2)}) %collective-permute-start) | collective-permute-done | bytes 819232 | tf_op jit(solution)/shard_map/ppermute | solution.py:61
  26.5 1.5 collective-permute-start.3
  31.2 5.5 %collective-permute-done.5.refs_2_.refs_3_ = bf16[1024,640]{1,0:T(8,128)(2,1)S(1)} collective-permute-done((bf16[1024,640]{1,0:T(8,128)(2,1)}, bf16[1024,640]{1,0:T(8,128)(2,1)S(1)}, u32[]{:S(2)}, u32[]{:S(2)}) %collective-permute-start.5) | collective-permute-done | bytes 1310752 | tf_op jit(solution)/shard_map/ppermute | solution.py:31
  36.8 10.2 %collective-permute-done.2.refs_5_ = bf16[2,320,640]{2,1,0:T(8,128)(2,1)} collective-permute-done((bf16[2,320,640]{2,1,0:T(8,128)(2,1)}, bf16[2,320,640]{2,1,0:T(8,128)(2,1)}, u32[]{:S(2)}, u32[]{:S(2)}) %collective-permute-start.2) | collective-permute-done | bytes 819232 | tf_op jit(solution)/shard_map/ppermute | solution.py:61
  47.5 1.3 collective-permute-start.7
  48.8 1.5 collective-permute-start.8
  50.3 3.0 %collective-permute-done.8 = f32[16,1344]{1,0:T(8,128)S(1)} collective-permute-done((f32[16,1344]{1,0:T(8,128)S(1)}, f32[16,1344]{1,0:T(8,128)S(1)}, u32[]{:S(2)}, u32[]{:S(2)}) %collective-permute-start.8) | collective-permute-done | bytes 86048 | tf_op jit(solution)/shard_map/ppermute | solution.py:31
  55.6 10.0 %shard_map.169.refs_0_ = f32[2,1024,640]{2,1,0:T(8,128)} custom-call(s32[40]{0:T(128)} %concatenate.24.idx, bf16[1024,640]{1,0:T(8,128)(2,1)} %refs_1_, bf16[1024,640]{1,0:T(8,128)(2,1)} %copy-done.10, bf16[1024,640]{1,0:T(8,128)(2,1)} %copy-done.9, bf16[1024,640]{1,0:T(8,128)(2,1)} %copy-done.11, bf16[2,320,640]{2,1,0:T(8,128)(2,1)} %copy-done.15, ...), custom_call_target="tpu_custom_call" | custom-call | flops 1 | bytes 1 | tf_op jit(solution)/shard_map/pallas_call | solution.py:248
  66.5 5.9 %shard_map.170.lhs = bf16[4,640,1024]{2,1,0:T(8,128)(2,1)} custom-call(bf16[1024,640]{1,0:T(8,128)(2,1)} %refs_1_, bf16[1024,640]{1,0:T(8,128)(2,1)} %copy-done.10, bf16[1024,640]{1,0:T(8,128)(2,1)} %copy-done.9, bf16[1024,640]{1,0:T(8,128)(2,1)} %copy-done.11), custom_call_target="tpu_custom_call" | custom-call | flops 1 | bytes 1 | tf_op jit(solution)/shard_map/pallas_call | solution.py:113
  72.5 1.3 collective-permute-start.12
  74.7 2.2 collective-permute-start.13
  76.9 1.7 collective-permute-start.14
  78.6 2.8 %collective-permute-start.15 = (f32[16,640]{1,0:T(8,128)S(1)}, f32[16,640]{1,0:T(8,128)S(1)}, u32[]{:S(2)}, u32[]{:S(2)}) collective-permute-start(f32[16,640]{1,0:T(8,128)S(1)} %pad_maximum_fusion.5), channel_id=1, source_target_pairs={{0,24},{4,28},{8,0},{12,4},{16,8},{20,12},{24,16},{28,20},{1,25},{... | collective-permute-start | bytes 122888 | tf_op jit(solution)/shard_map/ppermute | solution.py:61
  81.4 6.7 %collective-permute-done.16 = bf16[320,640]{1,0:T(8,128)(2,1)S(1)} collective-permute-done((bf16[320,640]{1,0:T(8,128)(2,1)S(1)}, bf16[320,640]{1,0:T(8,128)(2,1)S(1)}, u32[]{:S(2)}, u32[]{:S(2)}) %collective-permute-start.16) | collective-permute-done | bytes 409632 | tf_op jit(solution)/shard_map/ppermute | solution.py:61
  88.2 1.6 collective-permute-start.20
  89.9 1.8 collective-permute-done.12.refs_8_
  93.0 11.1 %shard_map.171 = (bf16[1024,640]{1,0:T(8,128)(2,1)}, bf16[1024,640]{1,0:T(8,128)(2,1)}) custom-call(s32[40]{0:T(128)} %concatenate.24.idx, f32[2,1024,640]{2,1,0:T(8,128)} %shard_map.169.refs_0_, bf16[1024,640]{1,0:T(8,128)(2,1)} %refs_1_, bf16[1024,640]{1,0:T(8,128)(2,1)} %copy-done.10, bf16[1024,640]{1,0:T(8,128)(2,1)} %copy-done.9, ...), custom_call_target="tpu_custom_call" | custom-call | flops 1 | bytes 1 | tf_op jit(solution)/shard_map/pallas_call | solution.py:248
  105.0 2.7 %collective-permute-start.17 = (bf16[3,640]{1,0:T(4,128)(2,1)S(1)}, bf16[3,640]{1,0:T(4,128)(2,1)S(1)}, u32[]{:S(2)}, u32[]{:S(2)}) collective-permute-start(bf16[3,640]{1,0:T(4,128)(2,1)S(1)} %slice.141), channel_id=1, source_target_pairs={{0,4},{4,8},{8,12},{12,16},{16,20},{20,24},{24,28},{1,5},{5,9},{9,... | collective-permute-start | bytes 11528 | tf_op jit(solution)/shard_map/ppermute | solution.py:72
  109.1 1.6 maximum_convert_fusion
  110.7 3.4 %multiply_convert_fusion = (bf16[1024,640]{1,0:T(8,128)(2,1)}, f32[1024,640]{1,0:T(8,128)S(1)}, f32[1024,640]{1,0:T(8,128)S(1)}) fusion(f32[640]{0:T(1024)S(1)} %copy-done.24, bf16[1024,640]{1,0:T(8,128)(2,1)S(1)} %copy-done.8, f32[640]{0:T(1024)S(1)} %mul.319, f32[1027,640]{1,0:T(8,128)S(1)} %maximum_convert_fusion, f32[640]{0:T(1024)S(1)} %get-tuple-element.225, ...), kind=kLoop, calls=%fused_computation.27 | loop fusion | flops 13762560 | bytes 18368000 | tf_op jit(solution)/shard_map/convert_element_type | solution.py:440
  114.3 2.3 fusion.24
  116.6 2.1 collective-permute-done.19
  118.7 1.3 collective-permute-done.21
  120.0 1.6 collective-permute-start.22
  122.1 2.9 %collective-permute-done.22 = f32[24,1024]{1,0:T(8,128)S(1)} collective-permute-done((f32[24,1024]{1,0:T(8,128)S(1)}, f32[24,1024]{1,0:T(8,128)S(1)}, u32[]{:S(2)}, u32[]{:S(2)}) %collective-permute-start.22) | collective-permute-done | bytes 98336 | tf_op jit(solution)/shard_map/ppermute | solution.py:31
  125.1 2.3 fusion.26
  127.4 4.6 %multiply_reduce_fusion.2 = (f32[640]{0:T(1024)S(1)}, f32[640]{0:T(1024)S(1)}, f32[640]{0:T(1024)S(1)}, f32[640]{0:T(1024)S(1)}, f32[640]{0:T(1024)S(1)}, /*inde...) fusion(f32[1027,640]{1,0:T(8,128)S(1)} %maximum_convert_fusion, ...), kind=kLoop, calls=%fused_computation.20 | loop fusion | flops 22933120 | bytes 24934912 | tf_op jit(solution)/shard_map/reduce_sum | solution.py:461
  132.0 1.5 collective-permute-start.23
  133.5 1.6 collective-permute-start.26
  136.2 4.3 %shard_map.172 = (bf16[2,320,640]{2,1,0:T(8,128)(2,1)}, bf16[2,320,640]{2,1,0:T(8,128)(2,1)S(1)}) custom-call(s32[40]{0:T(128)S(1)} %copy-done.2, bf16[4,640,1024]{2,1,0:T(8,128)(2,1)S(1)} %bitcast.79, bf16[1024,640]{1,0:T(8,128)(2,1)S(1)} %fusion.6.rhs), custom_call_target="tpu_custom_call" | custom-call | flops 1 | bytes 1 | tf_op jit(solution)/shard_map/pallas_call | solution.py:288
  142.0 2.2 collective-permute-start.25
  145.6 4.3 %shard_map.173 = (bf16[2,320,640]{2,1,0:T(8,128)(2,1)}, bf16[2,320,640]{2,1,0:T(8,128)(2,1)S(1)}) custom-call(s32[40]{0:T(128)S(1)} %copy-done.2, bf16[4,640,1024]{2,1,0:T(8,128)(2,1)S(1)} %bitcast.79, bf16[1024,640]{1,0:T(8,128)(2,1)S(1)} %fusion.9.rhs), custom_call_target="tpu_custom_call" | custom-call | flops 1 | bytes 1 | tf_op jit(solution)/shard_map/pallas_call | solution.py:288
  149.9 3.4 %shard_map.174 = (bf16[1,320,640]{2,1,0:T(8,128)(2,1)S(1)}, bf16[1,320,640]{2,1,0:T(8,128)(2,1)S(1)}, bf16[1,320,640]{2,1,0:T(8,128)(2,1)S(1)}, bf16[1,320,640]{2,1,0:T(8,128)(2,1)S(1)}) custom-call(s32[40]{0:T(128)S(1)} %copy-done.2, bf16[4,640,1024]{2,1,0:T(8,128)(2,1)S(1)} %bitcast.79, bf16[1024,640]{1,0:T(8,128)(2,1)S(1)} %fusion.6.rhs), custom_call_target="tpu_custom_call" | custom-call | flops 1 | bytes 1 | tf_op jit(solution)/shard_map/pallas_call | solution.py:288
  153.3 1.6 fusion.11
  155.7 3.9 %collective-permute-start.28 = (f32[23,640]{1,0:T(8,128)S(1)}, f32[23,640]{1,0:T(8,128)S(1)}, u32[]{:S(2)}, u32[]{:S(2)}) collective-permute-start(f32[23,640]{1,0:T(8,128)S(1)} %concatenate.31), channel_id=1, source_target_pairs={{0,16},{4,20},{8,24},{12,28},{16,0},{20,4},{24,8},{28,12},{1,17},{... | collective-permute-start | bytes 176648 | tf_op jit(solution)/shard_map/ppermute | solution.py:61
  161.4 1.6 collective-permute-done.28
  164.4 2.4 collective-permute-start.30
  166.8 2.3 fusion.19
  169.8 3.5 %collective-permute-start.32 = (bf16[320,640]{1,0:T(8,128)(2,1)}, bf16[320,640]{1,0:T(8,128)(2,1)S(1)}, u32[]{:S(2)}, u32[]{:S(2)}) collective-permute-start(bf16[320,640]{1,0:T(8,128)(2,1)} %get-tuple-element.240), channel_id=1, source_target_pairs={{0,24},{4,28},{8,0},{12,4},{16,8},{20,12},{24,16},{28,20},{1,25},{... | collective-permute-start | bytes 1228808 | tf_op jit(solution)/shard_map/ppermute | solution.py:61
  174.4 11.1 %shard_map.175 = bf16[1024,640]{1,0:T(8,128)(2,1)} custom-call(s32[40]{0:T(128)} %concatenate.24.idx, bf16[1024,640]{1,0:T(8,128)(2,1)} %get-tuple-element.166.refs_0_, bf16[1024,640]{1,0:T(8,128)(2,1)} %copy-done.17, bf16[1024,640]{1,0:T(8,128)(2,1)} %collective-permute-done.26.refs_2_, bf16[1024,640]{1,0:T(8,128)(2,1)} %collective-permute-done.34.refs_3_, ...), custom_call_target="tpu_custom_call" | custom-call | flops 1 | bytes 1 | tf_op jit(solution)/shard_map/pallas_call | solution.py:171
  185.5 4.5 %collective-permute-done.32 = bf16[320,640]{1,0:T(8,128)(2,1)S(1)} collective-permute-done((bf16[320,640]{1,0:T(8,128)(2,1)}, bf16[320,640]{1,0:T(8,128)(2,1)S(1)}, u32[]{:S(2)}, u32[]{:S(2)}) %collective-permute-start.32) | collective-permute-done | bytes 409632 | tf_op jit(solution)/shard_map/ppermute | solution.py:61
  191.0 1.9 fusion.20
  192.9 1.5 collective-permute-start.36
  194.4 1.8 add_convert_fusion
  196.9 2.5 copy-done.1
  199.4 3.4 %shard_map.176 = (bf16[1,320,640]{2,1,0:T(8,128)(2,1)S(1)}, bf16[1,320,640]{2,1,0:T(8,128)(2,1)S(1)}, bf16[1,320,640]{2,1,0:T(8,128)(2,1)S(1)}, bf16[1,320,640]{2,1,0:T(8,128)(2,1)S(1)}) custom-call(s32[40]{0:T(128)S(1)} %copy-done.3, bf16[4,640,1024]{2,1,0:T(8,128)(2,1)S(1)} %copy-done.1, bf16[1024,640]{1,0:T(8,128)(2,1)S(1)} %fusion.9.rhs), custom_call_target="tpu_custom_call" | custom-call | flops 1 | bytes 1 | tf_op jit(solution)/shard_map/pallas_call | solution.py:288
  202.8 1.6 collective-permute-start.38
  204.4 1.8 collective-permute-start.37
  207.3 1.4 collective-permute-done.38
  208.8 4.4 %collective-permute-start.40 = (f32[16,640]{1,0:T(8,128)S(1)}, f32[16,640]{1,0:T(8,128)S(1)}, u32[]{:S(2)}, u32[]{:S(2)}) collective-permute-start(f32[16,640]{1,0:T(8,128)S(1)} %fusion.53), channel_id=1, source_target_pairs={{0,24},{4,28},{8,0},{12,4},{16,8},{20,12},{24,16},{28,20},{1,25},{... | collective-permute-start | bytes 122888 | tf_op jit(solution)/shard_map/ppermute | solution.py:61
  213.2 2.7 %collective-permute-done.39 = f32[16,640]{1,0:T(8,128)S(1)} collective-permute-done((f32[16,640]{1,0:T(8,128)S(1)}, f32[16,640]{1,0:T(8,128)S(1)}, u32[]{:S(2)}, u32[]{:S(2)}) %collective-permute-start.39) | collective-permute-done | bytes 40992 | tf_op jit(solution)/shard_map/ppermute | solution.py:61
  217.3 2.1 collective-permute-start.41
  219.4 2.1 fusion.22
  221.6 2.6 collective-permute-start.42
  227.2 1.6 collective-permute-start.46
  228.7 2.5 bitcast_add_fusion.1
  231.3 7.2 %collective-permute-done.44 = f32[16,640]{1,0:T(8,128)S(1)} collective-permute-done((f32[16,640]{1,0:T(8,128)S(1)}, f32[16,640]{1,0:T(8,128)S(1)}, u32[]{:S(2)}, u32[]{:S(2)}) %collective-permute-start.44) | collective-permute-done | bytes 40992 | tf_op jit(solution)/shard_map/ppermute | solution.py:67
  242.2 2.4 collective-permute-start.48
  245.2 2.3 fusion.28
  247.5 15.8 %collective-permute-done.48 = bf16[320,640]{1,0:T(8,128)(2,1)S(1)} collective-permute-done((bf16[320,640]{1,0:T(8,128)(2,1)S(1)}, bf16[320,640]{1,0:T(8,128)(2,1)S(1)}, u32[]{:S(2)}, u32[]{:S(2)}) %collective-permute-start.48) | collective-permute-done | bytes 409632 | tf_op jit(solution)/shard_map/ppermute | solution.py:61
  (190 shorter events, 36.3 us)
Async XLA Ops:
  0.6 27.3 %copy-start = (bf16[640,16]{0,1:T(8,128)(2,1)S(1)}, bf16[640,16]{0,1:T(8,128)(2,1)}, u32[]{:S(2)}) copy-start(bf16[640,16]{0,1:T(8,128)(2,1)} %param.19) | copy-start | bytes 61444
  0.7 27.3 %copy-start.6 = (bf16[1024,640]{1,0:T(8,128)(2,1)S(1)}, bf16[1024,640]{1,0:T(8,128)(2,1)}, u32[]{:S(2)}) copy-start(bf16[1024,640]{1,0:T(8,128)(2,1)} %refs_1_) | copy-start | bytes 3932164
  2.0 51.4 %copy-start.15 = (bf16[2,320,640]{2,1,0:T(8,128)(2,1)}, bf16[2,320,640]{2,1,0:T(8,128)(2,1)S(1)}, u32[]{:S(2)}) copy-start(bf16[2,320,640]{2,1,0:T(8,128)(2,1)S(1)} %pad_maximum_fusion.refs_4_) | copy-start | bytes 2457604
  2.0 23.5 %collective-permute-start = (bf16[2,320,640]{2,1,0:T(8,128)(2,1)S(1)}, bf16[2,320,640]{2,1,0:T(8,128)(2,1)}, u32[]{:S(2)}, u32[]{:S(2)}) collective-permute-start(bf16[2,320,640]{2,1,0:T(8,128)(2,1)S(1)} %pad_maximum_fusion.refs_4_), channel_id=1, source_target_pairs={{0,8},{4,12},{8,16},{12,20},{16,24},{20,28},{24,0},{28,4},{1,9},{5... | collective-permute-start | bytes 2457608 | tf_op jit(solution)/shard_map/ppermute | solution.py:61
  5.1 20.4 %collective-permute-start.1 = (bf16[2,320,640]{2,1,0:T(8,128)(2,1)S(1)}, bf16[2,320,640]{2,1,0:T(8,128)(2,1)}, u32[]{:S(2)}, u32[]{:S(2)}) collective-permute-start(bf16[2,320,640]{2,1,0:T(8,128)(2,1)S(1)} %pad_maximum_fusion.refs_4_), channel_id=1, source_target_pairs={{0,4},{4,0},{8,12},{12,8},{16,20},{20,16},{24,28},{28,24},{1,5},{5... | collective-permute-start | bytes 2457608 | tf_op jit(solution)/shard_map/ppermute | solution.py:67
  6.6 30.2 %collective-permute-start.5 = (bf16[1024,640]{1,0:T(8,128)(2,1)}, bf16[1024,640]{1,0:T(8,128)(2,1)S(1)}, u32[]{:S(2)}, u32[]{:S(2)}) collective-permute-start(bf16[1024,640]{1,0:T(8,128)(2,1)} %refs_1_), channel_id=1, source_target_pairs={{0,2},{1,3},{2,0},{3,1},{4,6},{5,7},{6,4},{7,5},{8,10},{9,11},{10,... | collective-permute-start | bytes 3932168 | tf_op jit(solution)/shard_map/ppermute | solution.py:31
  25.5 21.5 %collective-permute-start.2 = (bf16[2,320,640]{2,1,0:T(8,128)(2,1)}, bf16[2,320,640]{2,1,0:T(8,128)(2,1)}, u32[]{:S(2)}, u32[]{:S(2)}) collective-permute-start(bf16[2,320,640]{2,1,0:T(8,128)(2,1)} %collective-permute-done.refs_6_), channel_id=1, source_target_pairs={{0,8},{4,12},{8,16},{12,20},{16,24},{20,28},{24,0},{28,4},{1,9},{5... | collective-permute-start | bytes 2457608 | tf_op jit(solution)/shard_map/ppermute | solution.py:61
  26.5 20.5 %collective-permute-start.3 = (bf16[2,320,640]{2,1,0:T(8,128)(2,1)}, bf16[2,320,640]{2,1,0:T(8,128)(2,1)S(1)}, u32[]{:S(2)}, u32[]{:S(2)}) collective-permute-start(bf16[2,320,640]{2,1,0:T(8,128)(2,1)} %collective-permute-done.refs_6_), channel_id=1, source_target_pairs={{0,4},{4,0},{8,12},{12,8},{16,20},{20,16},{24,28},{28,24},{1,5},{5... | collective-permute-start | bytes 2457608 | tf_op jit(solution)/shard_map/ppermute | solution.py:67
  29.8 1.4 collective-permute-start.4
  36.8 16.6 %copy-start.9 = (bf16[1024,640]{1,0:T(8,128)(2,1)}, bf16[1024,640]{1,0:T(8,128)(2,1)S(1)}, u32[]{:S(2)}) copy-start(bf16[1024,640]{1,0:T(8,128)(2,1)S(1)} %collective-permute-done.5.refs_2_.refs_3_) | copy-start | bytes 3932164
  47.0 6.4 %collective-permute-start.9 = (bf16[1024,640]{1,0:T(8,128)(2,1)S(1)}, bf16[1024,640]{1,0:T(8,128)(2,1)S(1)}, u32[]{:S(2)}, u32[]{:S(2)}) collective-permute-start(bf16[1024,640]{1,0:T(8,128)(2,1)S(1)} %copy-done.6), channel_id=1, source_target_pairs={{0,1},{1,0},{2,3},{3,2},{4,5},{5,4},{6,7},{7,6},{8,9},{9,8},{10,11... | collective-permute-start | bytes 3932168 | tf_op jit(solution)/shard_map/ppermute | solution.py:31
  47.0 6.4 %collective-permute-start.10 = (bf16[1024,640]{1,0:T(8,128)(2,1)S(1)}, bf16[1024,640]{1,0:T(8,128)(2,1)S(1)}, u32[]{:S(2)}, u32[]{:S(2)}) collective-permute-start(bf16[1024,640]{1,0:T(8,128)(2,1)S(1)} %collective-permute-done.5.refs_2_.refs_3_), channel_id=1, source_target_pairs={{0,1},{1,0},{2,3},{3,2},{4,5},{5,4},{6,7},{7,6},{8,9},{9,8},{10,11... | collective-permute-start | bytes 3932168 | tf_op jit(solution)/shard_map/ppermute | solution.py:31
  47.5 25.0 %collective-permute-start.6 = (bf16[2,320,640]{2,1,0:T(8,128)(2,1)}, bf16[2,320,640]{2,1,0:T(8,128)(2,1)}, u32[]{:S(2)}, u32[]{:S(2)}) collective-permute-start(bf16[2,320,640]{2,1,0:T(8,128)(2,1)} %collective-permute-done.2.refs_5_), channel_id=1, source_target_pairs={{0,8},{4,12},{8,16},{12,20},{16,24},{20,28},{24,0},{28,4},{1,9},{5... | collective-permute-start | bytes 2457608 | tf_op jit(solution)/shard_map/ppermute | solution.py:61
  47.5 25.0 %collective-permute-start.7 = (bf16[2,320,640]{2,1,0:T(8,128)(2,1)}, bf16[2,320,640]{2,1,0:T(8,128)(2,1)}, u32[]{:S(2)}, u32[]{:S(2)}) collective-permute-start(bf16[2,320,640]{2,1,0:T(8,128)(2,1)} %collective-permute-done.2.refs_5_), channel_id=1, source_target_pairs={{0,4},{4,0},{8,12},{12,8},{16,20},{20,16},{24,28},{28,24},{1,5},{5... | collective-permute-start | bytes 2457608 | tf_op jit(solution)/shard_map/ppermute | solution.py:67
  48.8 4.5 %collective-permute-start.8 = (f32[16,1344]{1,0:T(8,128)S(1)}, f32[16,1344]{1,0:T(8,128)S(1)}, u32[]{:S(2)}, u32[]{:S(2)}) collective-permute-start(f32[16,1344]{1,0:T(8,128)S(1)} %fusion.49), channel_id=1, source_target_pairs={{0,2},{1,3},{2,0},{3,1},{4,6},{5,7},{6,4},{7,5},{8,10},{9,11},{10,... | collective-permute-start | bytes 258056 | tf_op jit(solution)/shard_map/ppermute | solution.py:31
  65.6 6.9 %collective-permute-start.11 = (f32[16,320]{1,0:T(8,128)S(1)}, f32[16,320]{1,0:T(8,128)S(1)}, u32[]{:S(2)}, u32[]{:S(2)}) collective-permute-start(f32[16,320]{1,0:T(8,128)S(1)} %slice.169), channel_id=1, source_target_pairs={{0,4},{4,0},{8,12},{12,8},{16,20},{20,16},{24,28},{28,24},{1,5},{5... | collective-permute-start | bytes 61448 | tf_op jit(solution)/shard_map/ppermute | solution.py:67
  72.5 19.2 %collective-permute-start.12 = (bf16[2,320,640]{2,1,0:T(8,128)(2,1)}, bf16[2,320,640]{2,1,0:T(8,128)(2,1)S(1)}, u32[]{:S(2)}, u32[]{:S(2)}) collective-permute-start(bf16[2,320,640]{2,1,0:T(8,128)(2,1)} %collective-permute-done.6.refs_7_), channel_id=1, source_target_pairs={{0,4},{4,0},{8,12},{12,8},{16,20},{20,16},{24,28},{28,24},{1,5},{5... | collective-permute-start | bytes 2457608 | tf_op jit(solution)/shard_map/ppermute | solution.py:67
  73.9 14.3 %collective-permute-start.16 = (bf16[320,640]{1,0:T(8,128)(2,1)S(1)}, bf16[320,640]{1,0:T(8,128)(2,1)S(1)}, u32[]{:S(2)}, u32[]{:S(2)}) collective-permute-start(bf16[320,640]{1,0:T(8,128)(2,1)S(1)} %copy-done.16), channel_id=1, source_target_pairs={{0,8},{4,12},{8,16},{12,20},{16,24},{20,28},{24,0},{28,4},{1,9},{5... | collective-permute-start | bytes 1228808 | tf_op jit(solution)/shard_map/ppermute | solution.py:61
  74.7 15.2 %collective-permute-start.13 = (f32[16,640]{1,0:T(8,128)S(1)}, f32[16,640]{1,0:T(8,128)S(1)}, u32[]{:S(2)}, u32[]{:S(2)}) collective-permute-start(f32[16,640]{1,0:T(8,128)S(1)} %pad_maximum_fusion.5), channel_id=1, source_target_pairs={{0,8},{4,12},{8,16},{12,20},{16,24},{20,28},{24,0},{28,4},{1,9},{5... | collective-permute-start | bytes 122888 | tf_op jit(solution)/shard_map/ppermute | solution.py:61
  76.9 13.1 %collective-permute-start.14 = (f32[16,640]{1,0:T(8,128)S(1)}, f32[16,640]{1,0:T(8,128)S(1)}, u32[]{:S(2)}, u32[]{:S(2)}) collective-permute-start(f32[16,640]{1,0:T(8,128)S(1)} %pad_maximum_fusion.5), channel_id=1, source_target_pairs={{0,16},{4,20},{8,24},{12,28},{16,0},{20,4},{24,8},{28,12},{1,17},{... | collective-permute-start | bytes 122888 | tf_op jit(solution)/shard_map/ppermute | solution.py:61
  78.6 11.4 %collective-permute-start.15 = (f32[16,640]{1,0:T(8,128)S(1)}, f32[16,640]{1,0:T(8,128)S(1)}, u32[]{:S(2)}, u32[]{:S(2)}) collective-permute-start(f32[16,640]{1,0:T(8,128)S(1)} %pad_maximum_fusion.5), channel_id=1, source_target_pairs={{0,24},{4,28},{8,0},{12,4},{16,8},{20,12},{24,16},{28,20},{1,25},{... | collective-permute-start | bytes 122888 | tf_op jit(solution)/shard_map/ppermute | solution.py:61
  88.2 28.4 %collective-permute-start.20 = (bf16[320,640]{1,0:T(8,128)(2,1)S(1)}, bf16[320,640]{1,0:T(8,128)(2,1)S(1)}, u32[]{:S(2)}, u32[]{:S(2)}) collective-permute-start(bf16[320,640]{1,0:T(8,128)(2,1)S(1)} %copy-done.16), channel_id=1, source_target_pairs={{0,24},{4,28},{8,0},{12,4},{16,8},{20,12},{24,16},{28,20},{1,25},{... | collective-permute-start | bytes 1228808 | tf_op jit(solution)/shard_map/ppermute | solution.py:61
  89.9 14.3 %copy-start.13 = (bf16[2,320,640]{2,1,0:T(8,128)(2,1)}, bf16[2,320,640]{2,1,0:T(8,128)(2,1)S(1)}, u32[]{:S(2)}) copy-start(bf16[2,320,640]{2,1,0:T(8,128)(2,1)S(1)} %pad_maximum_fusion.1.refs_4_) | copy-start | bytes 2457604
  91.7 27.0 %collective-permute-start.18 = (bf16[2,320,640]{2,1,0:T(8,128)(2,1)S(1)}, bf16[2,320,640]{2,1,0:T(8,128)(2,1)S(1)}, u32[]{:S(2)}, u32[]{:S(2)}) collective-permute-start(bf16[2,320,640]{2,1,0:T(8,128)(2,1)S(1)} %pad_maximum_fusion.1.refs_4_), channel_id=1, source_target_pairs={{0,4},{4,0},{8,12},{12,8},{16,20},{20,16},{24,28},{28,24},{1,5},{5... | collective-permute-start | bytes 2457608 | tf_op jit(solution)/shard_map/ppermute | solution.py:67
  105.0 4.1 %collective-permute-start.17 = (bf16[3,640]{1,0:T(4,128)(2,1)S(1)}, bf16[3,640]{1,0:T(4,128)(2,1)S(1)}, u32[]{:S(2)}, u32[]{:S(2)}) collective-permute-start(bf16[3,640]{1,0:T(4,128)(2,1)S(1)} %slice.141), channel_id=1, source_target_pairs={{0,4},{4,8},{8,12},{12,16},{16,20},{20,24},{24,28},{1,5},{5,9},{9,... | collective-permute-start | bytes 11528 | tf_op jit(solution)/shard_map/ppermute | solution.py:72
  107.8 11.0 %collective-permute-start.19 = (bf16[320,640]{1,0:T(8,128)(2,1)S(1)}, bf16[320,640]{1,0:T(8,128)(2,1)S(1)}, u32[]{:S(2)}, u32[]{:S(2)}) collective-permute-start(bf16[320,640]{1,0:T(8,128)(2,1)S(1)} %slice_bitcast_fusion), channel_id=1, source_target_pairs={{0,8},{4,12},{8,16},{12,20},{16,24},{20,28},{24,0},{28,4},{1,9},{5... | collective-permute-start | bytes 1228808 | tf_op jit(solution)/shard_map/ppermute | solution.py:61
  114.3 10.7 %copy-start.36 = (s32[1024]{0:T(1024)S(1)}, s32[1024]{0:T(1024)}, u32[]{:S(2)}) copy-start(s32[1024]{0:T(1024)} %param.10) | copy-start | bytes 12292
  118.7 8.7 %copy-start.18 = (bf16[2,320,640]{2,1,0:T(8,128)(2,1)}, bf16[2,320,640]{2,1,0:T(8,128)(2,1)S(1)}, u32[]{:S(2)}) copy-start(bf16[2,320,640]{2,1,0:T(8,128)(2,1)S(1)} %collective-permute-done.18.refs_5_) | copy-start | bytes 2457604
  118.7 1.3 collective-permute-start.21
  120.0 4.9 %collective-permute-start.22 = (f32[24,1024]{1,0:T(8,128)S(1)}, f32[24,1024]{1,0:T(8,128)S(1)}, u32[]{:S(2)}, u32[]{:S(2)}) collective-permute-start(f32[24,1024]{1,0:T(8,128)S(1)} %add.510), channel_id=1, source_target_pairs={{0,2},{1,3},{2,0},{3,1},{4,6},{5,7},{6,4},{7,5},{8,10},{9,11},{10,... | collective-permute-start | bytes 294920 | tf_op jit(solution)/shard_map/ppermute | solution.py:31
  121.7 10.3 %copy-start.14 = (bf16[2,320,640]{2,1,0:T(8,128)(2,1)}, bf16[2,320,640]{2,1,0:T(8,128)(2,1)S(1)}, u32[]{:S(2)}) copy-start(bf16[2,320,640]{2,1,0:T(8,128)(2,1)S(1)} %pad_maximum_fusion.2.refs_6_) | copy-start | bytes 2457604
  121.7 20.3 %collective-permute-start.24 = (bf16[2,320,640]{2,1,0:T(8,128)(2,1)S(1)}, bf16[2,320,640]{2,1,0:T(8,128)(2,1)S(1)}, u32[]{:S(2)}, u32[]{:S(2)}) collective-permute-start(bf16[2,320,640]{2,1,0:T(8,128)(2,1)S(1)} %pad_maximum_fusion.2.refs_6_), channel_id=1, source_target_pairs={{0,4},{4,0},{8,12},{12,8},{16,20},{20,16},{24,28},{28,24},{1,5},{5... | collective-permute-start | bytes 2457608 | tf_op jit(solution)/shard_map/ppermute | solution.py:67
  125.1 11.1 %slice-start = ((s8[5242880]{0:T(1024)(128)(4,1)}), s8[4194304]{0:T(1024)(128)(4,1)S(1)}, s32[]{:S(2)}) async-start(s8[5242880]{0:T(1024)(128)(4,1)} %bitcast.78), calls=%async_computation | async-start | bytes 8388608
  127.4 8.8 %slice-start.1 = ((s8[5242880]{0:T(1024)(128)(4,1)}), s8[1048576]{0:T(1024)(128)(4,1)S(1)}, s32[]{:S(2)}) async-start(s8[5242880]{0:T(1024)(128)(4,1)} %bitcast.78), calls=%async_computation.1 | async-start | bytes 2097152
  132.0 10.0 %collective-permute-start.23 = (f32[3,640]{1,0:T(4,128)S(1)}, f32[3,640]{1,0:T(4,128)S(1)}, u32[]{:S(2)}, u32[]{:S(2)}) collective-permute-start(f32[3,640]{1,0:T(4,128)S(1)} %slice.177), channel_id=1, source_target_pairs={{4,0},{8,4},{12,8},{16,12},{20,16},{24,20},{28,24},{5,1},{9,5},{13... | collective-permute-start | bytes 23048 | tf_op jit(solution)/shard_map/ppermute | solution.py:72
  133.5 30.4 %collective-permute-start.26 = (bf16[1024,640]{1,0:T(8,128)(2,1)}, bf16[1024,640]{1,0:T(8,128)(2,1)}, u32[]{:S(2)}, u32[]{:S(2)}) collective-permute-start(bf16[1024,640]{1,0:T(8,128)(2,1)} %get-tuple-element.166.refs_0_), channel_id=1, source_target_pairs={{0,2},{1,3},{2,0},{3,1},{4,6},{5,7},{6,4},{7,5},{8,10},{9,11},{10,... | collective-permute-start | bytes 3932168 | tf_op jit(solution)/shard_map/ppermute | solution.py:31
  142.0 21.9 %collective-permute-start.25 = (bf16[2,320,640]{2,1,0:T(8,128)(2,1)}, bf16[2,320,640]{2,1,0:T(8,128)(2,1)}, u32[]{:S(2)}, u32[]{:S(2)}) collective-permute-start(bf16[2,320,640]{2,1,0:T(8,128)(2,1)} %get-tuple-element.146), channel_id=1, source_target_pairs={{0,4},{4,0},{8,12},{12,8},{16,20},{20,16},{24,28},{28,24},{1,5},{5... | collective-permute-start | bytes 2457608 | tf_op jit(solution)/shard_map/ppermute | solution.py:67
  155.0 6.4 %collective-permute-start.27 = (f32[23,640]{1,0:T(8,128)S(1)}, f32[23,640]{1,0:T(8,128)S(1)}, u32[]{:S(2)}, u32[]{:S(2)}) collective-permute-start(f32[23,640]{1,0:T(8,128)S(1)} %concatenate.31), channel_id=1, source_target_pairs={{0,8},{4,12},{8,16},{12,20},{16,24},{20,28},{24,0},{28,4},{1,9},{5... | collective-permute-start | bytes 176648 | tf_op jit(solution)/shard_map/ppermute | solution.py:61
  155.7 7.2 %collective-permute-start.28 = (f32[23,640]{1,0:T(8,128)S(1)}, f32[23,640]{1,0:T(8,128)S(1)}, u32[]{:S(2)}, u32[]{:S(2)}) collective-permute-start(f32[23,640]{1,0:T(8,128)S(1)} %concatenate.31), channel_id=1, source_target_pairs={{0,16},{4,20},{8,24},{12,28},{16,0},{20,4},{24,8},{28,12},{1,17},{... | collective-permute-start | bytes 176648 | tf_op jit(solution)/shard_map/ppermute | solution.py:61
  159.6 4.2 %collective-permute-start.29 = (f32[23,640]{1,0:T(8,128)S(1)}, f32[23,640]{1,0:T(8,128)S(1)}, u32[]{:S(2)}, u32[]{:S(2)}) collective-permute-start(f32[23,640]{1,0:T(8,128)S(1)} %concatenate.31), channel_id=1, source_target_pairs={{0,24},{4,28},{8,0},{12,4},{16,8},{20,12},{24,16},{28,20},{1,25},{... | collective-permute-start | bytes 176648 | tf_op jit(solution)/shard_map/ppermute | solution.py:61
  161.4 24.1 %copy-start.25 = (f32[23,640]{1,0:T(8,128)}, f32[23,640]{1,0:T(8,128)S(1)}, u32[]{:S(2)}) copy-start(f32[23,640]{1,0:T(8,128)S(1)} %collective-permute-done.27) | copy-start | bytes 176644
  163.0 22.5 %copy-start.27 = (f32[23,640]{1,0:T(8,128)}, f32[23,640]{1,0:T(8,128)S(1)}, u32[]{:S(2)}) copy-start(f32[23,640]{1,0:T(8,128)S(1)} %collective-permute-done.28) | copy-start | bytes 176644
  163.8 21.6 %copy-start.29 = (f32[23,640]{1,0:T(8,128)}, f32[23,640]{1,0:T(8,128)S(1)}, u32[]{:S(2)}) copy-start(f32[23,640]{1,0:T(8,128)S(1)} %collective-permute-done.29) | copy-start | bytes 176644
  163.9 9.4 %collective-permute-start.33 = (bf16[1024,640]{1,0:T(8,128)(2,1)}, bf16[1024,640]{1,0:T(8,128)(2,1)S(1)}, u32[]{:S(2)}, u32[]{:S(2)}) collective-permute-start(bf16[1024,640]{1,0:T(8,128)(2,1)} %get-tuple-element.166.refs_0_), channel_id=1, source_target_pairs={{0,1},{1,0},{2,3},{3,2},{4,5},{5,4},{6,7},{7,6},{8,9},{9,8},{10,11... | collective-permute-start | bytes 3932168 | tf_op jit(solution)/shard_map/ppermute | solution.py:31
  163.9 9.4 %collective-permute-start.34 = (bf16[1024,640]{1,0:T(8,128)(2,1)}, bf16[1024,640]{1,0:T(8,128)(2,1)}, u32[]{:S(2)}, u32[]{:S(2)}) collective-permute-start(bf16[1024,640]{1,0:T(8,128)(2,1)} %collective-permute-done.26.refs_2_), channel_id=1, source_target_pairs={{0,1},{1,0},{2,3},{3,2},{4,5},{5,4},{6,7},{7,6},{8,9},{9,8},{10,11... | collective-permute-start | bytes 3932168 | tf_op jit(solution)/shard_map/ppermute | solution.py:31
  164.4 25.6 %collective-permute-start.30 = (bf16[2,320,640]{2,1,0:T(8,128)(2,1)}, bf16[2,320,640]{2,1,0:T(8,128)(2,1)}, u32[]{:S(2)}, u32[]{:S(2)}) collective-permute-start(bf16[2,320,640]{2,1,0:T(8,128)(2,1)} %copy-done.5), channel_id=1, source_target_pairs={{0,4},{4,0},{8,12},{12,8},{16,20},{20,16},{24,28},{28,24},{1,5},{5... | collective-permute-start | bytes 2457608 | tf_op jit(solution)/shard_map/ppermute | solution.py:67
  169.1 16.4 %collective-permute-start.31 = (bf16[320,640]{1,0:T(8,128)(2,1)}, bf16[320,640]{1,0:T(8,128)(2,1)S(1)}, u32[]{:S(2)}, u32[]{:S(2)}) collective-permute-start(bf16[320,640]{1,0:T(8,128)(2,1)} %get-tuple-element.241), channel_id=1, source_target_pairs={{0,8},{4,12},{8,16},{12,20},{16,24},{20,28},{24,0},{28,4},{1,9},{5... | collective-permute-start | bytes 1228808 | tf_op jit(solution)/shard_map/ppermute | solution.py:61
  169.8 24.6 %copy-start.7 = (bf16[1024,640]{1,0:T(8,128)(2,1)S(1)}, bf16[1024,640]{1,0:T(8,128)(2,1)}, u32[]{:S(2)}) copy-start(bf16[1024,640]{1,0:T(8,128)(2,1)} %refs_1_) | copy-start | bytes 3932164
  169.8 20.2 %collective-permute-start.32 = (bf16[320,640]{1,0:T(8,128)(2,1)}, bf16[320,640]{1,0:T(8,128)(2,1)S(1)}, u32[]{:S(2)}, u32[]{:S(2)}) collective-permute-start(bf16[320,640]{1,0:T(8,128)(2,1)} %get-tuple-element.240), channel_id=1, source_target_pairs={{0,24},{4,28},{8,0},{12,4},{16,8},{20,12},{24,16},{28,20},{1,25},{... | collective-permute-start | bytes 1228808 | tf_op jit(solution)/shard_map/ppermute | solution.py:61
  185.5 10.8 %copy-start.22 = (bf16[320,640]{1,0:T(8,128)(2,1)}, bf16[320,640]{1,0:T(8,128)(2,1)S(1)}, u32[]{:S(2)}) copy-start(bf16[320,640]{1,0:T(8,128)(2,1)S(1)} %collective-permute-done.31) | copy-start | bytes 1228804
  190.0 26.7 %collective-permute-start.35 = (bf16[2,320,640]{2,1,0:T(8,128)(2,1)}, bf16[2,320,640]{2,1,0:T(8,128)(2,1)}, u32[]{:S(2)}, u32[]{:S(2)}) collective-permute-start(bf16[2,320,640]{2,1,0:T(8,128)(2,1)} %get-tuple-element.174), channel_id=1, source_target_pairs={{0,4},{4,0},{8,12},{12,8},{16,20},{20,16},{24,28},{28,24},{1,5},{5... | collective-permute-start | bytes 2457608 | tf_op jit(solution)/shard_map/ppermute | solution.py:67
  192.9 23.8 %collective-permute-start.36 = (bf16[320,640]{1,0:T(8,128)(2,1)}, bf16[320,640]{1,0:T(8,128)(2,1)}, u32[]{:S(2)}, u32[]{:S(2)}) collective-permute-start(bf16[320,640]{1,0:T(8,128)(2,1)} %fusion.20), channel_id=1, source_target_pairs={{0,16},{4,20},{8,24},{12,28},{16,0},{20,4},{24,8},{28,12},{1,17},{... | collective-permute-start | bytes 1228808 | tf_op jit(solution)/shard_map/ppermute | solution.py:61
  202.8 6.0 %collective-permute-start.38 = (f32[16,640]{1,0:T(8,128)S(1)}, f32[16,640]{1,0:T(8,128)S(1)}, u32[]{:S(2)}, u32[]{:S(2)}) collective-permute-start(f32[16,640]{1,0:T(8,128)S(1)} %fusion.53), channel_id=1, source_target_pairs={{0,8},{4,12},{8,16},{12,20},{16,24},{20,28},{24,0},{28,4},{1,9},{5... | collective-permute-start | bytes 122888 | tf_op jit(solution)/shard_map/ppermute | solution.py:61
  204.4 12.2 %collective-permute-start.37 = (f32[23,640]{1,0:T(8,128)S(1)}, f32[23,640]{1,0:T(8,128)S(1)}, u32[]{:S(2)}, u32[]{:S(2)}) collective-permute-start(f32[23,640]{1,0:T(8,128)S(1)} %add_add_fusion), channel_id=1, source_target_pairs={{0,4},{4,0},{8,12},{12,8},{16,20},{20,16},{24,28},{28,24},{1,5},{5... | collective-permute-start | bytes 176648 | tf_op jit(solution)/shard_map/ppermute | solution.py:67
  206.2 9.6 %collective-permute-start.39 = (f32[16,640]{1,0:T(8,128)S(1)}, f32[16,640]{1,0:T(8,128)S(1)}, u32[]{:S(2)}, u32[]{:S(2)}) collective-permute-start(f32[16,640]{1,0:T(8,128)S(1)} %fusion.53), channel_id=1, source_target_pairs={{0,16},{4,20},{8,24},{12,28},{16,0},{20,4},{24,8},{28,12},{1,17},{... | collective-permute-start | bytes 122888 | tf_op jit(solution)/shard_map/ppermute | solution.py:61
  208.8 7.9 %collective-permute-start.40 = (f32[16,640]{1,0:T(8,128)S(1)}, f32[16,640]{1,0:T(8,128)S(1)}, u32[]{:S(2)}, u32[]{:S(2)}) collective-permute-start(f32[16,640]{1,0:T(8,128)S(1)} %fusion.53), channel_id=1, source_target_pairs={{0,24},{4,28},{8,0},{12,4},{16,8},{20,12},{24,16},{28,20},{1,25},{... | collective-permute-start | bytes 122888 | tf_op jit(solution)/shard_map/ppermute | solution.py:61
  217.3 24.8 %collective-permute-start.41 = (bf16[2,320,640]{2,1,0:T(8,128)(2,1)}, bf16[2,320,640]{2,1,0:T(8,128)(2,1)S(1)}, u32[]{:S(2)}, u32[]{:S(2)}) collective-permute-start(bf16[2,320,640]{2,1,0:T(8,128)(2,1)} %copy-done.4), channel_id=1, source_target_pairs={{0,4},{4,0},{8,12},{12,8},{16,20},{20,16},{24,28},{28,24},{1,5},{5... | collective-permute-start | bytes 2457608 | tf_op jit(solution)/shard_map/ppermute | solution.py:67
  221.6 19.3 %collective-permute-start.42 = (bf16[320,640]{1,0:T(8,128)(2,1)}, bf16[320,640]{1,0:T(8,128)(2,1)S(1)}, u32[]{:S(2)}, u32[]{:S(2)}) collective-permute-start(bf16[320,640]{1,0:T(8,128)(2,1)} %get-tuple-element.239), channel_id=1, source_target_pairs={{0,8},{4,12},{8,16},{12,20},{16,24},{20,28},{24,0},{28,4},{1,9},{5... | collective-permute-start | bytes 1228808 | tf_op jit(solution)/shard_map/ppermute | solution.py:61
  224.1 18.0 %collective-permute-start.43 = (bf16[320,640]{1,0:T(8,128)(2,1)S(1)}, bf16[320,640]{1,0:T(8,128)(2,1)S(1)}, u32[]{:S(2)}, u32[]{:S(2)}) collective-permute-start(bf16[320,640]{1,0:T(8,128)(2,1)S(1)} %get-tuple-element.238), channel_id=1, source_target_pairs={{0,24},{4,28},{8,0},{12,4},{16,8},{20,12},{24,16},{28,20},{1,25},{... | collective-permute-start | bytes 1228808 | tf_op jit(solution)/shard_map/ppermute | solution.py:61
  226.2 12.2 %collective-permute-start.44 = (f32[16,640]{1,0:T(8,128)S(1)}, f32[16,640]{1,0:T(8,128)S(1)}, u32[]{:S(2)}, u32[]{:S(2)}) collective-permute-start(f32[16,640]{1,0:T(8,128)S(1)} %add_add_fusion.1), channel_id=1, source_target_pairs={{0,4},{4,0},{8,12},{12,8},{16,20},{20,16},{24,28},{28,24},{1,5},{5... | collective-permute-start | bytes 122888 | tf_op jit(solution)/shard_map/ppermute | solution.py:67
  227.2 11.3 %collective-permute-start.46 = (f32[16,640]{1,0:T(8,128)S(1)}, f32[16,640]{1,0:T(8,128)}, u32[]{:S(2)}, u32[]{:S(2)}) collective-permute-start(f32[16,640]{1,0:T(8,128)S(1)} %slice.181), channel_id=1, source_target_pairs={{0,2},{1,3},{2,0},{3,1},{4,6},{5,7},{6,4},{7,5},{8,10},{9,11},{10,... | collective-permute-start | bytes 122888 | tf_op jit(solution)/shard_map/ppermute | solution.py:31
  238.5 2.4 collective-permute-start.45
  238.5 2.4 collective-permute-start.47
  242.2 21.1 %collective-permute-start.48 = (bf16[320,640]{1,0:T(8,128)(2,1)S(1)}, bf16[320,640]{1,0:T(8,128)(2,1)S(1)}, u32[]{:S(2)}, u32[]{:S(2)}) collective-permute-start(bf16[320,640]{1,0:T(8,128)(2,1)S(1)} %fusion.23), channel_id=1, source_target_pairs={{0,16},{4,20},{8,24},{12,28},{16,0},{20,4},{24,8},{28,12},{1,17},{... | collective-permute-start | bytes 1228808 | tf_op jit(solution)/shard_map/ppermute | solution.py:61
  (26 other events, 112.9 us)
where the time goes:
time: 265 us; the launch traced here: 264 us
  waiting for transfers between devices  90.1 us (34%)
  starting transfers between devices  69.2 us (26%)
  Pallas kernels  53.5 us (20%)
  other arithmetic  28.9 us (11%)
  matrix products  10.7 us (4%)
  local copies, waits for them, and re-layouts  10.6 us (4%)
    ppermute x21, waiting for transfers between devices, move_slow(): return lax.ppermute(value, 'seq', pairs)  65.7 us
    ppermute x21, starting transfers between devices, move_slow(): return lax.ppermute(value, 'seq', pairs)  38 us
    pallas_call x2, Pallas kernels, add_groups(): pl.pallas_call(functools.partial(group_kernel, n_feat, n_shard // len(ats...  21.1 us
    ppermute x13, starting transfers between devices, move_fast(): return lax.ppermute(value, 'seq', pairs)  17.7 us
    pallas_call x4, Pallas kernels, block_grads(): pl.pallas_call(functools.partial(blocks_kernel, sizes), out_shape=[jax.Sh...  15.4 us
    ppermute x13, waiting for transfers between devices, flip(): lax.ppermute(value, axis, [(i, i ^ bit) for i in range(lax.axis_size(axis...  14.2 us
    pallas_call x1, Pallas kernels, proj(): pl.pallas_call(functools.partial(proj_kernel, n_feat, counts), out_shape=...  11.1 us
    ppermute x13, starting transfers between devices, flip(): lax.ppermute(value, axis, [(i, i ^ bit) for i in range(lax.axis_size(axis...  9.27 us
  transfers between devices with their start and end apart: 49, of which 23 were waited for; matrix products, arithmetic and copies ran while one was open for 15% of the time, Pallas kernels for 20%

commit v1 on v0

--- a/solution.py
+++ b/solution.py
@@ -1,4 +1,5 @@
 import functools
+import math
 
 import jax
 import jax.numpy as jnp
@@ -14,6 +15,7 @@
 f32 = jnp.float32
 bf16 = jnp.bfloat16
 HI = lax.Precision.HIGHEST
+EDGE = 16
 LIGHT = pl.CostEstimate(flops=1, bytes_accessed=1, transcendentals=0)
 MIB = 1024 * 1024
 PROJ_VMEM = 58 * MIB
@@ -184,85 +186,327 @@
     )(idx, *feats, *shards)
 
 
-def group_kernel(n_feat, n_fast, n_use, first, ats, idx, *refs):
-    part = None if first else refs[0]
-    refs = refs if first else refs[1:]
-    n_shard, n_block = n_fast * len(ats), n_use * len(ats)
-    feats = refs[:n_feat]
-    shards = refs[n_feat : n_feat + n_shard]
-    outs = refs[n_feat + n_shard : -4]
-    fbuf, wbuf, fsem, wsem = refs[-4:]
-    count, rows = shards[0].shape[:2]
-    depth = fbuf.shape[2]
-    tile = outs[0].shape[-2]
-    step = pl.program_id(0)
+def bring(n_feat, n_fast, n_use, ats, idx, feats, edges, shards, bufs):
+    fbuf, ebuf, wbuf, fsem, esem, wsem = bufs
+    rows = shards[0].shape[1]
+    depth = feats[0].shape[1]
+    blocks = range(n_use * len(ats))
+
+    def slot(buf, m):
+        return buf.at[:, pl.ds(m * depth, depth)] if len(buf.shape) == 2 else buf.at[m]
 
     def w_copy(i):
         at = ats[i // n_fast] + n_use + i % n_fast
         place = pl.multiple_of((i // n_fast * n_fast + idx[at]) * rows, 16)
         return pltpu.make_async_copy(shards[i], wbuf.at[:, pl.ds(place, rows)], wsem.at[i])
 
+    for m in blocks:
+        for j in range(n_feat):
+
+            @pl.when(idx[ats[m // n_use] + m % n_use] == j)
+            def _():
+                pltpu.make_async_copy(feats[j], slot(fbuf, m), fsem.at[m]).start()
+                pltpu.make_async_copy(edges[j], slot(ebuf, m), esem.at[m]).start()
+
+    for i in range(len(shards)):
+        w_copy(i).start()
+    for i in range(len(shards)):
+        w_copy(i).wait()
+    for m in blocks:
+        pltpu.make_async_copy(edges[0], slot(ebuf, m), esem.at[m]).wait()
+        pltpu.make_async_copy(feats[0], slot(fbuf, m), fsem.at[m]).wait()
+
+
+def product(buf, here, weights):
+    if len(buf.shape) == 2:
+        return jnp.dot(buf[here, :], weights[...], preferred_element_type=f32)
+    depth = buf.shape[2]
+    total = None
+    for m in range(buf.shape[0]):
+        rhs = weights[m * depth : (m + 1) * depth, :]
+        term = jnp.dot(buf[m, here, :], rhs, preferred_element_type=f32)
+        total = term if total is None else total + term
+    return total
+
+
+def part_kernel(n_feat, n_fast, n_use, ats, more, idx, *refs):
+    if more:
+        part, part_edge = refs[:2]
+        refs = refs[2:]
+    n_shard = n_fast * len(ats)
+    feats, edges = refs[:n_feat], refs[n_feat : 2 * n_feat]
+    shards = refs[2 * n_feat : 2 * n_feat + n_shard]
+    out, out_edge = refs[2 * n_feat + n_shard : 2 * n_feat + n_shard + 2]
+    bufs = refs[-6:]
+    fbuf, ebuf, wbuf = bufs[:3]
+    step = pl.program_id(0)
+    tile = out.shape[1]
+
     @pl.when(step == 0)
     def _():
-        for m in range(n_block):
-            for j in range(n_feat):
-
-                @pl.when(idx[ats[m // n_use] + m % n_use] == j)
-                def _():
-                    pltpu.make_async_copy(feats[j], fbuf.at[m], fsem.at[m]).start()
-
-        for i in range(n_shard):
-            w_copy(i).start()
-        for i in range(n_shard):
-            w_copy(i).wait()
-        for m in range(n_block):
-            pltpu.make_async_copy(feats[0], fbuf.at[m], fsem.at[m]).wait()
+        bring(n_feat, n_fast, n_use, ats, idx, feats, edges, shards, bufs)
+        term = product(ebuf, pl.ds(0, EDGE), wbuf.at[1])
+        out_edge[...] = term + part_edge[...] if more else term
 
     here = pl.ds(pl.multiple_of(step * tile, tile), tile)
-    for w in range(count):
-        total = None if first else part[w]
-        for m in range(n_block):
-            rhs = wbuf[w, m * depth : (m + 1) * depth, :]
-            term = jnp.dot(fbuf[m, here, :], rhs, preferred_element_type=f32)
-            total = term if total is None else total + term
-        if len(outs) == 1:
-            outs[0][w] = total
-        else:
-            outs[w][...] = total.astype(bf16)
-
-
-def add_groups(part, feats, shards, idx, ats, n_use, final):
+    for w in range(2):
+        term = product(fbuf, here, wbuf.at[w])
+        out[w] = term + part[w] if more else term
+
+
+def front_kernel(n_feat, n_fast, n_use, ats, idx, part, part_edge, params, m_loc, *refs):
+    n_shard = n_fast * len(ats)
+    feats, edges = refs[:n_feat], refs[n_feat : 2 * n_feat]
+    shards = refs[2 * n_feat : 2 * n_feat + n_shard]
+    gate_out, x_out, edge_out, z_out = refs[2 * n_feat + n_shard : 2 * n_feat + n_shard + 4]
+    xs, zs, ms = refs[-9:-6]
+    bufs = refs[-6:]
+    fbuf, ebuf, wbuf = bufs[:3]
+    step = pl.program_id(0)
+    tile = x_out.shape[0]
+
+    @pl.when(step == 0)
+    def _():
+        bring(n_feat, n_fast, n_use, ats, idx, feats, edges, shards, bufs)
+        edge = (part_edge[...] + product(ebuf, pl.ds(0, EDGE), wbuf.at[1])).astype(bf16)
+        edge_out[...] = edge
+        high, low = halves(m_loc[...])
+        ms[...] = jnp.zeros_like(ms)
+        ms[0:VOCAB, :] = high
+        ms[VOCAB : 2 * VOCAB, :] = low
+        xs[0:8, :] = edge.astype(f32)[EDGE - 8 :, :]
+
+    @pl.when(step > 0)
+    def _():
+        xs[0:8, :] = xs[tile : tile + 8, :]
+
+    here = pl.ds(pl.multiple_of(step * tile, tile), tile)
+    x = (part[1] + product(fbuf, here, wbuf.at[1])).astype(bf16)
+    x_out[...] = x
+    xs[8 : 8 + tile, :] = x.astype(f32)
+    gate = (part[0] + product(fbuf, here, wbuf.at[0])).astype(bf16)
+    gate_out[...] = gate
+    gate = gate.astype(f32)
+    conv = params[4:5, :]
+    for k in range(KERNEL):
+        conv = conv + params[k : k + 1, :] * xs[5 + k : 5 + k + tile, :]
+    gated = conv * jax.nn.sigmoid(conv) * params[5:6, :] * (gate * jax.nn.sigmoid(gate))
+    normed = (gated * params[6:7, :]).astype(bf16)
+    z = lax.dot_general(
+        normed, ms[...], (((1,), (1,)), ((), ())), preferred_element_type=f32
+    )
+    square = jnp.sum(gated * gated, axis=1, keepdims=True)
+    lane = lax.broadcasted_iota(jnp.int32, z.shape, 1)
+    zs[here, :] = jnp.where(lane == 2 * VOCAB, square, z)
+
+    @pl.when(step == pl.num_programs(0) - 1)
+    def _():
+        turned_z = zs[...].T
+        z_out[0:VOCAB, :] = turned_z[0:VOCAB, :] + turned_z[VOCAB : 2 * VOCAB, :]
+        z_out[VOCAB:, :] = turned_z[2 * VOCAB : 2 * VOCAB + 8, :]
+
+
+def halves(value):
+    high = value.astype(bf16)
+    return high, (value - high.astype(f32)).astype(bf16)
+
+
+def in_specs_of(feats, edges, shards):
+    return [pl.BlockSpec(memory_space=pltpu.HBM)] * (len(feats) + len(edges) + len(shards))
+
+
+def buffers_of(feats, shards, n_block):
+    tok, depth = feats[0].shape
     count, rows, cols = shards[0].shape
-    tok, depth = feats[0].shape
-    n_feat, n_shard, n_block = len(feats), len(shards), n_use * len(ats)
+    joined = depth % 128 == 0
+    return [
+        pltpu.VMEM((tok, n_block * depth) if joined else (n_block, tok, depth), bf16),
+        pltpu.VMEM((EDGE, n_block * depth) if joined else (n_block, EDGE, depth), bf16),
+        pltpu.VMEM((count, len(shards) * rows, cols), bf16),
+        pltpu.SemaphoreType.DMA((n_block,)),
+        pltpu.SemaphoreType.DMA((n_block,)),
+        pltpu.SemaphoreType.DMA((len(shards),)),
+    ]
+
+
+def partial_products(parts, feats, edges, shards, idx, ats, n_use):
+    count, rows, cols = shards[0].shape
+    tok = feats[0].shape[0]
+    n_fast = len(shards) // len(ats)
     tile = tok // 4
-    any_spec = pl.BlockSpec(memory_space=pltpu.HBM)
-    whole = pl.BlockSpec((count, tile, cols), lambda i, idx: (0, i, 0))
-    if final:
-        out_shape = [jax.ShapeDtypeStruct((tok, cols), bf16)] * count
-        out_specs = [pl.BlockSpec((tile, cols), lambda i, idx: (i, 0))] * count
-    else:
-        out_shape = [jax.ShapeDtypeStruct((count, tok, cols), f32)]
-        out_specs = [whole]
-    parts = [] if part is None else [part]
+    part_specs = [
+        pl.BlockSpec((count, tile, cols), lambda i, idx: (0, i, 0)),
+        pl.BlockSpec((EDGE, cols), lambda i, idx: (0, 0)),
+    ]
     return pl.pallas_call(
-        functools.partial(group_kernel, n_feat, n_shard // len(ats), n_use, part is None, ats),
-        out_shape=out_shape,
+        functools.partial(part_kernel, len(feats), n_fast, n_use, ats, len(parts) > 0),
+        out_shape=[
+            jax.ShapeDtypeStruct((count, tok, cols), f32),
+            jax.ShapeDtypeStruct((EDGE, cols), f32),
+        ],
         grid_spec=pltpu.PrefetchScalarGridSpec(
             num_scalar_prefetch=1,
             grid=(tok // tile,),
-            in_specs=[whole] * len(parts) + [any_spec] * (n_feat + n_shard),
-            out_specs=out_specs,
-            scratch_shapes=[
-                pltpu.VMEM((n_block, tok, depth), bf16),
-                pltpu.VMEM((count, n_shard * rows, cols), bf16),
-                pltpu.SemaphoreType.DMA((n_block,)),
-                pltpu.SemaphoreType.DMA((n_shard,)),
-            ],
+            in_specs=part_specs[: len(parts)] + in_specs_of(feats, edges, shards),
+            out_specs=part_specs,
+            scratch_shapes=buffers_of(feats, shards, n_use * len(ats)),
         ),
         compiler_params=pltpu.CompilerParams(vmem_limit_bytes=PROJ_VMEM),
         cost_estimate=LIGHT,
-    )(idx, *parts, *feats, *shards)
+    )(idx, *parts, *feats, *edges, *shards)
+
+
+def front(part, part_edge, params, m_loc, feats, edges, shards, idx, ats, n_use):
+    count, rows, cols = shards[0].shape
+    tok = feats[0].shape[0]
+    n_fast = len(shards) // len(ats)
+    tile = tok // 4
+    fixed = [pl.BlockSpec(a.shape, lambda i, idx: (0, 0)) for a in (part_edge, params, m_loc)]
+    rows_spec = pl.BlockSpec((tile, cols), lambda i, idx: (i, 0))
+    return pl.pallas_call(
+        functools.partial(front_kernel, len(feats), n_fast, n_use, ats),
+        out_shape=[
+            jax.ShapeDtypeStruct((tok, cols), bf16),
+            jax.ShapeDtypeStruct((tok, cols), bf16),
+            jax.ShapeDtypeStruct((EDGE, cols), bf16),
+            jax.ShapeDtypeStruct((VOCAB + 8, tok), f32),
+        ],
+        grid_spec=pltpu.PrefetchScalarGridSpec(
+            num_scalar_prefetch=1,
+            grid=(tok // tile,),
+            in_specs=[pl.BlockSpec((count, tile, cols), lambda i, idx: (0, i, 0))]
+            + fixed
+            + in_specs_of(feats, edges, shards),
+            out_specs=[
+                rows_spec,
+                rows_spec,
+                pl.BlockSpec((EDGE, cols), lambda i, idx: (0, 0)),
+                pl.BlockSpec((VOCAB + 8, tok), lambda i, idx: (0, 0)),
+            ],
+            scratch_shapes=[
+                pltpu.VMEM((tile + 8, cols), f32),
+                pltpu.VMEM((tok, 128), f32),
+                pltpu.VMEM((128, cols), bf16),
+            ]
+            + buffers_of(feats, shards, n_use * len(ats)),
+        ),
+        compiler_params=pltpu.CompilerParams(vmem_limit_bytes=PROJ_VMEM),
+        cost_estimate=LIGHT,
+    )(idx, part, part_edge, params, m_loc, *feats, *edges, *shards)
+
+
+def back_kernel(
+    weight, n_sum, gate_in, x_in, edge, params, m_loc, resid_logits, targets, *refs
+):
+    parts = refs[:n_sum]
+    dgate_out, dconv_out, normed_out, dlogit_out, acc, square_out, xs = refs[n_sum:]
+    step = pl.program_id(0)
+    tile = x_in.shape[0]
+
+    @pl.when(step == 0)
+    def _():
+        acc[...] = jnp.zeros_like(acc)
+        xs[0:8, :] = edge[...].astype(f32)[EDGE - 8 :, :]
+
+    @pl.when(step > 0)
+    def _():
+        xs[0:8, :] = xs[tile : tile + 8, :]
+
+    sums = parts[0][...]
+    for other in parts[1:]:
+        sums = sums + other[...]
+    z = sums[0:VOCAB, :]
+    square_out[...] = sums[VOCAB:, :]
+    inverse = lax.rsqrt(sums[VOCAB : VOCAB + 1, :] / INNER + 1e-05)
+    raised = jnp.exp(resid_logits[...] + inverse * z)
+    probs = raised / jnp.sum(raised, axis=0, keepdims=True)
+    row = lax.broadcasted_iota(jnp.int32, probs.shape, 0)
+    onehot = jnp.where(row == targets[...], 1.0, 0.0)
+    dlogit = (probs - onehot) * weight
+    dlogit_out[...] = dlogit
+    dot_gn = jnp.sum(dlogit * z, axis=0, keepdims=True)
+    coef = inverse * inverse * inverse * dot_gn / INNER
+    which = lax.broadcasted_iota(jnp.int32, (8, tile), 0)
+    columns = jnp.where(which == 0, inverse, coef).T
+    inv, coef = columns[:, 0:1], columns[:, 1:2]
+
+    xs[8 : 8 + tile, :] = x_in[...].astype(f32)
+    conv = params[4:5, :]
+    for k in range(KERNEL):
+        conv = conv + params[k : k + 1, :] * xs[5 + k : 5 + k + tile, :]
+    scale, gain = params[5:6, :], params[6:7, :]
+    sig_conv = jax.nn.sigmoid(conv)
+    active = conv * sig_conv
+    gate = gate_in[...].astype(f32)
+    sig_gate = jax.nn.sigmoid(gate)
+    silu_gate = gate * sig_gate
+    gated = active * scale * silu_gate
+    normed = gated * gain
+    normed_out[...] = normed.astype(bf16)
+    high, low = halves(dlogit)
+    sums_out = jnp.dot(
+        jnp.concatenate([high, low], axis=0),
+        (normed * inv).astype(bf16),
+        preferred_element_type=f32,
+    )
+    acc[0:VOCAB, :] += sums_out[0:VOCAB, :] + sums_out[VOCAB:, :]
+    m_high, m_low = halves(m_loc[...])
+    dnormed = lax.dot_general(
+        jnp.concatenate([high, high, low], axis=0),
+        jnp.concatenate([m_high, m_low, m_high], axis=0),
+        (((0,), (0,)), ((), ())),
+        preferred_element_type=f32,
+    )
+    scaled = dnormed * inv
+    acc[VOCAB + 6 : VOCAB + 7, :] += jnp.sum(scaled * gated, axis=0, keepdims=True)
+    dgated = scaled * gain - gated * coef
+    both = dgated * active
+    acc[VOCAB + 5 : VOCAB + 6, :] += jnp.sum(both * silu_gate, axis=0, keepdims=True)
+    dgate_out[...] = (both * scale * slope(gate, sig_gate)).astype(bf16)
+    dconv = dgated * scale * silu_gate * slope(conv, sig_conv)
+    dconv_out[...] = dconv
+    acc[VOCAB + 4 : VOCAB + 5, :] += jnp.sum(dconv, axis=0, keepdims=True)
+    for k in range(KERNEL):
+        tap = jnp.sum(dconv * xs[5 + k : 5 + k + tile, :], axis=0, keepdims=True)
+        acc[VOCAB + k : VOCAB + k + 1, :] += tap
+
+
+def back(gate_pre, x_pre, edge, params, m_loc, sums, resid_logits, targets, weight):
+    tok, cols = x_pre.shape
+    tile = tok // 4
+    rows_spec = pl.BlockSpec((tile, cols), lambda i: (i, 0))
+
+    def fixed(a):
+        return pl.BlockSpec(a.shape, lambda i: (0, 0))
+
+    def tokens(a):
+        return pl.BlockSpec((a.shape[0], tile), lambda i: (0, i))
+
+    return pl.pallas_call(
+        functools.partial(back_kernel, weight, len(sums)),
+        out_shape=[
+            jax.ShapeDtypeStruct((tok, cols), bf16),
+            jax.ShapeDtypeStruct((tok, cols), f32),
+            jax.ShapeDtypeStruct((tok, cols), bf16),
+            jax.ShapeDtypeStruct((VOCAB, tok), f32),
+            jax.ShapeDtypeStruct((VOCAB + 8, cols), f32),
+            jax.ShapeDtypeStruct((8, tok), f32),
+        ],
+        grid=(tok // tile,),
+        in_specs=[rows_spec, rows_spec, fixed(edge), fixed(params), fixed(m_loc)]
+        + [tokens(a) for a in (resid_logits, targets, *sums)],
+        out_specs=[
+            rows_spec,
+            rows_spec,
+            rows_spec,
+            pl.BlockSpec((VOCAB, tile), lambda i: (0, i)),
+            pl.BlockSpec((VOCAB + 8, cols), lambda i: (0, 0)),
+            pl.BlockSpec((8, tile), lambda i: (0, i)),
+        ],
+        scratch_shapes=[pltpu.VMEM((tile + 8, cols), f32)],
+        compiler_params=pltpu.CompilerParams(vmem_limit_bytes=PROJ_VMEM),
+        cost_estimate=LIGHT,
+    )(gate_pre, x_pre, edge, params, m_loc, resid_logits, targets, *sums)
 
 
 def blocks_kernel(sizes, idx, lhs, rhs, *outs):
@@ -278,7 +522,7 @@
             at += 1
 
 
-def block_grads(feat_t, rhs, places, begin, sizes, rows):
+def block_grads(feat_t, rhs, places, begin, sizes, rows, vmem=16 * MIB):
     tok = feat_t.shape[2]
     cols = rhs.shape[1]
 
@@ -299,7 +543,7 @@
                 pl.BlockSpec((size, rows, cols), lambda i, idx: (0, 0, 0)) for size in sizes
             ],
         ),
-        compiler_params=pltpu.CompilerParams(vmem_limit_bytes=16 * MIB),
+        compiler_params=pltpu.CompilerParams(vmem_limit_bytes=vmem),
         cost_estimate=LIGHT,
     )(places, feat_t, rhs)
 
@@ -359,8 +603,8 @@
         came_fast = to_fast(now)
         if k == 0:
             feats = xor_gather(resid, "chan", 2)
-        if k == 1:
-            head_t = after(w_head.T, now)
+            edge = shifted(resid[tok_rows - EDGE :], 1)
+            head_t = w_head.T
             part_m = lax.dot_general(
                 head_t, w_out, (((1,), (1,)), ((), ())), preferred_element_type=f32
             )
@@ -369,103 +613,78 @@
             )
             early = jnp.concatenate([part_m, part_r], axis=1)
             early = early + flip(early, "chan", 1)
-            extra = [early] + feats
-        if k == 2:
+            extra = [idx, edge, early]
+        if k == 1:
             bit = 2
             while bit < chan_count:
                 early = early + flip(early, "chan", bit)
                 bit *= 2
+            own_m, resid_logits = early[:, :w_rows], early[:, w_rows:]
+            pair_m = jnp.concatenate([own_m] + to_fast(own_m), axis=1)
+            edges = xor_gather(after(edge, now), "chan", 2)
+            extra = [pair_m, resid_logits] + feats + edges
+        if k == 2:
             full = []
             for block in feats:
                 full += [block, flip(block, "chan", 1)]
-            feats = full
-            feat_t = turned(feats)
-            part = add_groups(
-                None, feats, shards[: 2 * fast], idx, group_at[:2], n_use, False
-            )[0]
-            own_m, resid_logits = early[:, :w_rows], early[:, w_rows:]
-            own_m = after(own_m, part)
-            pair_m = jnp.concatenate([own_m] + to_fast(own_m), axis=1)
-            extra = [pair_m, resid_logits, feat_t, part] + feats
+            feats, edges = full[:chan_count], full[chan_count:]
+            part, part_edge = partial_products(
+                [], feats, edges, shards[: 2 * fast], idx, group_at[:2], n_use
+            )
+            pair_m = after(pair_m, part)
+            moved_m = [move_slow(pair_m, k) for k in range(1, slow)]
+            extra = [pair_m, resid_logits, part, part_edge] + feats + edges + moved_m
         came, came_fast, extra = sync(came, came_fast, extra)
         now = came[0]
         shards += came_fast
         if k == 0:
-            idx = extra[0]
+            idx, edge, early = extra
         if k == 1:
-            early, feats = extra[0], extra[1:]
-    pair_m, resid_logits, feat_t, part = extra[:4]
-    feats = extra[4:]
+            pair_m, resid_logits, *feats = extra
+    pair_m, resid_logits, part, part_edge = extra[:4]
+    moved_m = extra[4 + 2 * chan_count :]
+    feats, edges = extra[4 : 4 + chan_count], extra[4 + chan_count : 4 + 2 * chan_count]
     shards.append(now)
     came_fast = to_fast(now)
-    moved_m = [move_slow(pair_m, k) for k in range(1, slow)]
+    part, part_edge = partial_products(
+        [part, part_edge], feats, edges, shards[2 * fast : 3 * fast], idx, group_at[2:3], n_use
+    )
+    feat_t = turned([after(feats[0], part)] + feats[1:])
     out_first = after(w_out, now)
     out_pair = jnp.stack([out_first, move_slow(out_first, 1)])
-    came_fast, moved_m, held = sync(came_fast, moved_m, [now, out_pair])
-    now, out_pair = held
-    out_pair_fast = to_fast(out_pair)
-    out_far = [move_slow(out_pair[1], 1), move_slow(out_first, 3)]
-    last = shards[2 * fast : 3 * fast] + [now] + came_fast
-    gate_pre, x_pre = add_groups(part, feats, last, idx, group_at[2:], n_use, True)
-
+    out_third = move_slow(out_first, 3)
+    per_chan = per_feat
     all_m = jnp.concatenate([pair_m] + moved_m, axis=1)
-    per_chan = per_feat
     pieces = [all_m[:, i * w_rows : (i + 1) * w_rows] for i in range(seq_count)]
     m_loc = jnp.concatenate(
         [picked(pieces, sources, chan * per_chan + i) for i in range(per_chan)], axis=1
     )
-    gain_m = m_loc * norm_gain[None, :]
-
-    before = shifted(x_pre[tok_rows - halo :], 1)
-    padded = jnp.concatenate([before, x_pre], axis=0).astype(f32)
-    conv_out = jnp.zeros((tok_rows, local_inner), f32) + conv_bias
-    for offset in range(KERNEL):
-        conv_out = conv_out + conv_weight[offset] * padded[offset : offset + tok_rows]
-    sig_conv = jax.nn.sigmoid(conv_out)
-    active = conv_out * sig_conv
-    gate_f32 = gate_pre.astype(f32)
-    sig_gate = jax.nn.sigmoid(gate_f32)
-    silu_gate = gate_f32 * sig_gate
     head_scale = jnp.repeat(skip_d, HEADDIM)
-    gated = active * head_scale * silu_gate
-    z_part = lax.dot_general(
-        gain_m, gated, (((1,), (1,)), ((), ())), precision=HI, preferred_element_type=f32
-    )
-    sq_part = jnp.sum(gated * gated, axis=1)
-    sums = jnp.concatenate([z_part, jnp.broadcast_to(sq_part[None], (8, tok_rows))])
-    held, out_pair_fast, out_far = sync([sums], out_pair_fast, out_far)
-    sums = xor_sum(held[0], "chan")
-    out_far = jnp.stack(out_far)
+    params = jnp.concatenate(
+        [conv_weight, conv_bias[None], head_scale[None], norm_gain[None], norm_gain[None]], axis=0
+    )
+    came_fast, held = sync(came_fast, [now, out_pair, out_third, feat_t, part, m_loc, params])
+    now, out_pair, out_third, feat_t, part, m_loc, params = held
+    out_pair_fast = to_fast(out_pair)
+    out_far = [move_slow(out_pair[1], 1), out_third]
+    last = [now] + came_fast
+
+    gate_pre, x_pre, x_edge, sums = front(
+        part, part_edge, params, m_loc, feats, edges, last, idx, group_at[3:], n_use
+    )
+    sums = [sums] + [flip(sums, "chan", j) for j in range(1, chan_count)]
+    out_far = jnp.stack([after(out_far[0], sums[0]), out_far[1]])
     out_far_fast = to_fast(out_far)
-    normed = (gated * norm_gain).astype(bf16)
-    normed_x = xor_gather(after(normed, sums), "chan", 2)
-    z_all = sums[:VOCAB]
-    inverse = lax.rsqrt(sums[VOCAB] / INNER + 1e-05)
-    raised = jnp.exp(resid_logits + inverse[None] * z_all)
-    probs = raised / jnp.sum(raised, axis=0, keepdims=True)
-    onehot = (targets[None, :] == jnp.arange(VOCAB, dtype=jnp.int32)[:, None]).astype(f32)
-    loss_weight = 4.0 / jnp.sqrt(jnp.asarray(tok_rows * seq_count, f32))
-    dlogit = (probs - onehot) * loss_weight
-    dot_gn = jnp.sum(dlogit * z_all, axis=0)
-    dnormed = lax.dot_general(
-        dlogit, m_loc, (((0,), (0,)), ((), ())), precision=HI, preferred_element_type=f32
-    )
-    inv = inverse[:, None]
-    dgated = inv * norm_gain * dnormed - gated * (inverse**3 * dot_gn / INNER)[:, None]
-    gain_local = jnp.sum(dnormed * gated * inv, axis=0)
-    skip_local = jnp.sum(dgated * active * silu_gate, axis=0)
-    dgate = (dgated * active * head_scale * slope(gate_f32, sig_gate)).astype(bf16)
-    dconv = dgated * head_scale * silu_gate * slope(conv_out, sig_conv)
-    bias_local = jnp.sum(dconv, axis=0)
-    taps_local = jnp.stack(
-        [jnp.sum(dconv * padded[offset : offset + tok_rows], axis=0) for offset in range(KERNEL)]
-    )
+    loss_weight = 4.0 / math.sqrt(tok_rows * seq_count)
+    dgate, dconv, normed, dlogit, mid, squares = back(
+        gate_pre, x_pre, x_edge, params, m_loc, sums, resid_logits, targets[None], loss_weight
+    )
+    normed_x = xor_gather(normed, "chan", 2)
     future = shifted(dconv[:halo], -1)
 
-    def far_grads(rhs):
-        sizes = [2] * (2 * fast - 2)
-        out = block_grads(feat_t, rhs, idx, n_idx // 2, sizes, w_rows)
-        return out[: fast - 1], out[fast - 1 :]
+    def far_grads(rhs, pair, vmem=16 * MIB):
+        begin = n_idx // 2 + pair * (2 * fast - 2)
+        return block_grads(feat_t, rhs, idx, begin, [2] * (fast - 1), w_rows, vmem)
 
     def near_grads(rhs):
         return block_grads(feat_t, rhs, idx, n_idx // 2 + len(far), [1] * slow, w_rows)
@@ -479,9 +698,8 @@
     def send_slow(own, came, i, k):
         return move_slow(total_of(own, came, i).astype(bf16), k)
 
-    far_gate = far_grads(dgate)
-    gate_first, gate_second, held, out_far_fast = sync(
-        *far_gate, [future, dconv, dlogit, dgate], out_far_fast
+    gate_first, held, out_pair_fast, out_far_fast = sync(
+        far_grads(dgate, 0, PROJ_VMEM), [future, dconv, dlogit, dgate], out_pair_fast, out_far_fast
     )
     future, dconv, dlogit, dgate = held
 
@@ -493,14 +711,10 @@
             dx_sum + conv_weight[offset] * dpadded[halo - offset : halo - offset + tok_rows]
         )
     dx_pre = dx_sum.astype(bf16)
-    out_local = lax.dot_general(
-        dlogit, gated * inv * norm_gain, (((1,), (0,)), ((), ())), precision=HI
-    )
-    mid = jnp.concatenate(
-        [out_local, taps_local, bias_local[None], skip_local[None], gain_local[None]], 0
-    )
+    gate_second = far_grads(dgate, 1)
     gate_own = near_grads(dgate)
-    x_first, x_second = far_grads(dx_pre)
+    x_first = far_grads(dx_pre, 0)
+    x_second = far_grads(dx_pre, 1)
     mid = after(mid, x_first[0], gate_own[0])
     mid_came = [move_slow(mid, k) for k in range(1, slow)]
     gate_first, gate_second, x_first, x_second, gate_own, normed_x, mid_came, held = sync(
@@ -517,20 +731,20 @@
     out_shards = [out_pair] + out_pair_fast + [out_far] + out_far_fast
     counts = [[k * fast + j for k in ks] for ks in ((0, 1), (2, 3)) for j in range(fast)]
     raw = proj(normed_all, out_shards, counts, idx)
-    gate_second, gate_slow, x_first, x_second, held = sync(
-        came, gate_slow, x_first, x_second, [raw, dx_pre]
-    )
-    raw, dx_pre = held
+    x_own = near_grads(dx_pre)
+    gate_second, gate_slow, x_first, x_second, x_own, held = sync(
+        came, gate_slow, x_first, x_second, x_own, [raw]
+    )
+    raw = held[0]
 
     came = send_fast(x_first)
     gate_slow.append(send_slow(gate_own[2], gate_second, 0, second[0]))
-    x_own = near_grads(dx_pre)
+    inv = lax.rsqrt(squares[0] / INNER + 1e-05)[:, None]
     new_resid = (resid.astype(f32) + inv * raw.astype(f32)).astype(bf16)
     head_local = lax.dot_general(
         dlogit, new_resid.astype(f32), (((1,), (0,)), ((), ())), precision=HI
     )
-    mid_came = to_fast(after(mid, x_own[0]))
-    head_local = after(head_local, x_own[0])
+    mid_came = to_fast(mid)
     head_came = [move_slow(head_local, k) for k in range(1, slow)]
     x_first, x_second, x_own, gate_slow, mid_came, head_came, held = sync(
         came, x_second, x_own, gate_slow, mid_came, head_came, [mid, head_local]

time: 265 us -> 260 us (0.981)
  Pallas kernels: 53.5 us -> 76.5 us
  waiting for transfers between devices: 90.1 us -> 73.7 us
  other arithmetic: 28.9 us -> 19.9 us
  matrix products: 10.7 us -> 4.83 us
    ppermute x21, waiting for transfers between devices: 65.7 us -> 33.9 us  [move_slow(): return lax.ppermute(value, 'seq', pairs)]
    pallas_call x2 -> x4, Pallas kernels: 21.1 us -> 42.2 us  [the longest x2 19.4 us: partial_products(): pl.pallas_call(functools.partial(part_kernel, len(feats), n_fast, n_use,...]
    ppermute x13 -> x17, waiting for transfers between devices: 14.2 us -> 24.1 us  [flip(): lax.ppermute(value, axis, [(i, i ^ bit) for i in range(lax.axis_size(axis...]
    ppermute x2, waiting for transfers between devices: 1.15 us -> 7.92 us  [shifted(): lax.ppermute(array, 'seq', [(i, i + by) for i in range(length) if 0 <= i...]
    dot_general x3 -> x0, matrix products: 6.16 us -> none  [the longest x1 2.28 us: per_device(): lax.dot_general(dlogit, m_loc, (((0,), (0,)), ((), ())), precision=HI, pr...]
    convert_element_type x3 -> x0, other arithmetic: 6.01 us -> none  [the longest x1 3.36 us: per_device(): normed = (gated * norm_gain).astype(bf16)]
    reduce_sum x4 -> x0, other arithmetic: 4.88 us -> none  [the longest x1 4.56 us: per_device(): jnp.sum(dconv * padded[offset:offset + tok_rows], axis=0)]
    pallas_call x4 -> x6, Pallas kernels: 15.4 us -> 17.3 us  [block_grads(): pl.pallas_call(functools.partial(blocks_kernel, sizes), out_shape=[jax.Sh...]
  transfers between devices with their start and end apart: 49 -> 53, of which waited for: 23 -> 17; matrix products, arithmetic and copies ran while one was open for 15% -> 11% of each run, Pallas kernels for 20% -> 30%
where the time goes in v1:
time: 260 us; the launch traced here: 258 us
  Pallas kernels  76.5 us (29%)
  waiting for transfers between devices  73.7 us (28%)
  starting transfers between devices  68.9 us (27%)
  other arithmetic  19.9 us (8%)
  local copies, waits for them, and re-layouts  13.1 us (5%)
  matrix products  4.83 us (2%)
    ppermute x21, starting transfers between devices, move_slow(): return lax.ppermute(value, 'seq', pairs)  36.3 us
    ppermute x21, waiting for transfers between devices, move_slow(): return lax.ppermute(value, 'seq', pairs)  33.9 us
    ppermute x17, waiting for transfers between devices, flip(): lax.ppermute(value, axis, [(i, i ^ bit) for i in range(lax.axis_size(axis...  24.1 us
    pallas_call x2, Pallas kernels, partial_products(): pl.pallas_call(functools.partial(part_kernel, len(feats), n_fast, n_use,...  19.4 us
    pallas_call x6, Pallas kernels, block_grads(): pl.pallas_call(functools.partial(blocks_kernel, sizes), out_shape=[jax.Sh...  17.3 us
    ppermute x13, starting transfers between devices, move_fast(): return lax.ppermute(value, 'seq', pairs)  17 us
    pallas_call x1, Pallas kernels, back(): pl.pallas_call(functools.partial(back_kernel, weight, len(sums)), out_sha...  11.7 us
    ppermute x17, starting transfers between devices, flip(): lax.ppermute(value, axis, [(i, i ^ bit) for i in range(lax.axis_size(axis...  11.2 us
  transfers between devices with their start and end apart: 53, of which 17 were waited for; matrix products, arithmetic and copies ran while one was open for 11% of the time, Pallas kernels for 30%

profile of v1, /device:TPU:0, one launch (start us, length us, event | category | flops | bytes accessed | tf_op | source)
XLA Modules:
  0.0 258.4 jit_solution(10312221930526814165)
XLA Ops:
  0.7 1.3 pad_maximum_fusion.refs_8_
  2.0 3.1 %collective-permute-start = (bf16[2,320,640]{2,1,0:T(8,128)(2,1)S(1)}, bf16[2,320,640]{2,1,0:T(8,128)(2,1)}, u32[]{:S(2)}, u32[]{:S(2)}) collective-permute-start(bf16[2,320,640]{2,1,0:T(8,128)(2,1)S(1)} %pad_maximum_fusion.refs_8_), channel_id=1, source_target_pairs={{0,8},{4,12},{8,16},{12,20},{16,24},{20,28},{24,0},{28,4},{1,9},{5... | collective-permute-start | bytes 2457608 | tf_op jit(solution)/shard_map/ppermute | solution.py:63
  5.1 1.5 collective-permute-start.1
  6.6 1.8 fusion.26
  9.4 1.5 collective-permute-start.8
  11.5 3.0 %collective-permute-start.2 = (bf16[16,640]{1,0:T(8,128)(2,1)}, bf16[16,640]{1,0:T(8,128)(2,1)}, u32[]{:S(2)}, u32[]{:S(2)}) collective-permute-start(bf16[16,640]{1,0:T(8,128)(2,1)} %slice.107), channel_id=1, source_target_pairs={{0,4},{4,8},{8,12},{12,16},{16,20},{20,24},{24,28},{1,5},{5,9},{9,... | collective-permute-start | bytes 61448 | tf_op jit(solution)/shard_map/ppermute | solution.py:74
  16.4 7.9 %collective-permute-done.2.refs_4_.refs_6_ = bf16[16,640]{1,0:T(8,128)(2,1)} collective-permute-done((bf16[16,640]{1,0:T(8,128)(2,1)}, bf16[16,640]{1,0:T(8,128)(2,1)}, u32[]{:S(2)}, u32[]{:S(2)}) %collective-permute-start.2) | collective-permute-done | bytes 20512 | tf_op jit(solution)/shard_map/ppermute | solution.py:74
  24.3 1.2 collective-permute-done.refs_10_
  25.5 1.4 collective-permute-start.4
  26.9 1.5 collective-permute-start.5
  28.5 1.5 collective-permute-start.6
  30.0 12.5 %collective-permute-done.6 = f32[16,1344]{1,0:T(8,128)S(1)} collective-permute-done((f32[16,1344]{1,0:T(8,128)S(1)}, f32[16,1344]{1,0:T(8,128)S(1)}, u32[]{:S(2)}, u32[]{:S(2)}) %collective-permute-start.6) | collective-permute-done | bytes 86048 | tf_op jit(solution)/shard_map/ppermute | solution.py:33
  43.1 1.5 collective-permute-start.9
  47.7 1.6 collective-permute-start.10
  49.3 1.5 collective-permute-start.11
  50.8 1.5 collective-permute-done.14.refs_5_.refs_7_
  55.7 9.8 %shard_map.169 = (f32[2,1024,640]{2,1,0:T(8,128)}, f32[16,640]{1,0:T(8,128)}) custom-call(s32[40]{0:T(128)} %concatenate.18.idx, bf16[1024,640]{1,0:T(8,128)(2,1)} %refs_0_.2, bf16[1024,640]{1,0:T(8,128)(2,1)} %copy-done.8, bf16[1024,640]{1,0:T(8,128)(2,1)} %copy-done.7, bf16[1024,640]{1,0:T(8,128)(2,1)} %copy-done.9, ...), custom_call_target="tpu_custom_call" | custom-call | flops 1 | bytes 1 | tf_op jit(solution)/shard_map/pallas_call | solution.py:341
  65.4 1.6 collective-permute-start.16
  67.0 1.2 collective-permute-start.17
  68.3 2.7 %collective-permute-start.18 = (f32[16,640]{1,0:T(8,128)S(1)}, f32[16,640]{1,0:T(8,128)S(1)}, u32[]{:S(2)}, u32[]{:S(2)}) collective-permute-start(f32[16,640]{1,0:T(8,128)S(1)} %pad_maximum_fusion.4), channel_id=1, source_target_pairs={{0,24},{4,28},{8,0},{12,4},{16,8},{20,12},{24,16},{28,20},{1,25},{... | collective-permute-start | bytes 122888 | tf_op jit(solution)/shard_map/ppermute | solution.py:63
  71.3 1.8 collective-permute-done.17
  73.2 1.4 collective-permute-start.19
  78.4 2.7 %collective-permute-start.21 = (bf16[320,640]{1,0:T(8,128)(2,1)}, bf16[320,640]{1,0:T(8,128)(2,1)S(1)}, u32[]{:S(2)}, u32[]{:S(2)}) collective-permute-start(bf16[320,640]{1,0:T(8,128)(2,1)} %param.18), channel_id=1, source_target_pairs={{0,24},{4,28},{8,0},{12,4},{16,8},{20,12},{24,16},{28,20},{1,25},{... | collective-permute-start | bytes 1228808 | tf_op jit(solution)/shard_map/ppermute | solution.py:63
  81.3 9.6 %shard_map.170 = (f32[2,1024,640]{2,1,0:T(8,128)}, f32[16,640]{1,0:T(8,128)}) custom-call(s32[40]{0:T(128)} %concatenate.18.idx, f32[2,1024,640]{2,1,0:T(8,128)} %get-tuple-element.152.refs_0_, f32[16,640]{1,0:T(8,128)} %get-tuple-element.153.refs_1_, bf16[1024,640]{1,0:T(8,128)(2,1)} %refs_0_.2, bf16[1024,640]{1,0:T(8,128)(2,1)} %copy-done.8, ...), custom_call_target="tpu_custom_call" | custom-call | flops 1 | bytes 1 | tf_op jit(solution)/shard_map/pallas_call | solution.py:341
  90.9 6.0 %shard_map.171.lhs = bf16[4,640,1024]{2,1,0:T(8,128)(2,1)} custom-call(bf16[1024,640]{1,0:T(8,128)(2,1)} %refs_0_.2, bf16[1024,640]{1,0:T(8,128)(2,1)} %copy-done.8, bf16[1024,640]{1,0:T(8,128)(2,1)} %copy-done.7, bf16[1024,640]{1,0:T(8,128)(2,1)} %copy-done.9), custom_call_target="tpu_custom_call" | custom-call | flops 1 | bytes 1 | tf_op jit(solution)/shard_map/pallas_call | solution.py:115
  99.4 11.1 %shard_map.172 = (bf16[1024,640]{1,0:T(8,128)(2,1)}, bf16[1024,640]{1,0:T(8,128)(2,1)}, bf16[16,640]{1,0:T(8,128)(2,1)}, f32[24,1024]{1,0:T(8,128)}) custom-call(s32[40]{0:T(128)} %concatenate.18.idx, f32[2,1024,640]{2,1,0:T(8,128)} %get-tuple-element.168.part, f32[16,640]{1,0:T(8,128)} %get-tuple-element.169.part_edge, f32[8,640]{1,0:T(8,128)} %concatenate.22.params, ...), custom_call_target="tpu_custom_call" | custom-call | flops 1 | bytes 1 | tf_op jit(solution)/shard_map/pallas_call | solution.py:366
  111.8 1.5 collective-permute-start.23
  113.7 3.9 %collective-permute-done.23.refs_2_ = f32[24,1024]{1,0:T(8,128)S(1)} collective-permute-done((f32[24,1024]{1,0:T(8,128)}, f32[24,1024]{1,0:T(8,128)S(1)}, u32[]{:S(2)}, u32[]{:S(2)}) %collective-permute-start.23) | collective-permute-done | bytes 98336 | tf_op jit(solution)/shard_map/ppermute | solution.py:33
  117.6 1.3 collective-permute-done.24.refs_3_
  119.6 11.7 %shard_map.173 = (bf16[1024,640]{1,0:T(8,128)(2,1)}, f32[1024,640]{1,0:T(8,128)}, bf16[1024,640]{1,0:T(8,128)(2,1)}, f32[16,1024]{1,0:T(8,128)}, f32[24,640]{1,0:T(8,128)}, /*index=5*/f32[8,1024]{1,0:T(8,128)}) custom-call(bf16[1024,640]{1,0:T(8,128)(2,1)} %get-tuple-element.174.gate_in, bf16[1024,640]{1,0:T(8,128)(2,1)} %get-tuple-element.175.x_in, ...), custom_call_target="tpu_custom_call" | custom-call | flops 1 | bytes 1 | tf_op jit(solution)/shard_map/pallas_call | solution.py:485
  131.3 1.6 collective-permute-start.30
  133.6 1.5 collective-permute-start.25
  135.1 4.7 %shard_map.174 = bf16[2,320,640]{2,1,0:T(8,128)(2,1)} custom-call(s32[40]{0:T(128)} %concatenate.18.idx, bf16[4,640,1024]{2,1,0:T(8,128)(2,1)} %shard_map.171.lhs, bf16[1024,640]{1,0:T(8,128)(2,1)} %get-tuple-element.188.rhs), custom_call_target="tpu_custom_call" | custom-call | flops 1 | bytes 1 | tf_op jit(solution)/shard_map/pallas_call | solution.py:532
  139.8 2.7 %collective-permute-start.29 = (bf16[2,320,640]{2,1,0:T(8,128)(2,1)}, bf16[2,320,640]{2,1,0:T(8,128)(2,1)S(1)}, u32[]{:S(2)}, u32[]{:S(2)}) collective-permute-start(bf16[2,320,640]{2,1,0:T(8,128)(2,1)} %shard_map.174), channel_id=1, source_target_pairs={{0,4},{4,0},{8,12},{12,8},{16,20},{20,16},{24,28},{28,24},{1,5},{5... | collective-permute-start | bytes 2457608 | tf_op jit(solution)/shard_map/ppermute | solution.py:69
  142.8 1.2 fusion.2.rhs
  145.1 2.0 shard_map.176
  147.1 3.4 %shard_map.178 = (bf16[1,320,640]{2,1,0:T(8,128)(2,1)S(1)}, bf16[1,320,640]{2,1,0:T(8,128)(2,1)S(1)}, bf16[1,320,640]{2,1,0:T(8,128)(2,1)S(1)}, bf16[1,320,640]{2,1,0:T(8,128)(2,1)S(1)}) custom-call(s32[40]{0:T(128)S(1)} %copy-done.4, bf16[4,640,1024]{2,1,0:T(8,128)(2,1)S(1)} %bitcast.74, bf16[1024,640]{1,0:T(8,128)(2,1)S(1)} %copy-done.1), custom_call_target="tpu_custom_call" | custom-call | flops 1 | bytes 1 | tf_op jit(solution)/shard_map/pallas_call | solution.py:532
  150.5 1.8 collective-permute-start.31
  152.2 2.4 collective-permute-start.32
  154.6 1.2 collective-permute-start.33
  155.8 1.9 shard_map.175
  157.8 2.0 shard_map.177
  159.8 3.1 %collective-permute-done.30.refs_2_ = bf16[1024,640]{1,0:T(8,128)(2,1)} collective-permute-done((bf16[1024,640]{1,0:T(8,128)(2,1)}, bf16[1024,640]{1,0:T(8,128)(2,1)}, u32[]{:S(2)}, u32[]{:S(2)}) %collective-permute-start.30) | collective-permute-done | bytes 1310752 | tf_op jit(solution)/shard_map/ppermute | solution.py:33
  166.5 2.8 %collective-permute-start.36 = (bf16[320,640]{1,0:T(8,128)(2,1)}, bf16[320,640]{1,0:T(8,128)(2,1)}, u32[]{:S(2)}, u32[]{:S(2)}) collective-permute-start(bf16[320,640]{1,0:T(8,128)(2,1)} %get-tuple-element.264), channel_id=1, source_target_pairs={{0,24},{4,28},{8,0},{12,4},{16,8},{20,12},{24,16},{28,20},{1,25},{... | collective-permute-start | bytes 1228808 | tf_op jit(solution)/shard_map/ppermute | solution.py:63
  170.0 3.4 %shard_map.179 = (bf16[1,320,640]{2,1,0:T(8,128)(2,1)S(1)}, bf16[1,320,640]{2,1,0:T(8,128)(2,1)S(1)}, bf16[1,320,640]{2,1,0:T(8,128)(2,1)S(1)}, bf16[1,320,640]{2,1,0:T(8,128)(2,1)S(1)}) custom-call(s32[40]{0:T(128)S(1)} %copy-done.4, bf16[4,640,1024]{2,1,0:T(8,128)(2,1)S(1)} %bitcast.74, bf16[1024,640]{1,0:T(8,128)(2,1)S(1)} %fusion.2.rhs), custom_call_target="tpu_custom_call" | custom-call | flops 1 | bytes 1 | tf_op jit(solution)/shard_map/pallas_call | solution.py:532
  175.7 11.0 %shard_map.180 = bf16[1024,640]{1,0:T(8,128)(2,1)} custom-call(s32[40]{0:T(128)} %concatenate.18.idx, bf16[1024,640]{1,0:T(8,128)(2,1)} %get-tuple-element.209.refs_0_, bf16[1024,640]{1,0:T(8,128)(2,1)} %copy-done.18, bf16[1024,640]{1,0:T(8,128)(2,1)} %collective-permute-done.30.refs_2_, bf16[1024,640]{1,0:T(8,128)(2,1)} %collective-permute-done.38.refs_3_, ...), custom_call_target="tpu_custom_call" | custom-call | flops 1 | bytes 1 | tf_op jit(solution)/shard_map/pallas_call | solution.py:173
  186.7 1.5 collective-permute-start.39
  188.2 1.9 fusion.6
  191.1 1.8 add_convert_fusion
  194.6 1.8 collective-permute-start.42
  196.3 1.2 collective-permute-start.43
  197.5 2.0 collective-permute-start.44
  199.5 5.0 %collective-permute-done.42 = f32[16,640]{1,0:T(8,128)S(1)} collective-permute-done((f32[16,640]{1,0:T(8,128)S(1)}, f32[16,640]{1,0:T(8,128)S(1)}, u32[]{:S(2)}, u32[]{:S(2)}) %collective-permute-start.42) | collective-permute-done | bytes 40992 | tf_op jit(solution)/shard_map/ppermute | solution.py:63
  204.5 9.3 %collective-permute-done.43 = f32[16,640]{1,0:T(8,128)} collective-permute-done((f32[16,640]{1,0:T(8,128)S(1)}, f32[16,640]{1,0:T(8,128)}, u32[]{:S(2)}, u32[]{:S(2)}) %collective-permute-start.43) | collective-permute-done | bytes 40992 | tf_op jit(solution)/shard_map/ppermute | solution.py:63
  214.2 2.3 fusion.8
  217.3 2.9 %collective-permute-start.47 = (bf16[320,640]{1,0:T(8,128)(2,1)}, bf16[320,640]{1,0:T(8,128)(2,1)S(1)}, u32[]{:S(2)}, u32[]{:S(2)}) collective-permute-start(bf16[320,640]{1,0:T(8,128)(2,1)} %get-tuple-element.262), channel_id=1, source_target_pairs={{0,24},{4,28},{8,0},{12,4},{16,8},{20,12},{24,16},{28,20},{1,25},{... | collective-permute-start | bytes 1228808 | tf_op jit(solution)/shard_map/ppermute | solution.py:63
  221.1 1.8 collective-permute-start.48
  222.9 1.6 collective-permute-start.50
  224.5 2.5 bitcast_add_fusion.1
  227.0 6.6 %collective-permute-done.48 = f32[16,640]{1,0:T(8,128)S(1)} collective-permute-done((f32[16,640]{1,0:T(8,128)S(1)}, f32[16,640]{1,0:T(8,128)S(1)}, u32[]{:S(2)}, u32[]{:S(2)}) %collective-permute-start.48) | collective-permute-done | bytes 40992 | tf_op jit(solution)/shard_map/ppermute | solution.py:69
  236.1 1.6 collective-permute-start.52
  237.7 1.4 add_bitcast_fusion
  239.1 2.3 fusion.11
  241.4 15.9 %collective-permute-done.52 = bf16[320,640]{1,0:T(8,128)(2,1)S(1)} collective-permute-done((bf16[320,640]{1,0:T(8,128)(2,1)S(1)}, bf16[320,640]{1,0:T(8,128)(2,1)S(1)}, u32[]{:S(2)}, u32[]{:S(2)}) %collective-permute-start.52) | collective-permute-done | bytes 409632 | tf_op jit(solution)/shard_map/ppermute | solution.py:63
  (173 shorter events, 36.4 us)
Async XLA Ops:
  0.7 8.7 %copy-start.5 = (bf16[1024,640]{1,0:T(8,128)(2,1)S(1)}, bf16[1024,640]{1,0:T(8,128)(2,1)}, u32[]{:S(2)}) copy-start(bf16[1024,640]{1,0:T(8,128)(2,1)} %refs_0_.2) | copy-start | bytes 3932164
  0.7 7.7 %copy-start.15 = (bf16[320,640]{1,0:T(8,128)(2,1)S(1)}, bf16[320,640]{1,0:T(8,128)(2,1)}, u32[]{:S(2)}) copy-start(bf16[320,640]{1,0:T(8,128)(2,1)} %param.18) | copy-start | bytes 1228804
  2.0 51.5 %copy-start.13 = (bf16[2,320,640]{2,1,0:T(8,128)(2,1)}, bf16[2,320,640]{2,1,0:T(8,128)(2,1)S(1)}, u32[]{:S(2)}) copy-start(bf16[2,320,640]{2,1,0:T(8,128)(2,1)S(1)} %pad_maximum_fusion.refs_8_) | copy-start | bytes 2457604
  2.0 23.5 %collective-permute-start = (bf16[2,320,640]{2,1,0:T(8,128)(2,1)S(1)}, bf16[2,320,640]{2,1,0:T(8,128)(2,1)}, u32[]{:S(2)}, u32[]{:S(2)}) collective-permute-start(bf16[2,320,640]{2,1,0:T(8,128)(2,1)S(1)} %pad_maximum_fusion.refs_8_), channel_id=1, source_target_pairs={{0,8},{4,12},{8,16},{12,20},{16,24},{20,28},{24,0},{28,4},{1,9},{5... | collective-permute-start | bytes 2457608 | tf_op jit(solution)/shard_map/ppermute | solution.py:63
  5.1 20.4 %collective-permute-start.1 = (bf16[2,320,640]{2,1,0:T(8,128)(2,1)S(1)}, bf16[2,320,640]{2,1,0:T(8,128)(2,1)}, u32[]{:S(2)}, u32[]{:S(2)}) collective-permute-start(bf16[2,320,640]{2,1,0:T(8,128)(2,1)S(1)} %pad_maximum_fusion.refs_8_), channel_id=1, source_target_pairs={{0,4},{4,0},{8,12},{12,8},{16,20},{20,16},{24,28},{28,24},{1,5},{5... | collective-permute-start | bytes 2457608 | tf_op jit(solution)/shard_map/ppermute | solution.py:69
  9.4 6.0 %collective-permute-start.3 = (f32[16,1344]{1,0:T(8,128)}, f32[16,1344]{1,0:T(8,128)}, u32[]{:S(2)}, u32[]{:S(2)}) collective-permute-start(f32[16,1344]{1,0:T(8,128)} %pad_maximum_fusion.3), channel_id=1, source_target_pairs={{0,1},{1,0},{2,3},{3,2},{4,5},{5,4},{6,7},{7,6},{8,9},{9,8},{10,11... | collective-permute-start | bytes 258056 | tf_op jit(solution)/shard_map/ppermute | solution.py:33
  9.4 37.7 %collective-permute-start.8 = (bf16[1024,640]{1,0:T(8,128)(2,1)S(1)}, bf16[1024,640]{1,0:T(8,128)(2,1)S(1)}, u32[]{:S(2)}, u32[]{:S(2)}) collective-permute-start(bf16[1024,640]{1,0:T(8,128)(2,1)S(1)} %copy-done.5), channel_id=1, source_target_pairs={{0,2},{1,3},{2,0},{3,1},{4,6},{5,7},{6,4},{7,5},{8,10},{9,11},{10,... | collective-permute-start | bytes 3932168 | tf_op jit(solution)/shard_map/ppermute | solution.py:33
  11.5 12.8 %collective-permute-start.2 = (bf16[16,640]{1,0:T(8,128)(2,1)}, bf16[16,640]{1,0:T(8,128)(2,1)}, u32[]{:S(2)}, u32[]{:S(2)}) collective-permute-start(bf16[16,640]{1,0:T(8,128)(2,1)} %slice.107), channel_id=1, source_target_pairs={{0,4},{4,8},{8,12},{12,16},{16,20},{20,24},{24,28},{1,5},{5,9},{9,... | collective-permute-start | bytes 61448 | tf_op jit(solution)/shard_map/ppermute | solution.py:74
  25.5 21.6 %collective-permute-start.4 = (bf16[2,320,640]{2,1,0:T(8,128)(2,1)}, bf16[2,320,640]{2,1,0:T(8,128)(2,1)}, u32[]{:S(2)}, u32[]{:S(2)}) collective-permute-start(bf16[2,320,640]{2,1,0:T(8,128)(2,1)} %collective-permute-done.refs_10_), channel_id=1, source_target_pairs={{0,8},{4,12},{8,16},{12,20},{16,24},{20,28},{24,0},{28,4},{1,9},{5... | collective-permute-start | bytes 2457608 | tf_op jit(solution)/shard_map/ppermute | solution.py:63
  26.9 20.2 %collective-permute-start.5 = (bf16[2,320,640]{2,1,0:T(8,128)(2,1)}, bf16[2,320,640]{2,1,0:T(8,128)(2,1)S(1)}, u32[]{:S(2)}, u32[]{:S(2)}) collective-permute-start(bf16[2,320,640]{2,1,0:T(8,128)(2,1)} %collective-permute-done.refs_10_), channel_id=1, source_target_pairs={{0,4},{4,0},{8,12},{12,8},{16,20},{20,16},{24,28},{28,24},{1,5},{5... | collective-permute-start | bytes 2457608 | tf_op jit(solution)/shard_map/ppermute | solution.py:69
  28.5 14.0 %collective-permute-start.6 = (f32[16,1344]{1,0:T(8,128)S(1)}, f32[16,1344]{1,0:T(8,128)S(1)}, u32[]{:S(2)}, u32[]{:S(2)}) collective-permute-start(f32[16,1344]{1,0:T(8,128)S(1)} %fusion.24), channel_id=1, source_target_pairs={{0,2},{1,3},{2,0},{3,1},{4,6},{5,7},{6,4},{7,5},{8,10},{9,11},{10,... | collective-permute-start | bytes 258056 | tf_op jit(solution)/shard_map/ppermute | solution.py:33
  42.5 3.9 %collective-permute-start.7 = (f32[16,320]{1,0:T(8,128)S(1)}, f32[16,320]{1,0:T(8,128)S(1)}, u32[]{:S(2)}, u32[]{:S(2)}) collective-permute-start(f32[16,320]{1,0:T(8,128)S(1)} %slice.141), channel_id=1, source_target_pairs={{0,4},{4,0},{8,12},{12,8},{16,20},{20,16},{24,28},{28,24},{1,5},{5... | collective-permute-start | bytes 61448 | tf_op jit(solution)/shard_map/ppermute | solution.py:69
  43.1 4.0 %collective-permute-start.9 = (bf16[16,640]{1,0:T(8,128)(2,1)}, bf16[16,640]{1,0:T(8,128)(2,1)S(1)}, u32[]{:S(2)}, u32[]{:S(2)}) collective-permute-start(bf16[16,640]{1,0:T(8,128)(2,1)} %collective-permute-done.2.refs_4_.refs_6_), channel_id=1, source_target_pairs={{0,2},{1,3},{2,0},{3,1},{4,6},{5,7},{6,4},{7,5},{8,10},{9,11},{10,... | collective-permute-start | bytes 61448 | tf_op jit(solution)/shard_map/ppermute | solution.py:33
  46.5 30.2 %copy-start.31 = (f32[4,640]{1,0:T(4,128)S(1)}, f32[4,640]{1,0:T(4,128)}, u32[]{:S(2)}) copy-start(f32[4,640]{1,0:T(4,128)} %param.14) | copy-start | bytes 30724
  47.1 6.4 %collective-permute-start.12 = (bf16[1024,640]{1,0:T(8,128)(2,1)S(1)}, bf16[1024,640]{1,0:T(8,128)(2,1)S(1)}, u32[]{:S(2)}, u32[]{:S(2)}) collective-permute-start(bf16[1024,640]{1,0:T(8,128)(2,1)S(1)} %copy-done.5), channel_id=1, source_target_pairs={{0,1},{1,0},{2,3},{3,2},{4,5},{5,4},{6,7},{7,6},{8,9},{9,8},{10,11... | collective-permute-start | bytes 3932168 | tf_op jit(solution)/shard_map/ppermute | solution.py:33
  47.2 6.4 %collective-permute-start.13 = (bf16[1024,640]{1,0:T(8,128)(2,1)S(1)}, bf16[1024,640]{1,0:T(8,128)(2,1)S(1)}, u32[]{:S(2)}, u32[]{:S(2)}) collective-permute-start(bf16[1024,640]{1,0:T(8,128)(2,1)S(1)} %collective-permute-done.8.refs_2_.refs_4_), channel_id=1, source_target_pairs={{0,1},{1,0},{2,3},{3,2},{4,5},{5,4},{6,7},{7,6},{8,9},{9,8},{10,11... | collective-permute-start | bytes 3932168 | tf_op jit(solution)/shard_map/ppermute | solution.py:33
  47.7 23.3 %collective-permute-start.10 = (bf16[2,320,640]{2,1,0:T(8,128)(2,1)}, bf16[2,320,640]{2,1,0:T(8,128)(2,1)}, u32[]{:S(2)}, u32[]{:S(2)}) collective-permute-start(bf16[2,320,640]{2,1,0:T(8,128)(2,1)} %collective-permute-done.4.refs_10_), channel_id=1, source_target_pairs={{0,8},{4,12},{8,16},{12,20},{16,24},{20,28},{24,0},{28,4},{1,9},{5... | collective-permute-start | bytes 2457608 | tf_op jit(solution)/shard_map/ppermute | solution.py:63
  49.3 21.7 %collective-permute-start.11 = (bf16[2,320,640]{2,1,0:T(8,128)(2,1)}, bf16[2,320,640]{2,1,0:T(8,128)(2,1)}, u32[]{:S(2)}, u32[]{:S(2)}) collective-permute-start(bf16[2,320,640]{2,1,0:T(8,128)(2,1)} %collective-permute-done.4.refs_10_), channel_id=1, source_target_pairs={{0,4},{4,0},{8,12},{12,8},{16,20},{20,16},{24,28},{28,24},{1,5},{5... | collective-permute-start | bytes 2457608 | tf_op jit(solution)/shard_map/ppermute | solution.py:69
  50.8 1.5 collective-permute-start.14
  52.3 1.2 collective-permute-start.15
  65.4 5.9 %collective-permute-start.16 = (f32[16,640]{1,0:T(8,128)S(1)}, f32[16,640]{1,0:T(8,128)S(1)}, u32[]{:S(2)}, u32[]{:S(2)}) collective-permute-start(f32[16,640]{1,0:T(8,128)S(1)} %pad_maximum_fusion.4), channel_id=1, source_target_pairs={{0,8},{4,12},{8,16},{12,20},{16,24},{20,28},{24,0},{28,4},{1,9},{5... | collective-permute-start | bytes 122888 | tf_op jit(solution)/shard_map/ppermute | solution.py:63
  67.0 6.1 %collective-permute-start.17 = (f32[16,640]{1,0:T(8,128)S(1)}, f32[16,640]{1,0:T(8,128)S(1)}, u32[]{:S(2)}, u32[]{:S(2)}) collective-permute-start(f32[16,640]{1,0:T(8,128)S(1)} %pad_maximum_fusion.4), channel_id=1, source_target_pairs={{0,16},{4,20},{8,24},{12,28},{16,0},{20,4},{24,8},{28,12},{1,17},{... | collective-permute-start | bytes 122888 | tf_op jit(solution)/shard_map/ppermute | solution.py:63
  68.3 4.9 %collective-permute-start.18 = (f32[16,640]{1,0:T(8,128)S(1)}, f32[16,640]{1,0:T(8,128)S(1)}, u32[]{:S(2)}, u32[]{:S(2)}) collective-permute-start(f32[16,640]{1,0:T(8,128)S(1)} %pad_maximum_fusion.4), channel_id=1, source_target_pairs={{0,24},{4,28},{8,0},{12,4},{16,8},{20,12},{24,16},{28,20},{1,25},{... | collective-permute-start | bytes 122888 | tf_op jit(solution)/shard_map/ppermute | solution.py:63
  73.2 24.9 %collective-permute-start.19 = (bf16[2,320,640]{2,1,0:T(8,128)(2,1)}, bf16[2,320,640]{2,1,0:T(8,128)(2,1)S(1)}, u32[]{:S(2)}, u32[]{:S(2)}) collective-permute-start(bf16[2,320,640]{2,1,0:T(8,128)(2,1)} %collective-permute-done.10.refs_8_), channel_id=1, source_target_pairs={{0,4},{4,0},{8,12},{12,8},{16,20},{20,16},{24,28},{28,24},{1,5},{5... | collective-permute-start | bytes 2457608 | tf_op jit(solution)/shard_map/ppermute | solution.py:69
  77.4 20.3 %collective-permute-start.20 = (bf16[320,640]{1,0:T(8,128)(2,1)}, bf16[320,640]{1,0:T(8,128)(2,1)S(1)}, u32[]{:S(2)}, u32[]{:S(2)}) collective-permute-start(bf16[320,640]{1,0:T(8,128)(2,1)} %param.18), channel_id=1, source_target_pairs={{0,8},{4,12},{8,16},{12,20},{16,24},{20,28},{24,0},{28,4},{1,9},{5... | collective-permute-start | bytes 1228808 | tf_op jit(solution)/shard_map/ppermute | solution.py:63
  78.4 19.6 %collective-permute-start.21 = (bf16[320,640]{1,0:T(8,128)(2,1)}, bf16[320,640]{1,0:T(8,128)(2,1)S(1)}, u32[]{:S(2)}, u32[]{:S(2)}) collective-permute-start(bf16[320,640]{1,0:T(8,128)(2,1)} %param.18), channel_id=1, source_target_pairs={{0,24},{4,28},{8,0},{12,4},{16,8},{20,12},{24,16},{28,20},{1,25},{... | collective-permute-start | bytes 1228808 | tf_op jit(solution)/shard_map/ppermute | solution.py:63
  97.8 12.8 %copy-start.12 = (bf16[2,320,640]{2,1,0:T(8,128)(2,1)}, bf16[2,320,640]{2,1,0:T(8,128)(2,1)S(1)}, u32[]{:S(2)}) copy-start(bf16[2,320,640]{2,1,0:T(8,128)(2,1)S(1)} %pad_maximum_fusion.1.refs_4_) | copy-start | bytes 2457604
  98.1 12.4 %collective-permute-start.27 = (bf16[320,640]{1,0:T(8,128)(2,1)S(1)}, bf16[320,640]{1,0:T(8,128)(2,1)S(1)}, u32[]{:S(2)}, u32[]{:S(2)}) collective-permute-start(bf16[320,640]{1,0:T(8,128)(2,1)S(1)} %slice_bitcast_fusion), channel_id=1, source_target_pairs={{0,8},{4,12},{8,16},{12,20},{16,24},{20,28},{24,0},{28,4},{1,9},{5... | collective-permute-start | bytes 1228808 | tf_op jit(solution)/shard_map/ppermute | solution.py:63
  98.5 41.3 %collective-permute-start.26 = (bf16[2,320,640]{2,1,0:T(8,128)(2,1)S(1)}, bf16[2,320,640]{2,1,0:T(8,128)(2,1)S(1)}, u32[]{:S(2)}, u32[]{:S(2)}) collective-permute-start(bf16[2,320,640]{2,1,0:T(8,128)(2,1)S(1)} %pad_maximum_fusion.1.refs_4_), channel_id=1, source_target_pairs={{0,4},{4,0},{8,12},{12,8},{16,20},{20,16},{24,28},{28,24},{1,5},{5... | collective-permute-start | bytes 2457608 | tf_op jit(solution)/shard_map/ppermute | solution.py:69
  110.7 29.1 %copy-start.14 = (bf16[2,320,640]{2,1,0:T(8,128)(2,1)}, bf16[2,320,640]{2,1,0:T(8,128)(2,1)S(1)}, u32[]{:S(2)}) copy-start(bf16[2,320,640]{2,1,0:T(8,128)(2,1)S(1)} %pad_maximum_fusion.2.refs_6_) | copy-start | bytes 2457604
  110.7 29.1 %collective-permute-start.28 = (bf16[2,320,640]{2,1,0:T(8,128)(2,1)S(1)}, bf16[2,320,640]{2,1,0:T(8,128)(2,1)S(1)}, u32[]{:S(2)}, u32[]{:S(2)}) collective-permute-start(bf16[2,320,640]{2,1,0:T(8,128)(2,1)S(1)} %pad_maximum_fusion.2.refs_6_), channel_id=1, source_target_pairs={{0,4},{4,0},{8,12},{12,8},{16,20},{20,16},{24,28},{28,24},{1,5},{5... | collective-permute-start | bytes 2457608 | tf_op jit(solution)/shard_map/ppermute | solution.py:69
  111.8 1.9 collective-permute-start.22
  111.8 5.8 %collective-permute-start.23 = (f32[24,1024]{1,0:T(8,128)}, f32[24,1024]{1,0:T(8,128)S(1)}, u32[]{:S(2)}, u32[]{:S(2)}) collective-permute-start(f32[24,1024]{1,0:T(8,128)} %get-tuple-element.178.refs_0_), channel_id=1, source_target_pairs={{0,2},{1,3},{2,0},{3,1},{4,6},{5,7},{6,4},{7,5},{8,10},{9,11},{10,... | collective-permute-start | bytes 294920 | tf_op jit(solution)/shard_map/ppermute | solution.py:33
  113.3 5.7 %collective-permute-start.24 = (f32[24,1024]{1,0:T(8,128)}, f32[24,1024]{1,0:T(8,128)S(1)}, u32[]{:S(2)}, u32[]{:S(2)}) collective-permute-start(f32[24,1024]{1,0:T(8,128)} %get-tuple-element.178.refs_0_), channel_id=1, source_target_pairs={{0,3},{1,2},{2,1},{3,0},{4,7},{5,6},{6,5},{7,4},{8,11},{9,10},{10,... | collective-permute-start | bytes 294920 | tf_op jit(solution)/shard_map/ppermute | solution.py:33
  131.3 31.6 %collective-permute-start.30 = (bf16[1024,640]{1,0:T(8,128)(2,1)}, bf16[1024,640]{1,0:T(8,128)(2,1)}, u32[]{:S(2)}, u32[]{:S(2)}) collective-permute-start(bf16[1024,640]{1,0:T(8,128)(2,1)} %get-tuple-element.209.refs_0_), channel_id=1, source_target_pairs={{0,2},{1,3},{2,0},{3,1},{4,6},{5,7},{6,4},{7,5},{8,10},{9,11},{10,... | collective-permute-start | bytes 3932168 | tf_op jit(solution)/shard_map/ppermute | solution.py:33
  133.6 6.2 %collective-permute-start.25 = (f32[3,640]{1,0:T(4,128)S(1)}, f32[3,640]{1,0:T(4,128)S(1)}, u32[]{:S(2)}, u32[]{:S(2)}) collective-permute-start(f32[3,640]{1,0:T(4,128)S(1)} %slice.119), channel_id=1, source_target_pairs={{4,0},{8,4},{12,8},{16,12},{20,16},{24,20},{28,24},{5,1},{9,5},{13... | collective-permute-start | bytes 23048 | tf_op jit(solution)/shard_map/ppermute | solution.py:74
  135.1 7.4 %copy-start.10 = (f32[1024,640]{1,0:T(8,128)S(1)}, f32[1024,640]{1,0:T(8,128)}, u32[]{:S(2)}) copy-start(f32[1024,640]{1,0:T(8,128)} %get-tuple-element.189) | copy-start | bytes 7864324
  139.8 23.1 %collective-permute-start.29 = (bf16[2,320,640]{2,1,0:T(8,128)(2,1)}, bf16[2,320,640]{2,1,0:T(8,128)(2,1)S(1)}, u32[]{:S(2)}, u32[]{:S(2)}) collective-permute-start(bf16[2,320,640]{2,1,0:T(8,128)(2,1)} %shard_map.174), channel_id=1, source_target_pairs={{0,4},{4,0},{8,12},{12,8},{16,20},{20,16},{24,28},{28,24},{1,5},{5... | collective-permute-start | bytes 2457608 | tf_op jit(solution)/shard_map/ppermute | solution.py:69
  150.4 7.3 %copy-start.2 = (bf16[1,320,640]{2,1,0:T(8,128)(2,1)}, bf16[1,320,640]{2,1,0:T(8,128)(2,1)S(1)}, u32[]{:S(2)}) copy-start(bf16[1,320,640]{2,1,0:T(8,128)(2,1)S(1)} %get-tuple-element.214) | copy-start | bytes 1228804
  150.5 9.3 %collective-permute-start.31 = (f32[24,640]{1,0:T(8,128)S(1)}, f32[24,640]{1,0:T(8,128)S(1)}, u32[]{:S(2)}, u32[]{:S(2)}) collective-permute-start(f32[24,640]{1,0:T(8,128)S(1)} %copy-done.30), channel_id=1, source_target_pairs={{0,8},{4,12},{8,16},{12,20},{16,24},{20,28},{24,0},{28,4},{1,9},{5... | collective-permute-start | bytes 184328 | tf_op jit(solution)/shard_map/ppermute | solution.py:63
  152.2 7.5 %collective-permute-start.32 = (f32[24,640]{1,0:T(8,128)S(1)}, f32[24,640]{1,0:T(8,128)S(1)}, u32[]{:S(2)}, u32[]{:S(2)}) collective-permute-start(f32[24,640]{1,0:T(8,128)S(1)} %copy-done.30), channel_id=1, source_target_pairs={{0,16},{4,20},{8,24},{12,28},{16,0},{20,4},{24,8},{28,12},{1,17},{... | collective-permute-start | bytes 184328 | tf_op jit(solution)/shard_map/ppermute | solution.py:63
  154.6 5.2 %collective-permute-start.33 = (f32[24,640]{1,0:T(8,128)S(1)}, f32[24,640]{1,0:T(8,128)S(1)}, u32[]{:S(2)}, u32[]{:S(2)}) collective-permute-start(f32[24,640]{1,0:T(8,128)S(1)} %copy-done.30), channel_id=1, source_target_pairs={{0,24},{4,28},{8,0},{12,4},{16,8},{20,12},{24,16},{28,20},{1,25},{... | collective-permute-start | bytes 184328 | tf_op jit(solution)/shard_map/ppermute | solution.py:63
  162.9 10.6 %collective-permute-start.37 = (bf16[1024,640]{1,0:T(8,128)(2,1)S(1)}, bf16[1024,640]{1,0:T(8,128)(2,1)S(1)}, u32[]{:S(2)}, u32[]{:S(2)}) collective-permute-start(bf16[1024,640]{1,0:T(8,128)(2,1)S(1)} %copy-done.17), channel_id=1, source_target_pairs={{0,1},{1,0},{2,3},{3,2},{4,5},{5,4},{6,7},{7,6},{8,9},{9,8},{10,11... | collective-permute-start | bytes 3932168 | tf_op jit(solution)/shard_map/ppermute | solution.py:33
  162.9 12.8 %collective-permute-start.38 = (bf16[1024,640]{1,0:T(8,128)(2,1)}, bf16[1024,640]{1,0:T(8,128)(2,1)}, u32[]{:S(2)}, u32[]{:S(2)}) collective-permute-start(bf16[1024,640]{1,0:T(8,128)(2,1)} %collective-permute-done.30.refs_2_), channel_id=1, source_target_pairs={{0,1},{1,0},{2,3},{3,2},{4,5},{5,4},{6,7},{7,6},{8,9},{9,8},{10,11... | collective-permute-start | bytes 3932168 | tf_op jit(solution)/shard_map/ppermute | solution.py:33
  163.4 23.3 %collective-permute-start.34 = (bf16[2,320,640]{2,1,0:T(8,128)(2,1)S(1)}, bf16[2,320,640]{2,1,0:T(8,128)(2,1)}, u32[]{:S(2)}, u32[]{:S(2)}) collective-permute-start(bf16[2,320,640]{2,1,0:T(8,128)(2,1)S(1)} %shard_map.175), channel_id=1, source_target_pairs={{0,4},{4,0},{8,12},{12,8},{16,20},{20,16},{24,28},{28,24},{1,5},{5... | collective-permute-start | bytes 2457608 | tf_op jit(solution)/shard_map/ppermute | solution.py:69
  165.4 21.3 %collective-permute-start.35 = (bf16[320,640]{1,0:T(8,128)(2,1)}, bf16[320,640]{1,0:T(8,128)(2,1)}, u32[]{:S(2)}, u32[]{:S(2)}) collective-permute-start(bf16[320,640]{1,0:T(8,128)(2,1)} %get-tuple-element.265), channel_id=1, source_target_pairs={{0,8},{4,12},{8,16},{12,20},{16,24},{20,28},{24,0},{28,4},{1,9},{5... | collective-permute-start | bytes 1228808 | tf_op jit(solution)/shard_map/ppermute | solution.py:63
  166.5 20.2 %collective-permute-start.36 = (bf16[320,640]{1,0:T(8,128)(2,1)}, bf16[320,640]{1,0:T(8,128)(2,1)}, u32[]{:S(2)}, u32[]{:S(2)}) collective-permute-start(bf16[320,640]{1,0:T(8,128)(2,1)} %get-tuple-element.264), channel_id=1, source_target_pairs={{0,24},{4,28},{8,0},{12,4},{16,8},{20,12},{24,16},{28,20},{1,25},{... | collective-permute-start | bytes 1228808 | tf_op jit(solution)/shard_map/ppermute | solution.py:63
  173.5 17.6 %copy-start.6 = (bf16[1024,640]{1,0:T(8,128)(2,1)S(1)}, bf16[1024,640]{1,0:T(8,128)(2,1)}, u32[]{:S(2)}) copy-start(bf16[1024,640]{1,0:T(8,128)(2,1)} %refs_0_.2) | copy-start | bytes 3932164
  174.6 22.9 %collective-permute-start.41 = (f32[24,640]{1,0:T(8,128)S(1)}, f32[24,640]{1,0:T(8,128)S(1)}, u32[]{:S(2)}, u32[]{:S(2)}) collective-permute-start(f32[24,640]{1,0:T(8,128)S(1)} %add_add_fusion), channel_id=1, source_target_pairs={{0,4},{4,0},{8,12},{12,8},{16,20},{20,16},{24,28},{28,24},{1,5},{5... | collective-permute-start | bytes 184328 | tf_op jit(solution)/shard_map/ppermute | solution.py:69
  186.7 27.1 %collective-permute-start.39 = (bf16[2,320,640]{2,1,0:T(8,128)(2,1)S(1)}, bf16[2,320,640]{2,1,0:T(8,128)(2,1)}, u32[]{:S(2)}, u32[]{:S(2)}) collective-permute-start(bf16[2,320,640]{2,1,0:T(8,128)(2,1)S(1)} %shard_map.176), channel_id=1, source_target_pairs={{0,4},{4,0},{8,12},{12,8},{16,20},{20,16},{24,28},{28,24},{1,5},{5... | collective-permute-start | bytes 2457608 | tf_op jit(solution)/shard_map/ppermute | solution.py:69
  190.1 23.7 %collective-permute-start.40 = (bf16[320,640]{1,0:T(8,128)(2,1)}, bf16[320,640]{1,0:T(8,128)(2,1)}, u32[]{:S(2)}, u32[]{:S(2)}) collective-permute-start(bf16[320,640]{1,0:T(8,128)(2,1)} %fusion.6), channel_id=1, source_target_pairs={{0,16},{4,20},{8,24},{12,28},{16,0},{20,4},{24,8},{28,12},{1,17},{... | collective-permute-start | bytes 1228808 | tf_op jit(solution)/shard_map/ppermute | solution.py:63
  194.6 9.9 %collective-permute-start.42 = (f32[16,640]{1,0:T(8,128)S(1)}, f32[16,640]{1,0:T(8,128)S(1)}, u32[]{:S(2)}, u32[]{:S(2)}) collective-permute-start(f32[16,640]{1,0:T(8,128)S(1)} %fusion.27), channel_id=1, source_target_pairs={{0,8},{4,12},{8,16},{12,20},{16,24},{20,28},{24,0},{28,4},{1,9},{5... | collective-permute-start | bytes 122888 | tf_op jit(solution)/shard_map/ppermute | solution.py:63
  196.3 17.5 %collective-permute-start.43 = (f32[16,640]{1,0:T(8,128)S(1)}, f32[16,640]{1,0:T(8,128)}, u32[]{:S(2)}, u32[]{:S(2)}) collective-permute-start(f32[16,640]{1,0:T(8,128)S(1)} %fusion.27), channel_id=1, source_target_pairs={{0,16},{4,20},{8,24},{12,28},{16,0},{20,4},{24,8},{28,12},{1,17},{... | collective-permute-start | bytes 122888 | tf_op jit(solution)/shard_map/ppermute | solution.py:63
  197.5 16.3 %collective-permute-start.44 = (f32[16,640]{1,0:T(8,128)S(1)}, f32[16,640]{1,0:T(8,128)}, u32[]{:S(2)}, u32[]{:S(2)}) collective-permute-start(f32[16,640]{1,0:T(8,128)S(1)} %fusion.27), channel_id=1, source_target_pairs={{0,24},{4,28},{8,0},{12,4},{16,8},{20,12},{24,16},{28,20},{1,25},{... | collective-permute-start | bytes 122888 | tf_op jit(solution)/shard_map/ppermute | solution.py:63
  199.5 25.0 %copy-start.3 = (bf16[1,320,640]{2,1,0:T(8,128)(2,1)S(1)}, bf16[1,320,640]{2,1,0:T(8,128)(2,1)}, u32[]{:S(2)}) copy-start(bf16[1,320,640]{2,1,0:T(8,128)(2,1)} %copy-done.2) | copy-start | bytes 1228804
  204.5 12.9 %copy-start.32 = (f32[16,640]{1,0:T(8,128)}, f32[16,640]{1,0:T(8,128)S(1)}, u32[]{:S(2)}) copy-start(f32[16,640]{1,0:T(8,128)S(1)} %collective-permute-done.42) | copy-start | bytes 122884
  213.8 22.2 %collective-permute-start.45 = (bf16[2,320,640]{2,1,0:T(8,128)(2,1)S(1)}, bf16[2,320,640]{2,1,0:T(8,128)(2,1)S(1)}, u32[]{:S(2)}, u32[]{:S(2)}) collective-permute-start(bf16[2,320,640]{2,1,0:T(8,128)(2,1)S(1)} %shard_map.177), channel_id=1, source_target_pairs={{0,4},{4,0},{8,12},{12,8},{16,20},{20,16},{24,28},{28,24},{1,5},{5... | collective-permute-start | bytes 2457608 | tf_op jit(solution)/shard_map/ppermute | solution.py:69
  216.4 19.6 %collective-permute-start.46 = (bf16[320,640]{1,0:T(8,128)(2,1)}, bf16[320,640]{1,0:T(8,128)(2,1)S(1)}, u32[]{:S(2)}, u32[]{:S(2)}) collective-permute-start(bf16[320,640]{1,0:T(8,128)(2,1)} %get-tuple-element.263), channel_id=1, source_target_pairs={{0,8},{4,12},{8,16},{12,20},{16,24},{20,28},{24,0},{28,4},{1,9},{5... | collective-permute-start | bytes 1228808 | tf_op jit(solution)/shard_map/ppermute | solution.py:63
  217.3 18.7 %collective-permute-start.47 = (bf16[320,640]{1,0:T(8,128)(2,1)}, bf16[320,640]{1,0:T(8,128)(2,1)S(1)}, u32[]{:S(2)}, u32[]{:S(2)}) collective-permute-start(bf16[320,640]{1,0:T(8,128)(2,1)} %get-tuple-element.262), channel_id=1, source_target_pairs={{0,24},{4,28},{8,0},{12,4},{16,8},{20,12},{24,16},{28,20},{1,25},{... | collective-permute-start | bytes 1228808 | tf_op jit(solution)/shard_map/ppermute | solution.py:63
  221.1 12.5 %collective-permute-start.48 = (f32[16,640]{1,0:T(8,128)S(1)}, f32[16,640]{1,0:T(8,128)S(1)}, u32[]{:S(2)}, u32[]{:S(2)}) collective-permute-start(f32[16,640]{1,0:T(8,128)S(1)} %add_add_fusion.1), channel_id=1, source_target_pairs={{0,4},{4,0},{8,12},{12,8},{16,20},{20,16},{24,28},{28,24},{1,5},{5... | collective-permute-start | bytes 122888 | tf_op jit(solution)/shard_map/ppermute | solution.py:69
  222.9 10.7 %collective-permute-start.50 = (f32[16,640]{1,0:T(8,128)S(1)}, f32[16,640]{1,0:T(8,128)S(1)}, u32[]{:S(2)}, u32[]{:S(2)}) collective-permute-start(f32[16,640]{1,0:T(8,128)S(1)} %slice.146), channel_id=1, source_target_pairs={{0,2},{1,3},{2,0},{3,1},{4,6},{5,7},{6,4},{7,5},{8,10},{9,11},{10,... | collective-permute-start | bytes 122888 | tf_op jit(solution)/shard_map/ppermute | solution.py:33
  233.6 2.4 collective-permute-start.49
  233.6 2.4 collective-permute-start.51
  236.1 21.2 %collective-permute-start.52 = (bf16[320,640]{1,0:T(8,128)(2,1)S(1)}, bf16[320,640]{1,0:T(8,128)(2,1)S(1)}, u32[]{:S(2)}, u32[]{:S(2)}) collective-permute-start(bf16[320,640]{1,0:T(8,128)(2,1)S(1)} %fusion.9), channel_id=1, source_target_pairs={{0,16},{4,20},{8,24},{12,28},{16,0},{20,4},{24,8},{28,12},{1,17},{... | collective-permute-start | bytes 1228808 | tf_op jit(solution)/shard_map/ppermute | solution.py:63
  (25 other events, 78.9 us)

commit v2 on v1

--- a/solution.py
+++ b/solution.py
@@ -258,7 +258,8 @@
     n_shard = n_fast * len(ats)
     feats, edges = refs[:n_feat], refs[n_feat : 2 * n_feat]
     shards = refs[2 * n_feat : 2 * n_feat + n_shard]
-    gate_out, x_out, edge_out, z_out = refs[2 * n_feat + n_shard : 2 * n_feat + n_shard + 4]
+    outs = refs[2 * n_feat + n_shard :]
+    gate_out, x_out, normed_out, edge_out, z_out = outs[:5]
     xs, zs, ms = refs[-9:-6]
     bufs = refs[-6:]
     fbuf, ebuf, wbuf = bufs[:3]
@@ -292,6 +293,7 @@
         conv = conv + params[k : k + 1, :] * xs[5 + k : 5 + k + tile, :]
     gated = conv * jax.nn.sigmoid(conv) * params[5:6, :] * (gate * jax.nn.sigmoid(gate))
     normed = (gated * params[6:7, :]).astype(bf16)
+    normed_out[...] = normed
     z = lax.dot_general(
         normed, ms[...], (((1,), (1,)), ((), ())), preferred_element_type=f32
     )
@@ -368,6 +370,7 @@
         out_shape=[
             jax.ShapeDtypeStruct((tok, cols), bf16),
             jax.ShapeDtypeStruct((tok, cols), bf16),
+            jax.ShapeDtypeStruct((tok, cols), bf16),
             jax.ShapeDtypeStruct((EDGE, cols), bf16),
             jax.ShapeDtypeStruct((VOCAB + 8, tok), f32),
         ],
@@ -378,6 +381,7 @@
             + fixed
             + in_specs_of(feats, edges, shards),
             out_specs=[
+                rows_spec,
                 rows_spec,
                 rows_spec,
                 pl.BlockSpec((EDGE, cols), lambda i, idx: (0, 0)),
@@ -399,7 +403,7 @@
     weight, n_sum, gate_in, x_in, edge, params, m_loc, resid_logits, targets, *refs
 ):
     parts = refs[:n_sum]
-    dgate_out, dconv_out, normed_out, dlogit_out, acc, square_out, xs = refs[n_sum:]
+    dgate_out, dconv_out, first_out, dlogit_out, acc, square_out, xs = refs[n_sum:]
     step = pl.program_id(0)
     tile = x_in.shape[0]
 
@@ -442,7 +446,6 @@
     silu_gate = gate * sig_gate
     gated = active * scale * silu_gate
     normed = gated * gain
-    normed_out[...] = normed.astype(bf16)
     high, low = halves(dlogit)
     sums_out = jnp.dot(
         jnp.concatenate([high, low], axis=0),
@@ -465,6 +468,11 @@
     dgate_out[...] = (both * scale * slope(gate, sig_gate)).astype(bf16)
     dconv = dgated * scale * silu_gate * slope(conv, sig_conv)
     dconv_out[...] = dconv
+
+    @pl.when(step == 0)
+    def _():
+        first_out[...] = dconv[0:8, :]
+
     acc[VOCAB + 4 : VOCAB + 5, :] += jnp.sum(dconv, axis=0, keepdims=True)
     for k in range(KERNEL):
         tap = jnp.sum(dconv * xs[5 + k : 5 + k + tile, :], axis=0, keepdims=True)
@@ -487,7 +495,7 @@
         out_shape=[
             jax.ShapeDtypeStruct((tok, cols), bf16),
             jax.ShapeDtypeStruct((tok, cols), f32),
-            jax.ShapeDtypeStruct((tok, cols), bf16),
+            jax.ShapeDtypeStruct((8, cols), f32),
             jax.ShapeDtypeStruct((VOCAB, tok), f32),
             jax.ShapeDtypeStruct((VOCAB + 8, cols), f32),
             jax.ShapeDtypeStruct((8, tok), f32),
@@ -498,7 +506,7 @@
         out_specs=[
             rows_spec,
             rows_spec,
-            rows_spec,
+            pl.BlockSpec((8, cols), lambda i: (0, 0)),
             pl.BlockSpec((VOCAB, tile), lambda i: (0, i)),
             pl.BlockSpec((VOCAB + 8, cols), lambda i: (0, 0)),
             pl.BlockSpec((8, tile), lambda i: (0, i)),
@@ -560,7 +568,7 @@
 
 
 def slow_order():
-    return [1, 3, 2, 0]
+    return [2, 3, 1, 0]
 
 
 def per_device(
@@ -613,7 +621,10 @@
             )
             early = jnp.concatenate([part_m, part_r], axis=1)
             early = early + flip(early, "chan", 1)
-            extra = [idx, edge, early]
+            head_scale = jnp.repeat(skip_d, HEADDIM)
+            params = [conv_weight, conv_bias[None], head_scale[None]] + [norm_gain[None]] * 2
+            params = jnp.concatenate(params, axis=0)
+            extra = [idx, edge, early, params]
         if k == 1:
             bit = 2
             while bit < chan_count:
@@ -633,16 +644,15 @@
             )
             pair_m = after(pair_m, part)
             moved_m = [move_slow(pair_m, k) for k in range(1, slow)]
-            extra = [pair_m, resid_logits, part, part_edge] + feats + edges + moved_m
+            extra = [pair_m, resid_logits, part, part_edge] + feats + edges
         came, came_fast, extra = sync(came, came_fast, extra)
         now = came[0]
         shards += came_fast
         if k == 0:
-            idx, edge, early = extra
+            idx, edge, early, params = extra
         if k == 1:
             pair_m, resid_logits, *feats = extra
     pair_m, resid_logits, part, part_edge = extra[:4]
-    moved_m = extra[4 + 2 * chan_count :]
     feats, edges = extra[4 : 4 + chan_count], extra[4 + chan_count : 4 + 2 * chan_count]
     shards.append(now)
     came_fast = to_fast(now)
@@ -659,28 +669,24 @@
     m_loc = jnp.concatenate(
         [picked(pieces, sources, chan * per_chan + i) for i in range(per_chan)], axis=1
     )
-    head_scale = jnp.repeat(skip_d, HEADDIM)
-    params = jnp.concatenate(
-        [conv_weight, conv_bias[None], head_scale[None], norm_gain[None], norm_gain[None]], axis=0
-    )
-    came_fast, held = sync(came_fast, [now, out_pair, out_third, feat_t, part, m_loc, params])
-    now, out_pair, out_third, feat_t, part, m_loc, params = held
+    came_fast, held = sync(came_fast, [now, out_pair, feat_t, part, m_loc])
+    now, out_pair, feat_t, part, m_loc = held
     out_pair_fast = to_fast(out_pair)
     out_far = [move_slow(out_pair[1], 1), out_third]
     last = [now] + came_fast
 
-    gate_pre, x_pre, x_edge, sums = front(
+    gate_pre, x_pre, normed, x_edge, sums = front(
         part, part_edge, params, m_loc, feats, edges, last, idx, group_at[3:], n_use
     )
     sums = [sums] + [flip(sums, "chan", j) for j in range(1, chan_count)]
     out_far = jnp.stack([after(out_far[0], sums[0]), out_far[1]])
     out_far_fast = to_fast(out_far)
     loss_weight = 4.0 / math.sqrt(tok_rows * seq_count)
-    dgate, dconv, normed, dlogit, mid, squares = back(
+    normed_x = xor_gather(after(normed, *sums[1:]), "chan", 2)
+    dgate, dconv, dfirst, dlogit, mid, squares = back(
         gate_pre, x_pre, x_edge, params, m_loc, sums, resid_logits, targets[None], loss_weight
     )
-    normed_x = xor_gather(normed, "chan", 2)
-    future = shifted(dconv[:halo], -1)
+    future = shifted(dfirst, -1)[:halo]
 
     def far_grads(rhs, pair, vmem=16 * MIB):
         begin = n_idx // 2 + pair * (2 * fast - 2)
@@ -695,8 +701,7 @@
     def total_of(own, came, i):
         return own[0].astype(f32) + sum(block[i].astype(f32) for block in came)
 
-    def send_slow(own, came, i, k):
-        return move_slow(total_of(own, came, i).astype(bf16), k)
+    hops = [1, 3]
 
     gate_first, held, out_pair_fast, out_far_fast = sync(
         far_grads(dgate, 0, PROJ_VMEM), [future, dconv, dlogit, dgate], out_pair_fast, out_far_fast
@@ -724,27 +729,30 @@
     mid = slow_total(mid, mid_came)
 
     came = send_fast(gate_second)
-    gate_slow = [send_slow(gate_own[i], gate_first, i, first[i]) for i in range(2)]
+    gate_terms = [total_of(gate_own[i], gate_first, i).astype(bf16) for i in range(2)]
+    gate_slow = [move_slow(term, by) for term, by in zip(gate_terms, hops)]
     normed_all = []
     for block in normed_x:
         normed_all += [block, flip(block, "chan", 1)]
     out_shards = [out_pair] + out_pair_fast + [out_far] + out_far_fast
     counts = [[k * fast + j for k in ks] for ks in ((0, 1), (2, 3)) for j in range(fast)]
     raw = proj(normed_all, out_shards, counts, idx)
-    x_own = near_grads(dx_pre)
-    gate_second, gate_slow, x_first, x_second, x_own, held = sync(
-        came, gate_slow, x_first, x_second, x_own, [raw]
-    )
-    raw = held[0]
+    gate_second, gate_slow, x_first, x_second, held = sync(
+        came, gate_slow, x_first, x_second, [raw, dx_pre]
+    )
+    raw, dx_pre = held
 
     came = send_fast(x_first)
-    gate_slow.append(send_slow(gate_own[2], gate_second, 0, second[0]))
+    term = total_of(gate_own[2], gate_second, 0) + gate_slow[0].astype(f32)
+    gate_slow[0] = move_slow(term.astype(bf16), 1)
     inv = lax.rsqrt(squares[0] / INNER + 1e-05)[:, None]
     new_resid = (resid.astype(f32) + inv * raw.astype(f32)).astype(bf16)
     head_local = lax.dot_general(
         dlogit, new_resid.astype(f32), (((1,), (0,)), ((), ())), precision=HI
     )
+    x_own = near_grads(dx_pre)
     mid_came = to_fast(mid)
+    head_local = after(head_local, x_own[0])
     head_came = [move_slow(head_local, k) for k in range(1, slow)]
     x_first, x_second, x_own, gate_slow, mid_came, head_came, held = sync(
         came, x_second, x_own, gate_slow, mid_came, head_came, [mid, head_local]
@@ -755,12 +763,13 @@
 
     came = send_fast(x_second)
     x_terms = [total_of(x_own[i], x_first, i).astype(bf16) for i in range(2)]
-    x_slow = [move_slow(x_terms[i], first[i]) for i in range(2)]
+    x_slow = [move_slow(term, by) for term, by in zip(x_terms, hops)]
     head_came = to_fast(after(head_local, *x_terms))
     g_pieces = xor_gather(after(mid[:VOCAB], *x_terms), "chan")
     x_second, x_slow, head_came, g_pieces = sync(came, x_slow, head_came, g_pieces)
 
-    x_slow.append(send_slow(x_own[2], x_second, 0, second[0]))
+    term = total_of(x_own[2], x_second, 0) + x_slow[0].astype(f32)
+    x_slow[0] = move_slow(term.astype(bf16), 1)
     head_local = head_local + sum(head_came)
     grad_gate_in = total_of(gate_own[3], gate_second, 1) + sum(
         block.astype(f32) for block in gate_slow

time: 260 us -> 246 us (0.946)
  waiting for transfers between devices: 73.7 us -> 58.6 us
  local copies, waits for them, and re-layouts: 13.1 us -> 17.4 us
  starting transfers between devices: 68.9 us -> 65.9 us
    ppermute x21, waiting for transfers between devices: 33.9 us -> 25.7 us  [move_slow(): return lax.ppermute(value, 'seq', pairs)]
    ppermute x2, waiting for transfers between devices: 7.92 us -> 2.7 us  [shifted(): lax.ppermute(array, 'seq', [(i, i + by) for i in range(length) if 0 <= i...]
    ppermute x17, waiting for transfers between devices: 24.1 us -> 21 us  [flip(): lax.ppermute(value, axis, [(i, i ^ bit) for i in range(lax.axis_size(axis...]
    unnamed x73 -> x75, local copies, waits for them, and re-layouts: 6.18 us -> 8.8 us
  transfers between devices with their start and end apart: 53 -> 53, of which waited for: 17 -> 19; matrix products, arithmetic and copies ran while one was open for 11% -> 12% of each run, Pallas kernels for 30% -> 31%
where the time goes in v2:
time: 246 us; the launch traced here: 245 us
  Pallas kernels  76.5 us (31%)
  starting transfers between devices  65.9 us (27%)
  waiting for transfers between devices  58.6 us (24%)
  other arithmetic  21.3 us (9%)
  local copies, waits for them, and re-layouts  17.4 us (7%)
  matrix products  4.08 us (2%)
    ppermute x21, starting transfers between devices, move_slow(): return lax.ppermute(value, 'seq', pairs)  34.5 us
    ppermute x21, waiting for transfers between devices, move_slow(): return lax.ppermute(value, 'seq', pairs)  25.7 us
    ppermute x17, waiting for transfers between devices, flip(): lax.ppermute(value, axis, [(i, i ^ bit) for i in range(lax.axis_size(axis...  21 us
    pallas_call x2, Pallas kernels, partial_products(): pl.pallas_call(functools.partial(part_kernel, len(feats), n_fast, n_use,...  19.4 us
    pallas_call x6, Pallas kernels, block_grads(): pl.pallas_call(functools.partial(blocks_kernel, sizes), out_shape=[jax.Sh...  17.3 us
    ppermute x13, starting transfers between devices, move_fast(): return lax.ppermute(value, 'seq', pairs)  16.3 us
    pallas_call x1, Pallas kernels, front(): pl.pallas_call(functools.partial(front_kernel, len(feats), n_fast, n_use,...  11.7 us
    pallas_call x1, Pallas kernels, back(): pl.pallas_call(functools.partial(back_kernel, weight, len(sums)), out_sha...  11.1 us
  transfers between devices with their start and end apart: 53, of which 19 were waited for; matrix products, arithmetic and copies ran while one was open for 12% of the time, Pallas kernels for 31%

profile of v2, /device:TPU:0, one launch (start us, length us, event | category | flops | bytes accessed | tf_op | source)
XLA Modules:
  0.0 245.2 jit_solution(3385262025379030609)
XLA Ops:
  0.7 1.3 pad_maximum_fusion.refs_8_
  2.0 3.1 %collective-permute-start = (bf16[2,320,640]{2,1,0:T(8,128)(2,1)S(1)}, bf16[2,320,640]{2,1,0:T(8,128)(2,1)}, u32[]{:S(2)}, u32[]{:S(2)}) collective-permute-start(bf16[2,320,640]{2,1,0:T(8,128)(2,1)S(1)} %pad_maximum_fusion.refs_8_), channel_id=1, source_target_pairs={{0,8},{4,12},{8,16},{12,20},{16,24},{20,28},{24,0},{28,4},{1,9},{5... | collective-permute-start | bytes 2457608 | tf_op jit(solution)/shard_map/ppermute | solution.py:63
  5.1 1.5 collective-permute-start.1
  6.6 1.8 fusion.26
  9.4 1.5 collective-permute-start.8
  11.5 3.0 %collective-permute-start.2 = (bf16[16,640]{1,0:T(8,128)(2,1)}, bf16[16,640]{1,0:T(8,128)(2,1)}, u32[]{:S(2)}, u32[]{:S(2)}) collective-permute-start(bf16[16,640]{1,0:T(8,128)(2,1)} %slice.107), channel_id=1, source_target_pairs={{0,4},{4,8},{8,12},{12,16},{16,20},{20,24},{24,28},{1,5},{5,9},{9,... | collective-permute-start | bytes 61448 | tf_op jit(solution)/shard_map/ppermute | solution.py:74
  15.3 1.3 broadcast_in_dim.40
  16.6 1.3 broadcast_in_dim_reshape.3
  18.6 1.4 concatenate.20.params
  21.6 2.7 %collective-permute-done.2.refs_4_.refs_6_ = bf16[16,640]{1,0:T(8,128)(2,1)} collective-permute-done((bf16[16,640]{1,0:T(8,128)(2,1)}, bf16[16,640]{1,0:T(8,128)(2,1)}, u32[]{:S(2)}, u32[]{:S(2)}) %collective-permute-start.2) | collective-permute-done | bytes 20512 | tf_op jit(solution)/shard_map/ppermute | solution.py:74
  25.5 1.4 collective-permute-start.4
  26.9 1.5 collective-permute-start.5
  28.5 1.5 collective-permute-start.6
  30.0 12.5 %collective-permute-done.6 = f32[16,1344]{1,0:T(8,128)S(1)} collective-permute-done((f32[16,1344]{1,0:T(8,128)S(1)}, f32[16,1344]{1,0:T(8,128)S(1)}, u32[]{:S(2)}, u32[]{:S(2)}) %collective-permute-start.6) | collective-permute-done | bytes 86048 | tf_op jit(solution)/shard_map/ppermute | solution.py:33
  43.1 1.5 collective-permute-start.9
  47.7 1.6 collective-permute-start.10
  49.3 1.5 collective-permute-start.11
  50.8 1.5 collective-permute-done.14.refs_5_.refs_7_
  55.7 9.7 %shard_map.169 = (f32[2,1024,640]{2,1,0:T(8,128)}, f32[16,640]{1,0:T(8,128)}) custom-call(s32[40]{0:T(128)} %concatenate.18.idx, bf16[1024,640]{1,0:T(8,128)(2,1)} %refs_0_.2, bf16[1024,640]{1,0:T(8,128)(2,1)} %copy-done.10, bf16[1024,640]{1,0:T(8,128)(2,1)} %copy-done.9, bf16[1024,640]{1,0:T(8,128)(2,1)} %copy-done.11, ...), custom_call_target="tpu_custom_call" | custom-call | flops 1 | bytes 1 | tf_op jit(solution)/shard_map/pallas_call | solution.py:343
  65.4 4.6 %collective-permute-done.10.refs_8_ = bf16[2,320,640]{2,1,0:T(8,128)(2,1)} collective-permute-done((bf16[2,320,640]{2,1,0:T(8,128)(2,1)}, bf16[2,320,640]{2,1,0:T(8,128)(2,1)}, u32[]{:S(2)}, u32[]{:S(2)}) %collective-permute-start.10) | collective-permute-done | bytes 819232 | tf_op jit(solution)/shard_map/ppermute | solution.py:63
  70.1 1.5 collective-permute-start.16
  71.6 1.7 collective-permute-start.20
  74.4 2.4 collective-permute-start.17
  76.8 9.6 %shard_map.170 = (f32[2,1024,640]{2,1,0:T(8,128)}, f32[16,640]{1,0:T(8,128)}) custom-call(s32[40]{0:T(128)} %concatenate.18.idx, f32[2,1024,640]{2,1,0:T(8,128)} %get-tuple-element.147.refs_0_, f32[16,640]{1,0:T(8,128)} %get-tuple-element.148.refs_1_, bf16[1024,640]{1,0:T(8,128)(2,1)} %refs_0_.2, bf16[1024,640]{1,0:T(8,128)(2,1)} %copy-done.10, ...), custom_call_target="tpu_custom_call" | custom-call | flops 1 | bytes 1 | tf_op jit(solution)/shard_map/pallas_call | solution.py:343
  86.4 6.0 %shard_map.171.lhs = bf16[4,640,1024]{2,1,0:T(8,128)(2,1)} custom-call(bf16[1024,640]{1,0:T(8,128)(2,1)} %refs_0_.2, bf16[1024,640]{1,0:T(8,128)(2,1)} %copy-done.10, bf16[1024,640]{1,0:T(8,128)(2,1)} %copy-done.9, bf16[1024,640]{1,0:T(8,128)(2,1)} %copy-done.11), custom_call_target="tpu_custom_call" | custom-call | flops 1 | bytes 1 | tf_op jit(solution)/shard_map/pallas_call | solution.py:115
  93.8 3.5 %collective-permute-start.27 = (bf16[320,640]{1,0:T(8,128)(2,1)S(1)}, bf16[320,640]{1,0:T(8,128)(2,1)S(1)}, u32[]{:S(2)}, u32[]{:S(2)}) collective-permute-start(bf16[320,640]{1,0:T(8,128)(2,1)S(1)} %copy-done.18), channel_id=1, source_target_pairs={{0,24},{4,28},{8,0},{12,4},{16,8},{20,12},{24,16},{28,20},{1,25},{... | collective-permute-start | bytes 1228808 | tf_op jit(solution)/shard_map/ppermute | solution.py:63
  97.9 11.7 %shard_map.172 = (bf16[1024,640]{1,0:T(8,128)(2,1)}, bf16[1024,640]{1,0:T(8,128)(2,1)}, bf16[1024,640]{1,0:T(8,128)(2,1)}, bf16[16,640]{1,0:T(8,128)(2,1)}, f32[24,1024]{1,0:T(8,128)}) custom-call(s32[40]{0:T(128)} %concatenate.18.idx, f32[2,1024,640]{2,1,0:T(8,128)} %get-tuple-element.160.part, f32[16,640]{1,0:T(8,128)} %get-tuple-element.161.part_edge, ...), custom_call_target="tpu_custom_call" | custom-call | flops 1 | bytes 1 | tf_op jit(solution)/shard_map/pallas_call | solution.py:368
  109.7 1.9 collective-permute-done.27
  112.2 1.5 collective-permute-start.22
  114.1 3.9 %collective-permute-done.22.refs_2_ = f32[24,1024]{1,0:T(8,128)S(1)} collective-permute-done((f32[24,1024]{1,0:T(8,128)}, f32[24,1024]{1,0:T(8,128)S(1)}, u32[]{:S(2)}, u32[]{:S(2)}) %collective-permute-start.22) | collective-permute-done | bytes 98336 | tf_op jit(solution)/shard_map/ppermute | solution.py:33
  118.0 1.3 collective-permute-done.23.refs_3_
  119.3 1.5 collective-permute-start.30
  120.8 11.1 %shard_map.173 = (bf16[1024,640]{1,0:T(8,128)(2,1)}, f32[1024,640]{1,0:T(8,128)}, f32[8,640]{1,0:T(8,128)}, f32[16,1024]{1,0:T(8,128)}, f32[24,640]{1,0:T(8,128)}, /*index=5*/f32[8,1024]{1,0:T(8,128)}) custom-call(bf16[1024,640]{1,0:T(8,128)(2,1)} %get-tuple-element.166.gate_in, bf16[1024,640]{1,0:T(8,128)(2,1)} %get-tuple-element.167.x_in, ...), custom_call_target="tpu_custom_call" | custom-call | flops 1 | bytes 1 | tf_op jit(solution)/shard_map/pallas_call | solution.py:493
  132.0 1.5 collective-permute-start.24
  133.5 4.6 %shard_map.174 = bf16[2,320,640]{2,1,0:T(8,128)(2,1)} custom-call(s32[40]{0:T(128)} %concatenate.18.idx, bf16[4,640,1024]{2,1,0:T(8,128)(2,1)} %shard_map.171.lhs, bf16[1024,640]{1,0:T(8,128)(2,1)} %get-tuple-element.180.rhs), custom_call_target="tpu_custom_call" | custom-call | flops 1 | bytes 1 | tf_op jit(solution)/shard_map/pallas_call | solution.py:540
  138.2 2.7 %collective-permute-start.29 = (bf16[2,320,640]{2,1,0:T(8,128)(2,1)}, bf16[2,320,640]{2,1,0:T(8,128)(2,1)S(1)}, u32[]{:S(2)}, u32[]{:S(2)}) collective-permute-start(bf16[2,320,640]{2,1,0:T(8,128)(2,1)} %shard_map.174), channel_id=1, source_target_pairs={{0,4},{4,0},{8,12},{12,8},{16,20},{20,16},{24,28},{28,24},{1,5},{5... | collective-permute-start | bytes 2457608 | tf_op jit(solution)/shard_map/ppermute | solution.py:69
  143.5 2.0 shard_map.176
  145.5 3.4 %shard_map.178 = (bf16[1,320,640]{2,1,0:T(8,128)(2,1)S(1)}, bf16[1,320,640]{2,1,0:T(8,128)(2,1)S(1)}, bf16[1,320,640]{2,1,0:T(8,128)(2,1)S(1)}, bf16[1,320,640]{2,1,0:T(8,128)(2,1)S(1)}) custom-call(s32[40]{0:T(128)S(1)} %copy-done.5, bf16[4,640,1024]{2,1,0:T(8,128)(2,1)S(1)} %bitcast.78, bf16[1024,640]{1,0:T(8,128)(2,1)S(1)} %copy-done.2), custom_call_target="tpu_custom_call" | custom-call | flops 1 | bytes 1 | tf_op jit(solution)/shard_map/pallas_call | solution.py:540
  148.9 1.8 collective-permute-start.31
  150.6 2.0 collective-permute-start.32
  152.6 1.9 collective-permute-start.33
  154.5 2.0 shard_map.175
  156.5 2.0 shard_map.177
  160.0 1.7 collective-permute-start.34
  162.9 1.7 collective-permute-start.35
  164.5 2.2 collective-permute-start.36
  169.3 11.0 %shard_map.179 = bf16[1024,640]{1,0:T(8,128)(2,1)} custom-call(s32[40]{0:T(128)} %concatenate.18.idx, bf16[1024,640]{1,0:T(8,128)(2,1)} %get-tuple-element.197.refs_0_, bf16[1024,640]{1,0:T(8,128)(2,1)} %copy-done.20, bf16[1024,640]{1,0:T(8,128)(2,1)} %collective-permute-done.30.refs_2_, bf16[1024,640]{1,0:T(8,128)(2,1)} %collective-permute-done.38.refs_3_, ...), custom_call_target="tpu_custom_call" | custom-call | flops 1 | bytes 1 | tf_op jit(solution)/shard_map/pallas_call | solution.py:173
  180.3 4.2 %collective-permute-done.36 = bf16[320,640]{1,0:T(8,128)(2,1)} collective-permute-done((bf16[320,640]{1,0:T(8,128)(2,1)}, bf16[320,640]{1,0:T(8,128)(2,1)}, u32[]{:S(2)}, u32[]{:S(2)}) %collective-permute-start.36) | collective-permute-done | bytes 409632 | tf_op jit(solution)/shard_map/ppermute | solution.py:63
  184.4 1.3 collective-permute-start.39
  185.8 2.1 fusion.5
  188.5 1.8 add_convert_fusion
  192.0 2.5 %copy-done.1 = bf16[4,640,1024]{2,1,0:T(8,128)(2,1)S(1)} copy-done((bf16[4,640,1024]{2,1,0:T(8,128)(2,1)S(1)}, bf16[4,640,1024]{2,1,0:T(8,128)(2,1)}, u32[]{:S(2)}) %copy-start.1) | copy-done | bytes 5242904
  194.5 3.4 %shard_map.180 = (bf16[1,320,640]{2,1,0:T(8,128)(2,1)S(1)}, bf16[1,320,640]{2,1,0:T(8,128)(2,1)S(1)}, bf16[1,320,640]{2,1,0:T(8,128)(2,1)S(1)}, bf16[1,320,640]{2,1,0:T(8,128)(2,1)S(1)}) custom-call(s32[40]{0:T(128)S(1)} %copy-done.6, bf16[4,640,1024]{2,1,0:T(8,128)(2,1)S(1)} %copy-done.1, bf16[1024,640]{1,0:T(8,128)(2,1)S(1)} %fusion.2.rhs), custom_call_target="tpu_custom_call" | custom-call | flops 1 | bytes 1 | tf_op jit(solution)/shard_map/pallas_call | solution.py:540
  198.7 1.3 collective-permute-start.42
  199.9 2.4 collective-permute-start.43
  202.4 1.3 collective-permute-start.44
  207.3 2.3 fusion.9
  210.5 2.8 %collective-permute-start.47 = (bf16[320,640]{1,0:T(8,128)(2,1)}, bf16[320,640]{1,0:T(8,128)(2,1)S(1)}, u32[]{:S(2)}, u32[]{:S(2)}) collective-permute-start(bf16[320,640]{1,0:T(8,128)(2,1)} %get-tuple-element.252), channel_id=1, source_target_pairs={{0,24},{4,28},{8,0},{12,4},{16,8},{20,12},{24,16},{28,20},{1,25},{... | collective-permute-start | bytes 1228808 | tf_op jit(solution)/shard_map/ppermute | solution.py:63
  214.2 1.4 collective-permute-start.48
  216.5 2.4 bitcast_add_fusion.3
  218.9 7.1 %collective-permute-done.48 = f32[16,640]{1,0:T(8,128)S(1)} collective-permute-done((f32[16,640]{1,0:T(8,128)S(1)}, f32[16,640]{1,0:T(8,128)S(1)}, u32[]{:S(2)}, u32[]{:S(2)}) %collective-permute-start.48) | collective-permute-done | bytes 40992 | tf_op jit(solution)/shard_map/ppermute | solution.py:69
  231.3 1.5 fusion.11
  232.8 10.3 %collective-permute-done.52 = bf16[320,640]{1,0:T(8,128)(2,1)S(1)} collective-permute-done((bf16[320,640]{1,0:T(8,128)(2,1)S(1)}, bf16[320,640]{1,0:T(8,128)(2,1)S(1)}, u32[]{:S(2)}, u32[]{:S(2)}) %collective-permute-start.52) | collective-permute-done | bytes 409632 | tf_op jit(solution)/shard_map/ppermute | solution.py:63
  243.1 2.1 bitcast_add_fusion.1
  (175 shorter events, 39.1 us)
Async XLA Ops:
  0.7 8.7 %copy-start.7 = (bf16[1024,640]{1,0:T(8,128)(2,1)S(1)}, bf16[1024,640]{1,0:T(8,128)(2,1)}, u32[]{:S(2)}) copy-start(bf16[1024,640]{1,0:T(8,128)(2,1)} %refs_0_.2) | copy-start | bytes 3932164
  0.7 7.7 %copy-start.17 = (bf16[320,640]{1,0:T(8,128)(2,1)S(1)}, bf16[320,640]{1,0:T(8,128)(2,1)}, u32[]{:S(2)}) copy-start(bf16[320,640]{1,0:T(8,128)(2,1)} %param.18) | copy-start | bytes 1228804
  0.7 14.0 %copy-start.34 = (f32[640]{0:T(1024)S(1)}, f32[640]{0:T(1024)}, u32[]{:S(2)}) copy-start(f32[640]{0:T(1024)} %param.15) | copy-start | bytes 7684
  2.0 51.5 %copy-start.15 = (bf16[2,320,640]{2,1,0:T(8,128)(2,1)}, bf16[2,320,640]{2,1,0:T(8,128)(2,1)S(1)}, u32[]{:S(2)}) copy-start(bf16[2,320,640]{2,1,0:T(8,128)(2,1)S(1)} %pad_maximum_fusion.refs_8_) | copy-start | bytes 2457604
  2.0 23.5 %collective-permute-start = (bf16[2,320,640]{2,1,0:T(8,128)(2,1)S(1)}, bf16[2,320,640]{2,1,0:T(8,128)(2,1)}, u32[]{:S(2)}, u32[]{:S(2)}) collective-permute-start(bf16[2,320,640]{2,1,0:T(8,128)(2,1)S(1)} %pad_maximum_fusion.refs_8_), channel_id=1, source_target_pairs={{0,8},{4,12},{8,16},{12,20},{16,24},{20,28},{24,0},{28,4},{1,9},{5... | collective-permute-start | bytes 2457608 | tf_op jit(solution)/shard_map/ppermute | solution.py:63
  5.1 20.4 %collective-permute-start.1 = (bf16[2,320,640]{2,1,0:T(8,128)(2,1)S(1)}, bf16[2,320,640]{2,1,0:T(8,128)(2,1)}, u32[]{:S(2)}, u32[]{:S(2)}) collective-permute-start(bf16[2,320,640]{2,1,0:T(8,128)(2,1)S(1)} %pad_maximum_fusion.refs_8_), channel_id=1, source_target_pairs={{0,4},{4,0},{8,12},{12,8},{16,20},{20,16},{24,28},{28,24},{1,5},{5... | collective-permute-start | bytes 2457608 | tf_op jit(solution)/shard_map/ppermute | solution.py:69
  9.4 11.2 %collective-permute-start.3 = (f32[16,1344]{1,0:T(8,128)}, f32[16,1344]{1,0:T(8,128)}, u32[]{:S(2)}, u32[]{:S(2)}) collective-permute-start(f32[16,1344]{1,0:T(8,128)} %pad_maximum_fusion.3), channel_id=1, source_target_pairs={{0,1},{1,0},{2,3},{3,2},{4,5},{5,4},{6,7},{7,6},{8,9},{9,8},{10,11... | collective-permute-start | bytes 258056 | tf_op jit(solution)/shard_map/ppermute | solution.py:33
  9.4 37.7 %collective-permute-start.8 = (bf16[1024,640]{1,0:T(8,128)(2,1)S(1)}, bf16[1024,640]{1,0:T(8,128)(2,1)S(1)}, u32[]{:S(2)}, u32[]{:S(2)}) collective-permute-start(bf16[1024,640]{1,0:T(8,128)(2,1)S(1)} %copy-done.7), channel_id=1, source_target_pairs={{0,2},{1,3},{2,0},{3,1},{4,6},{5,7},{6,4},{7,5},{8,10},{9,11},{10,... | collective-permute-start | bytes 3932168 | tf_op jit(solution)/shard_map/ppermute | solution.py:33
  11.5 12.8 %collective-permute-start.2 = (bf16[16,640]{1,0:T(8,128)(2,1)}, bf16[16,640]{1,0:T(8,128)(2,1)}, u32[]{:S(2)}, u32[]{:S(2)}) collective-permute-start(bf16[16,640]{1,0:T(8,128)(2,1)} %slice.107), channel_id=1, source_target_pairs={{0,4},{4,8},{8,12},{12,16},{16,20},{20,24},{24,28},{1,5},{5,9},{9,... | collective-permute-start | bytes 61448 | tf_op jit(solution)/shard_map/ppermute | solution.py:74
  25.5 21.6 %collective-permute-start.4 = (bf16[2,320,640]{2,1,0:T(8,128)(2,1)}, bf16[2,320,640]{2,1,0:T(8,128)(2,1)}, u32[]{:S(2)}, u32[]{:S(2)}) collective-permute-start(bf16[2,320,640]{2,1,0:T(8,128)(2,1)} %collective-permute-done.refs_10_), channel_id=1, source_target_pairs={{0,8},{4,12},{8,16},{12,20},{16,24},{20,28},{24,0},{28,4},{1,9},{5... | collective-permute-start | bytes 2457608 | tf_op jit(solution)/shard_map/ppermute | solution.py:63
  26.9 20.2 %collective-permute-start.5 = (bf16[2,320,640]{2,1,0:T(8,128)(2,1)}, bf16[2,320,640]{2,1,0:T(8,128)(2,1)S(1)}, u32[]{:S(2)}, u32[]{:S(2)}) collective-permute-start(bf16[2,320,640]{2,1,0:T(8,128)(2,1)} %collective-permute-done.refs_10_), channel_id=1, source_target_pairs={{0,4},{4,0},{8,12},{12,8},{16,20},{20,16},{24,28},{28,24},{1,5},{5... | collective-permute-start | bytes 2457608 | tf_op jit(solution)/shard_map/ppermute | solution.py:69
  28.5 14.0 %collective-permute-start.6 = (f32[16,1344]{1,0:T(8,128)S(1)}, f32[16,1344]{1,0:T(8,128)S(1)}, u32[]{:S(2)}, u32[]{:S(2)}) collective-permute-start(f32[16,1344]{1,0:T(8,128)S(1)} %fusion.24), channel_id=1, source_target_pairs={{0,2},{1,3},{2,0},{3,1},{4,6},{5,7},{6,4},{7,5},{8,10},{9,11},{10,... | collective-permute-start | bytes 258056 | tf_op jit(solution)/shard_map/ppermute | solution.py:33
  42.5 3.9 %collective-permute-start.7 = (f32[16,320]{1,0:T(8,128)S(1)}, f32[16,320]{1,0:T(8,128)S(1)}, u32[]{:S(2)}, u32[]{:S(2)}) collective-permute-start(f32[16,320]{1,0:T(8,128)S(1)} %slice.141), channel_id=1, source_target_pairs={{0,4},{4,0},{8,12},{12,8},{16,20},{20,16},{24,28},{28,24},{1,5},{5... | collective-permute-start | bytes 61448 | tf_op jit(solution)/shard_map/ppermute | solution.py:69
  43.1 4.0 %collective-permute-start.9 = (bf16[16,640]{1,0:T(8,128)(2,1)}, bf16[16,640]{1,0:T(8,128)(2,1)S(1)}, u32[]{:S(2)}, u32[]{:S(2)}) collective-permute-start(bf16[16,640]{1,0:T(8,128)(2,1)} %collective-permute-done.2.refs_4_.refs_6_), channel_id=1, source_target_pairs={{0,2},{1,3},{2,0},{3,1},{4,6},{5,7},{6,4},{7,5},{8,10},{9,11},{10,... | collective-permute-start | bytes 61448 | tf_op jit(solution)/shard_map/ppermute | solution.py:33
  47.1 6.4 %collective-permute-start.12 = (bf16[1024,640]{1,0:T(8,128)(2,1)S(1)}, bf16[1024,640]{1,0:T(8,128)(2,1)S(1)}, u32[]{:S(2)}, u32[]{:S(2)}) collective-permute-start(bf16[1024,640]{1,0:T(8,128)(2,1)S(1)} %copy-done.7), channel_id=1, source_target_pairs={{0,1},{1,0},{2,3},{3,2},{4,5},{5,4},{6,7},{7,6},{8,9},{9,8},{10,11... | collective-permute-start | bytes 3932168 | tf_op jit(solution)/shard_map/ppermute | solution.py:33
  47.2 6.4 %collective-permute-start.13 = (bf16[1024,640]{1,0:T(8,128)(2,1)S(1)}, bf16[1024,640]{1,0:T(8,128)(2,1)S(1)}, u32[]{:S(2)}, u32[]{:S(2)}) collective-permute-start(bf16[1024,640]{1,0:T(8,128)(2,1)S(1)} %collective-permute-done.8.refs_2_.refs_4_), channel_id=1, source_target_pairs={{0,1},{1,0},{2,3},{3,2},{4,5},{5,4},{6,7},{7,6},{8,9},{9,8},{10,11... | collective-permute-start | bytes 3932168 | tf_op jit(solution)/shard_map/ppermute | solution.py:33
  47.7 22.3 %collective-permute-start.10 = (bf16[2,320,640]{2,1,0:T(8,128)(2,1)}, bf16[2,320,640]{2,1,0:T(8,128)(2,1)}, u32[]{:S(2)}, u32[]{:S(2)}) collective-permute-start(bf16[2,320,640]{2,1,0:T(8,128)(2,1)} %collective-permute-done.4.refs_10_), channel_id=1, source_target_pairs={{0,8},{4,12},{8,16},{12,20},{16,24},{20,28},{24,0},{28,4},{1,9},{5... | collective-permute-start | bytes 2457608 | tf_op jit(solution)/shard_map/ppermute | solution.py:63
  49.3 20.8 %collective-permute-start.11 = (bf16[2,320,640]{2,1,0:T(8,128)(2,1)}, bf16[2,320,640]{2,1,0:T(8,128)(2,1)}, u32[]{:S(2)}, u32[]{:S(2)}) collective-permute-start(bf16[2,320,640]{2,1,0:T(8,128)(2,1)} %collective-permute-done.4.refs_10_), channel_id=1, source_target_pairs={{0,4},{4,0},{8,12},{12,8},{16,20},{20,16},{24,28},{28,24},{1,5},{5... | collective-permute-start | bytes 2457608 | tf_op jit(solution)/shard_map/ppermute | solution.py:69
  50.8 1.5 collective-permute-start.14
  52.4 1.2 collective-permute-start.15
  70.1 23.4 %collective-permute-start.16 = (bf16[2,320,640]{2,1,0:T(8,128)(2,1)}, bf16[2,320,640]{2,1,0:T(8,128)(2,1)S(1)}, u32[]{:S(2)}, u32[]{:S(2)}) collective-permute-start(bf16[2,320,640]{2,1,0:T(8,128)(2,1)} %collective-permute-done.10.refs_8_), channel_id=1, source_target_pairs={{0,4},{4,0},{8,12},{12,8},{16,20},{20,16},{24,28},{28,24},{1,5},{5... | collective-permute-start | bytes 2457608 | tf_op jit(solution)/shard_map/ppermute | solution.py:69
  71.6 20.8 %collective-permute-start.20 = (f32[16,640]{1,0:T(8,128)S(1)}, f32[16,640]{1,0:T(8,128)S(1)}, u32[]{:S(2)}, u32[]{:S(2)}) collective-permute-start(f32[16,640]{1,0:T(8,128)S(1)} %pad_maximum_fusion.4), channel_id=1, source_target_pairs={{0,24},{4,28},{8,0},{12,4},{16,8},{20,12},{24,16},{28,20},{1,25},{... | collective-permute-start | bytes 122888 | tf_op jit(solution)/shard_map/ppermute | solution.py:63
  73.3 19.1 %collective-permute-start.19 = (f32[16,640]{1,0:T(8,128)S(1)}, f32[16,640]{1,0:T(8,128)S(1)}, u32[]{:S(2)}, u32[]{:S(2)}) collective-permute-start(f32[16,640]{1,0:T(8,128)S(1)} %pad_maximum_fusion.4), channel_id=1, source_target_pairs={{0,16},{4,20},{8,24},{12,28},{16,0},{20,4},{24,8},{28,12},{1,17},{... | collective-permute-start | bytes 122888 | tf_op jit(solution)/shard_map/ppermute | solution.py:63
  74.1 18.3 %collective-permute-start.18 = (f32[16,640]{1,0:T(8,128)S(1)}, f32[16,640]{1,0:T(8,128)S(1)}, u32[]{:S(2)}, u32[]{:S(2)}) collective-permute-start(f32[16,640]{1,0:T(8,128)S(1)} %pad_maximum_fusion.4), channel_id=1, source_target_pairs={{0,8},{4,12},{8,16},{12,20},{16,24},{20,28},{24,0},{28,4},{1,9},{5... | collective-permute-start | bytes 122888 | tf_op jit(solution)/shard_map/ppermute | solution.py:63
  74.4 18.9 %collective-permute-start.17 = (bf16[320,640]{1,0:T(8,128)(2,1)}, bf16[320,640]{1,0:T(8,128)(2,1)S(1)}, u32[]{:S(2)}, u32[]{:S(2)}) collective-permute-start(bf16[320,640]{1,0:T(8,128)(2,1)} %param.18), channel_id=1, source_target_pairs={{0,8},{4,12},{8,16},{12,20},{16,24},{20,28},{24,0},{28,4},{1,9},{5... | collective-permute-start | bytes 1228808 | tf_op jit(solution)/shard_map/ppermute | solution.py:63
  93.4 16.2 %copy-start.14 = (bf16[2,320,640]{2,1,0:T(8,128)(2,1)}, bf16[2,320,640]{2,1,0:T(8,128)(2,1)S(1)}, u32[]{:S(2)}) copy-start(bf16[2,320,640]{2,1,0:T(8,128)(2,1)S(1)} %pad_maximum_fusion.1.refs_4_) | copy-start | bytes 2457604
  93.5 16.2 %collective-permute-start.26 = (bf16[320,640]{1,0:T(8,128)(2,1)S(1)}, bf16[320,640]{1,0:T(8,128)(2,1)S(1)}, u32[]{:S(2)}, u32[]{:S(2)}) collective-permute-start(bf16[320,640]{1,0:T(8,128)(2,1)S(1)} %slice_bitcast_fusion), channel_id=1, source_target_pairs={{0,8},{4,12},{8,16},{12,20},{16,24},{20,28},{24,0},{28,4},{1,9},{5... | collective-permute-start | bytes 1228808 | tf_op jit(solution)/shard_map/ppermute | solution.py:63
  93.8 17.7 %collective-permute-start.27 = (bf16[320,640]{1,0:T(8,128)(2,1)S(1)}, bf16[320,640]{1,0:T(8,128)(2,1)S(1)}, u32[]{:S(2)}, u32[]{:S(2)}) collective-permute-start(bf16[320,640]{1,0:T(8,128)(2,1)S(1)} %copy-done.18), channel_id=1, source_target_pairs={{0,24},{4,28},{8,0},{12,4},{16,8},{20,12},{24,16},{28,20},{1,25},{... | collective-permute-start | bytes 1228808 | tf_op jit(solution)/shard_map/ppermute | solution.py:63
  97.4 40.8 %collective-permute-start.25 = (bf16[2,320,640]{2,1,0:T(8,128)(2,1)S(1)}, bf16[2,320,640]{2,1,0:T(8,128)(2,1)S(1)}, u32[]{:S(2)}, u32[]{:S(2)}) collective-permute-start(bf16[2,320,640]{2,1,0:T(8,128)(2,1)S(1)} %pad_maximum_fusion.1.refs_4_), channel_id=1, source_target_pairs={{0,4},{4,0},{8,12},{12,8},{16,20},{20,16},{24,28},{28,24},{1,5},{5... | collective-permute-start | bytes 2457608 | tf_op jit(solution)/shard_map/ppermute | solution.py:69
  109.6 23.8 %copy-start.33 = (f32[4,640]{1,0:T(4,128)S(1)}, f32[4,640]{1,0:T(4,128)}, u32[]{:S(2)}) copy-start(f32[4,640]{1,0:T(4,128)} %param.14) | copy-start | bytes 30724
  111.6 26.5 %copy-start.16 = (bf16[2,320,640]{2,1,0:T(8,128)(2,1)}, bf16[2,320,640]{2,1,0:T(8,128)(2,1)S(1)}, u32[]{:S(2)}) copy-start(bf16[2,320,640]{2,1,0:T(8,128)(2,1)S(1)} %pad_maximum_fusion.2.refs_6_) | copy-start | bytes 2457604
  111.6 26.6 %collective-permute-start.28 = (bf16[2,320,640]{2,1,0:T(8,128)(2,1)S(1)}, bf16[2,320,640]{2,1,0:T(8,128)(2,1)S(1)}, u32[]{:S(2)}, u32[]{:S(2)}) collective-permute-start(bf16[2,320,640]{2,1,0:T(8,128)(2,1)S(1)} %pad_maximum_fusion.2.refs_6_), channel_id=1, source_target_pairs={{0,4},{4,0},{8,12},{12,8},{16,20},{20,16},{24,28},{28,24},{1,5},{5... | collective-permute-start | bytes 2457608 | tf_op jit(solution)/shard_map/ppermute | solution.py:69
  112.2 1.9 collective-permute-start.21
  112.2 5.8 %collective-permute-start.22 = (f32[24,1024]{1,0:T(8,128)}, f32[24,1024]{1,0:T(8,128)S(1)}, u32[]{:S(2)}, u32[]{:S(2)}) collective-permute-start(f32[24,1024]{1,0:T(8,128)} %get-tuple-element.170.refs_0_), channel_id=1, source_target_pairs={{0,2},{1,3},{2,0},{3,1},{4,6},{5,7},{6,4},{7,5},{8,10},{9,11},{10,... | collective-permute-start | bytes 294920 | tf_op jit(solution)/shard_map/ppermute | solution.py:33
  113.7 5.6 %collective-permute-start.23 = (f32[24,1024]{1,0:T(8,128)}, f32[24,1024]{1,0:T(8,128)S(1)}, u32[]{:S(2)}, u32[]{:S(2)}) collective-permute-start(f32[24,1024]{1,0:T(8,128)} %get-tuple-element.170.refs_0_), channel_id=1, source_target_pairs={{0,3},{1,2},{2,1},{3,0},{4,7},{5,6},{6,5},{7,4},{8,11},{9,10},{10,... | collective-permute-start | bytes 294920 | tf_op jit(solution)/shard_map/ppermute | solution.py:33
  119.3 39.2 %collective-permute-start.30 = (bf16[1024,640]{1,0:T(8,128)(2,1)}, bf16[1024,640]{1,0:T(8,128)(2,1)}, u32[]{:S(2)}, u32[]{:S(2)}) collective-permute-start(bf16[1024,640]{1,0:T(8,128)(2,1)} %get-tuple-element.197.refs_0_), channel_id=1, source_target_pairs={{0,2},{1,3},{2,0},{3,1},{4,6},{5,7},{6,4},{7,5},{8,10},{9,11},{10,... | collective-permute-start | bytes 3932168 | tf_op jit(solution)/shard_map/ppermute | solution.py:33
  132.0 6.2 %collective-permute-start.24 = (f32[8,640]{1,0:T(8,128)}, f32[8,640]{1,0:T(8,128)S(1)}, u32[]{:S(2)}, u32[]{:S(2)}) collective-permute-start(f32[8,640]{1,0:T(8,128)} %get-tuple-element.174), channel_id=1, source_target_pairs={{4,0},{8,4},{12,8},{16,12},{20,16},{24,20},{28,24},{5,1},{9,5},{13... | collective-permute-start | bytes 61448 | tf_op jit(solution)/shard_map/ppermute | solution.py:74
  133.5 7.4 %copy-start.12 = (f32[1024,640]{1,0:T(8,128)S(1)}, f32[1024,640]{1,0:T(8,128)}, u32[]{:S(2)}) copy-start(f32[1024,640]{1,0:T(8,128)} %get-tuple-element.181) | copy-start | bytes 7864324
  138.2 21.3 %collective-permute-start.29 = (bf16[2,320,640]{2,1,0:T(8,128)(2,1)}, bf16[2,320,640]{2,1,0:T(8,128)(2,1)S(1)}, u32[]{:S(2)}, u32[]{:S(2)}) collective-permute-start(bf16[2,320,640]{2,1,0:T(8,128)(2,1)} %shard_map.174), channel_id=1, source_target_pairs={{0,4},{4,0},{8,12},{12,8},{16,20},{20,16},{24,28},{28,24},{1,5},{5... | collective-permute-start | bytes 2457608 | tf_op jit(solution)/shard_map/ppermute | solution.py:69
  148.9 9.6 %collective-permute-start.31 = (f32[24,640]{1,0:T(8,128)S(1)}, f32[24,640]{1,0:T(8,128)S(1)}, u32[]{:S(2)}, u32[]{:S(2)}) collective-permute-start(f32[24,640]{1,0:T(8,128)S(1)} %copy-done.32), channel_id=1, source_target_pairs={{0,8},{4,12},{8,16},{12,20},{16,24},{20,28},{24,0},{28,4},{1,9},{5... | collective-permute-start | bytes 184328 | tf_op jit(solution)/shard_map/ppermute | solution.py:63
  150.6 7.9 %collective-permute-start.32 = (f32[24,640]{1,0:T(8,128)S(1)}, f32[24,640]{1,0:T(8,128)S(1)}, u32[]{:S(2)}, u32[]{:S(2)}) collective-permute-start(f32[24,640]{1,0:T(8,128)S(1)} %copy-done.32), channel_id=1, source_target_pairs={{0,16},{4,20},{8,24},{12,28},{16,0},{20,4},{24,8},{28,12},{1,17},{... | collective-permute-start | bytes 184328 | tf_op jit(solution)/shard_map/ppermute | solution.py:63
  152.6 5.9 %collective-permute-start.33 = (f32[24,640]{1,0:T(8,128)S(1)}, f32[24,640]{1,0:T(8,128)S(1)}, u32[]{:S(2)}, u32[]{:S(2)}) collective-permute-start(f32[24,640]{1,0:T(8,128)S(1)} %copy-done.32), channel_id=1, source_target_pairs={{0,24},{4,28},{8,0},{12,4},{16,8},{20,12},{24,16},{28,20},{1,25},{... | collective-permute-start | bytes 184328 | tf_op jit(solution)/shard_map/ppermute | solution.py:63
  159.5 8.0 %collective-permute-start.37 = (bf16[1024,640]{1,0:T(8,128)(2,1)S(1)}, bf16[1024,640]{1,0:T(8,128)(2,1)S(1)}, u32[]{:S(2)}, u32[]{:S(2)}) collective-permute-start(bf16[1024,640]{1,0:T(8,128)(2,1)S(1)} %copy-done.19), channel_id=1, source_target_pairs={{0,1},{1,0},{2,3},{3,2},{4,5},{5,4},{6,7},{7,6},{8,9},{9,8},{10,11... | collective-permute-start | bytes 3932168 | tf_op jit(solution)/shard_map/ppermute | solution.py:33
  159.5 9.8 %collective-permute-start.38 = (bf16[1024,640]{1,0:T(8,128)(2,1)}, bf16[1024,640]{1,0:T(8,128)(2,1)}, u32[]{:S(2)}, u32[]{:S(2)}) collective-permute-start(bf16[1024,640]{1,0:T(8,128)(2,1)} %collective-permute-done.30.refs_2_), channel_id=1, source_target_pairs={{0,1},{1,0},{2,3},{3,2},{4,5},{5,4},{6,7},{7,6},{8,9},{9,8},{10,11... | collective-permute-start | bytes 3932168 | tf_op jit(solution)/shard_map/ppermute | solution.py:33
  160.0 24.5 %collective-permute-start.34 = (bf16[2,320,640]{2,1,0:T(8,128)(2,1)S(1)}, bf16[2,320,640]{2,1,0:T(8,128)(2,1)}, u32[]{:S(2)}, u32[]{:S(2)}) collective-permute-start(bf16[2,320,640]{2,1,0:T(8,128)(2,1)S(1)} %shard_map.175), channel_id=1, source_target_pairs={{0,4},{4,0},{8,12},{12,8},{16,20},{20,16},{24,28},{28,24},{1,5},{5... | collective-permute-start | bytes 2457608 | tf_op jit(solution)/shard_map/ppermute | solution.py:69
  162.9 17.4 %collective-permute-start.35 = (bf16[320,640]{1,0:T(8,128)(2,1)}, bf16[320,640]{1,0:T(8,128)(2,1)}, u32[]{:S(2)}, u32[]{:S(2)}) collective-permute-start(bf16[320,640]{1,0:T(8,128)(2,1)} %get-tuple-element.255), channel_id=1, source_target_pairs={{0,8},{4,12},{8,16},{12,20},{16,24},{20,28},{24,0},{28,4},{1,9},{5... | collective-permute-start | bytes 1228808 | tf_op jit(solution)/shard_map/ppermute | solution.py:63
  164.5 19.9 %collective-permute-start.36 = (bf16[320,640]{1,0:T(8,128)(2,1)}, bf16[320,640]{1,0:T(8,128)(2,1)}, u32[]{:S(2)}, u32[]{:S(2)}) collective-permute-start(bf16[320,640]{1,0:T(8,128)(2,1)} %get-tuple-element.254), channel_id=1, source_target_pairs={{0,24},{4,28},{8,0},{12,4},{16,8},{20,12},{24,16},{28,20},{1,25},{... | collective-permute-start | bytes 1228808 | tf_op jit(solution)/shard_map/ppermute | solution.py:63
  167.5 21.0 %copy-start.8 = (bf16[1024,640]{1,0:T(8,128)(2,1)S(1)}, bf16[1024,640]{1,0:T(8,128)(2,1)}, u32[]{:S(2)}) copy-start(bf16[1024,640]{1,0:T(8,128)(2,1)} %refs_0_.2) | copy-start | bytes 3932164
  168.6 33.8 %collective-permute-start.41 = (f32[24,640]{1,0:T(8,128)S(1)}, f32[24,640]{1,0:T(8,128)S(1)}, u32[]{:S(2)}, u32[]{:S(2)}) collective-permute-start(f32[24,640]{1,0:T(8,128)S(1)} %add_add_fusion), channel_id=1, source_target_pairs={{0,4},{4,0},{8,12},{12,8},{16,20},{20,16},{24,28},{28,24},{1,5},{5... | collective-permute-start | bytes 184328 | tf_op jit(solution)/shard_map/ppermute | solution.py:69
  180.3 11.1 %copy-start.31 = (f32[16,1024]{1,0:T(8,128)S(1)}, f32[16,1024]{1,0:T(8,128)}, u32[]{:S(2)}) copy-start(f32[16,1024]{1,0:T(8,128)} %get-tuple-element.219) | copy-start | bytes 196612
  184.4 22.0 %collective-permute-start.39 = (bf16[2,320,640]{2,1,0:T(8,128)(2,1)S(1)}, bf16[2,320,640]{2,1,0:T(8,128)(2,1)}, u32[]{:S(2)}, u32[]{:S(2)}) collective-permute-start(bf16[2,320,640]{2,1,0:T(8,128)(2,1)S(1)} %shard_map.176), channel_id=1, source_target_pairs={{0,4},{4,0},{8,12},{12,8},{16,20},{20,16},{24,28},{28,24},{1,5},{5... | collective-permute-start | bytes 2457608 | tf_op jit(solution)/shard_map/ppermute | solution.py:69
  187.8 18.7 %collective-permute-start.40 = (bf16[320,640]{1,0:T(8,128)(2,1)}, bf16[320,640]{1,0:T(8,128)(2,1)}, u32[]{:S(2)}, u32[]{:S(2)}) collective-permute-start(bf16[320,640]{1,0:T(8,128)(2,1)} %fusion.5), channel_id=1, source_target_pairs={{0,8},{4,12},{8,16},{12,20},{16,24},{20,28},{24,0},{28,4},{1,9},{5... | collective-permute-start | bytes 1228808 | tf_op jit(solution)/shard_map/ppermute | solution.py:63
  198.7 5.9 %collective-permute-start.42 = (f32[16,640]{1,0:T(8,128)S(1)}, f32[16,640]{1,0:T(8,128)S(1)}, u32[]{:S(2)}, u32[]{:S(2)}) collective-permute-start(f32[16,640]{1,0:T(8,128)S(1)} %fusion.27), channel_id=1, source_target_pairs={{0,8},{4,12},{8,16},{12,20},{16,24},{20,28},{24,0},{28,4},{1,9},{5... | collective-permute-start | bytes 122888 | tf_op jit(solution)/shard_map/ppermute | solution.py:63
  199.9 5.5 %collective-permute-start.43 = (f32[16,640]{1,0:T(8,128)S(1)}, f32[16,640]{1,0:T(8,128)}, u32[]{:S(2)}, u32[]{:S(2)}) collective-permute-start(f32[16,640]{1,0:T(8,128)S(1)} %fusion.27), channel_id=1, source_target_pairs={{0,16},{4,20},{8,24},{12,28},{16,0},{20,4},{24,8},{28,12},{1,17},{... | collective-permute-start | bytes 122888 | tf_op jit(solution)/shard_map/ppermute | solution.py:63
  202.4 4.1 %collective-permute-start.44 = (f32[16,640]{1,0:T(8,128)S(1)}, f32[16,640]{1,0:T(8,128)}, u32[]{:S(2)}, u32[]{:S(2)}) collective-permute-start(f32[16,640]{1,0:T(8,128)S(1)} %fusion.27), channel_id=1, source_target_pairs={{0,24},{4,28},{8,0},{12,4},{16,8},{20,12},{24,16},{28,20},{1,25},{... | collective-permute-start | bytes 122888 | tf_op jit(solution)/shard_map/ppermute | solution.py:63
  206.5 22.7 %copy-start.4 = (bf16[1,320,640]{2,1,0:T(8,128)(2,1)S(1)}, bf16[1,320,640]{2,1,0:T(8,128)(2,1)}, u32[]{:S(2)}) copy-start(bf16[1,320,640]{2,1,0:T(8,128)(2,1)} %copy-done.3) | copy-start | bytes 1228804
  206.5 22.7 %collective-permute-start.45 = (bf16[2,320,640]{2,1,0:T(8,128)(2,1)S(1)}, bf16[2,320,640]{2,1,0:T(8,128)(2,1)}, u32[]{:S(2)}, u32[]{:S(2)}) collective-permute-start(bf16[2,320,640]{2,1,0:T(8,128)(2,1)S(1)} %shard_map.177), channel_id=1, source_target_pairs={{0,4},{4,0},{8,12},{12,8},{16,20},{20,16},{24,28},{28,24},{1,5},{5... | collective-permute-start | bytes 2457608 | tf_op jit(solution)/shard_map/ppermute | solution.py:69
  209.5 19.0 %collective-permute-start.46 = (bf16[320,640]{1,0:T(8,128)(2,1)}, bf16[320,640]{1,0:T(8,128)(2,1)S(1)}, u32[]{:S(2)}, u32[]{:S(2)}) collective-permute-start(bf16[320,640]{1,0:T(8,128)(2,1)} %get-tuple-element.253), channel_id=1, source_target_pairs={{0,8},{4,12},{8,16},{12,20},{16,24},{20,28},{24,0},{28,4},{1,9},{5... | collective-permute-start | bytes 1228808 | tf_op jit(solution)/shard_map/ppermute | solution.py:63
  210.5 18.7 %collective-permute-start.47 = (bf16[320,640]{1,0:T(8,128)(2,1)}, bf16[320,640]{1,0:T(8,128)(2,1)S(1)}, u32[]{:S(2)}, u32[]{:S(2)}) collective-permute-start(bf16[320,640]{1,0:T(8,128)(2,1)} %get-tuple-element.252), channel_id=1, source_target_pairs={{0,24},{4,28},{8,0},{12,4},{16,8},{20,12},{24,16},{28,20},{1,25},{... | collective-permute-start | bytes 1228808 | tf_op jit(solution)/shard_map/ppermute | solution.py:63
  214.2 11.9 %collective-permute-start.48 = (f32[16,640]{1,0:T(8,128)S(1)}, f32[16,640]{1,0:T(8,128)S(1)}, u32[]{:S(2)}, u32[]{:S(2)}) collective-permute-start(f32[16,640]{1,0:T(8,128)S(1)} %add_add_fusion.1), channel_id=1, source_target_pairs={{0,4},{4,0},{8,12},{12,8},{16,20},{20,16},{24,28},{28,24},{1,5},{5... | collective-permute-start | bytes 122888 | tf_op jit(solution)/shard_map/ppermute | solution.py:69
  215.6 10.5 %collective-permute-start.50 = (f32[16,640]{1,0:T(8,128)S(1)}, f32[16,640]{1,0:T(8,128)S(1)}, u32[]{:S(2)}, u32[]{:S(2)}) collective-permute-start(f32[16,640]{1,0:T(8,128)S(1)} %slice.153), channel_id=1, source_target_pairs={{0,2},{1,3},{2,0},{3,1},{4,6},{5,7},{6,4},{7,5},{8,10},{9,11},{10,... | collective-permute-start | bytes 122888 | tf_op jit(solution)/shard_map/ppermute | solution.py:33
  226.0 2.4 collective-permute-start.49
  226.0 2.4 collective-permute-start.51
  230.4 12.8 %collective-permute-start.52 = (bf16[320,640]{1,0:T(8,128)(2,1)S(1)}, bf16[320,640]{1,0:T(8,128)(2,1)S(1)}, u32[]{:S(2)}, u32[]{:S(2)}) collective-permute-start(bf16[320,640]{1,0:T(8,128)(2,1)S(1)} %fusion.4), channel_id=1, source_target_pairs={{0,8},{4,12},{8,16},{12,20},{16,24},{20,28},{24,0},{28,4},{1,9},{5... | collective-permute-start | bytes 1228808 | tf_op jit(solution)/shard_map/ppermute | solution.py:63
  (26 other events, 81.7 us)

commit v3 on v2

--- a/solution.py
+++ b/solution.py
@@ -679,8 +679,8 @@
         part, part_edge, params, m_loc, feats, edges, last, idx, group_at[3:], n_use
     )
     sums = [sums] + [flip(sums, "chan", j) for j in range(1, chan_count)]
-    out_far = jnp.stack([after(out_far[0], sums[0]), out_far[1]])
-    out_far_fast = to_fast(out_far)
+    out_far = [after(out_far[0], sums[0])[None], after(out_far[1], *sums[1:])[None]]
+    out_far_fast = to_fast(out_far[0]) + to_fast(out_far[1])
     loss_weight = 4.0 / math.sqrt(tok_rows * seq_count)
     normed_x = xor_gather(after(normed, *sums[1:]), "chan", 2)
     dgate, dconv, dfirst, dlogit, mid, squares = back(
@@ -734,11 +734,14 @@
     normed_all = []
     for block in normed_x:
         normed_all += [block, flip(block, "chan", 1)]
-    out_shards = [out_pair] + out_pair_fast + [out_far] + out_far_fast
-    counts = [[k * fast + j for k in ks] for ks in ((0, 1), (2, 3)) for j in range(fast)]
+    out_shards = [out_pair] + out_pair_fast
+    counts = [[k * fast + j for k in (0, 1)] for j in range(fast)]
+    for k in (2, 3):
+        out_shards += [out_far[k - 2]] + out_far_fast[(k - 2) * (fast - 1) : (k - 1) * (fast - 1)]
+        counts += [[k * fast + j] for j in range(fast)]
     raw = proj(normed_all, out_shards, counts, idx)
-    gate_second, gate_slow, x_first, x_second, held = sync(
-        came, gate_slow, x_first, x_second, [raw, dx_pre]
+    gate_second, gate_slow[:1], x_first, x_second, held = sync(
+        came, gate_slow[:1], x_first, x_second, [raw, dx_pre]
     )
     raw, dx_pre = held
 
@@ -774,7 +777,8 @@
     grad_gate_in = total_of(gate_own[3], gate_second, 1) + sum(
         block.astype(f32) for block in gate_slow
     )
-    grad_x_in = total_of(x_own[3], x_second, 1) + sum(block.astype(f32) for block in x_slow)
+    rest = total_of(x_own[3], x_second, 1) + x_slow[1].astype(f32)
+    grad_x_in = lax.optimization_barrier(rest) + x_slow[0].astype(f32)
     grad_head = head_local.T
     seq = lax.axis_index("seq")
     g_chan = picked(g_pieces, [chan ^ j for j in range(chan_count)], seq // per_chan)

time: 246 us -> 238 us (0.967)
  waiting for transfers between devices: 58.6 us -> 49.8 us
    ppermute x21, waiting for transfers between devices: 25.7 us -> 17.4 us  [move_slow(): return lax.ppermute(value, 'seq', pairs)]
    ppermute x13 -> x14, waiting for transfers between devices: 9.22 us -> 8.34 us  [move_fast(): return lax.ppermute(value, 'seq', pairs)]
    ppermute x13 -> x14, starting transfers between devices: 16.3 us -> 16.3 us  [move_fast(): return lax.ppermute(value, 'seq', pairs)]
    unnamed x75 -> x91, local copies, waits for them, and re-layouts: 8.8 us -> 8.81 us
  transfers between devices with their start and end apart: 53 -> 54, of which waited for: 19 -> 18; matrix products, arithmetic and copies ran while one was open for 12% -> 13% of each run, Pallas kernels for 31% -> 32%
where the time goes in v3:
time: 238 us; the launch traced here: 237 us
  Pallas kernels  76.4 us (32%)
  starting transfers between devices  66.4 us (28%)
  waiting for transfers between devices  49.8 us (21%)
  other arithmetic  20.3 us (9%)
  local copies, waits for them, and re-layouts  17.4 us (7%)
  matrix products  4.84 us (2%)
    ppermute x21, starting transfers between devices, move_slow(): return lax.ppermute(value, 'seq', pairs)  34.6 us
    ppermute x17, waiting for transfers between devices, flip(): lax.ppermute(value, axis, [(i, i ^ bit) for i in range(lax.axis_size(axis...  20.1 us
    pallas_call x2, Pallas kernels, partial_products(): pl.pallas_call(functools.partial(part_kernel, len(feats), n_fast, n_use,...  19.3 us
    ppermute x21, waiting for transfers between devices, move_slow(): return lax.ppermute(value, 'seq', pairs)  17.4 us
    pallas_call x6, Pallas kernels, block_grads(): pl.pallas_call(functools.partial(blocks_kernel, sizes), out_shape=[jax.Sh...  17.3 us
    ppermute x14, starting transfers between devices, move_fast(): return lax.ppermute(value, 'seq', pairs)  16.3 us
    pallas_call x1, Pallas kernels, front(): pl.pallas_call(functools.partial(front_kernel, len(feats), n_fast, n_use,...  11.7 us
    pallas_call x1, Pallas kernels, back(): pl.pallas_call(functools.partial(back_kernel, weight, len(sums)), out_sha...  11.2 us
  transfers between devices with their start and end apart: 54, of which 18 were waited for; matrix products, arithmetic and copies ran while one was open for 13% of the time, Pallas kernels for 32%

profile of v3, /device:TPU:0, one launch (start us, length us, event | category | flops | bytes accessed | tf_op | source)
XLA Modules:
  0.0 236.7 jit_solution(7086274701146729620)
XLA Ops:
  0.7 1.3 pad_maximum_fusion.refs_8_
  2.0 3.1 %collective-permute-start = (bf16[2,320,640]{2,1,0:T(8,128)(2,1)S(1)}, bf16[2,320,640]{2,1,0:T(8,128)(2,1)}, u32[]{:S(2)}, u32[]{:S(2)}) collective-permute-start(bf16[2,320,640]{2,1,0:T(8,128)(2,1)S(1)} %pad_maximum_fusion.refs_8_), channel_id=1, source_target_pairs={{0,8},{4,12},{8,16},{12,20},{16,24},{20,28},{24,0},{28,4},{1,9},{5... | collective-permute-start | bytes 2457608 | tf_op jit(solution)/shard_map/ppermute | solution.py:63
  5.1 1.5 collective-permute-start.1
  6.6 1.8 fusion.26
  9.4 1.5 collective-permute-start.8
  11.5 3.0 %collective-permute-start.2 = (bf16[16,640]{1,0:T(8,128)(2,1)}, bf16[16,640]{1,0:T(8,128)(2,1)}, u32[]{:S(2)}, u32[]{:S(2)}) collective-permute-start(bf16[16,640]{1,0:T(8,128)(2,1)} %slice.107), channel_id=1, source_target_pairs={{0,4},{4,8},{8,12},{12,16},{16,20},{20,24},{24,28},{1,5},{5,9},{9,... | collective-permute-start | bytes 61448 | tf_op jit(solution)/shard_map/ppermute | solution.py:74
  15.3 1.3 broadcast_in_dim.46
  16.6 1.3 broadcast_in_dim_reshape.3
  18.6 1.3 concatenate.20.params
  21.6 2.7 %collective-permute-done.2.refs_4_.refs_6_ = bf16[16,640]{1,0:T(8,128)(2,1)} collective-permute-done((bf16[16,640]{1,0:T(8,128)(2,1)}, bf16[16,640]{1,0:T(8,128)(2,1)}, u32[]{:S(2)}, u32[]{:S(2)}) %collective-permute-start.2) | collective-permute-done | bytes 20512 | tf_op jit(solution)/shard_map/ppermute | solution.py:74
  25.5 1.4 collective-permute-start.4
  26.9 1.5 collective-permute-start.5
  28.5 1.5 collective-permute-start.6
  30.0 12.5 %collective-permute-done.6 = f32[16,1344]{1,0:T(8,128)S(1)} collective-permute-done((f32[16,1344]{1,0:T(8,128)S(1)}, f32[16,1344]{1,0:T(8,128)S(1)}, u32[]{:S(2)}, u32[]{:S(2)}) %collective-permute-start.6) | collective-permute-done | bytes 86048 | tf_op jit(solution)/shard_map/ppermute | solution.py:33
  43.1 1.5 collective-permute-start.9
  47.7 1.6 collective-permute-start.10
  49.3 1.5 collective-permute-start.11
  50.8 1.5 collective-permute-done.14.refs_5_.refs_7_
  55.7 9.7 %shard_map.169 = (f32[2,1024,640]{2,1,0:T(8,128)}, f32[16,640]{1,0:T(8,128)}) custom-call(s32[40]{0:T(128)} %concatenate.18.idx, bf16[1024,640]{1,0:T(8,128)(2,1)} %refs_0_.2, bf16[1024,640]{1,0:T(8,128)(2,1)} %copy-done.9, bf16[1024,640]{1,0:T(8,128)(2,1)} %copy-done.8, bf16[1024,640]{1,0:T(8,128)(2,1)} %copy-done.10, ...), custom_call_target="tpu_custom_call" | custom-call | flops 1 | bytes 1 | tf_op jit(solution)/shard_map/pallas_call | solution.py:343
  65.4 4.6 %collective-permute-done.10.refs_8_ = bf16[2,320,640]{2,1,0:T(8,128)(2,1)} collective-permute-done((bf16[2,320,640]{2,1,0:T(8,128)(2,1)}, bf16[2,320,640]{2,1,0:T(8,128)(2,1)}, u32[]{:S(2)}, u32[]{:S(2)}) %collective-permute-start.10) | collective-permute-done | bytes 819232 | tf_op jit(solution)/shard_map/ppermute | solution.py:63
  70.1 1.5 collective-permute-start.16
  71.6 1.7 collective-permute-start.20
  74.4 2.4 %collective-permute-start.17 = (bf16[320,640]{1,0:T(8,128)(2,1)}, bf16[320,640]{1,0:T(8,128)(2,1)S(1)}, u32[]{:S(2)}, u32[]{:S(2)}) collective-permute-start(bf16[320,640]{1,0:T(8,128)(2,1)} %param.18), channel_id=1, source_target_pairs={{0,8},{4,12},{8,16},{12,20},{16,24},{20,28},{24,0},{28,4},{1,9},{5... | collective-permute-start | bytes 1228808 | tf_op jit(solution)/shard_map/ppermute | solution.py:63
  76.8 9.6 %shard_map.170 = (f32[2,1024,640]{2,1,0:T(8,128)}, f32[16,640]{1,0:T(8,128)}) custom-call(s32[40]{0:T(128)} %concatenate.18.idx, f32[2,1024,640]{2,1,0:T(8,128)} %get-tuple-element.148.refs_0_, f32[16,640]{1,0:T(8,128)} %get-tuple-element.149.refs_1_, bf16[1024,640]{1,0:T(8,128)(2,1)} %refs_0_.2, bf16[1024,640]{1,0:T(8,128)(2,1)} %copy-done.9, ...), custom_call_target="tpu_custom_call" | custom-call | flops 1 | bytes 1 | tf_op jit(solution)/shard_map/pallas_call | solution.py:343
  86.4 5.9 %shard_map.171.lhs = bf16[4,640,1024]{2,1,0:T(8,128)(2,1)} custom-call(bf16[1024,640]{1,0:T(8,128)(2,1)} %refs_0_.2, bf16[1024,640]{1,0:T(8,128)(2,1)} %copy-done.9, bf16[1024,640]{1,0:T(8,128)(2,1)} %copy-done.8, bf16[1024,640]{1,0:T(8,128)(2,1)} %copy-done.10), custom_call_target="tpu_custom_call" | custom-call | flops 1 | bytes 1 | tf_op jit(solution)/shard_map/pallas_call | solution.py:115
  92.4 1.5 collective-permute-start.28
  96.1 11.7 %shard_map.172 = (bf16[1024,640]{1,0:T(8,128)(2,1)}, bf16[1024,640]{1,0:T(8,128)(2,1)}, bf16[1024,640]{1,0:T(8,128)(2,1)}, bf16[16,640]{1,0:T(8,128)(2,1)}, f32[24,1024]{1,0:T(8,128)}) custom-call(s32[40]{0:T(128)} %concatenate.18.idx, f32[2,1024,640]{2,1,0:T(8,128)} %get-tuple-element.161.part, f32[16,640]{1,0:T(8,128)} %get-tuple-element.162.part_edge, ...), custom_call_target="tpu_custom_call" | custom-call | flops 1 | bytes 1 | tf_op jit(solution)/shard_map/pallas_call | solution.py:368
  107.9 1.6 collective-permute-start.22
  110.6 3.1 %collective-permute-done.22.refs_2_ = f32[24,1024]{1,0:T(8,128)S(1)} collective-permute-done((f32[24,1024]{1,0:T(8,128)}, f32[24,1024]{1,0:T(8,128)S(1)}, u32[]{:S(2)}, u32[]{:S(2)}) %collective-permute-start.22) | collective-permute-done | bytes 98336 | tf_op jit(solution)/shard_map/ppermute | solution.py:33
  115.0 1.5 collective-permute-start.31
  116.4 1.5 collective-permute-start.29
  118.5 11.2 %shard_map.173 = (bf16[1024,640]{1,0:T(8,128)(2,1)}, f32[1024,640]{1,0:T(8,128)}, f32[8,640]{1,0:T(8,128)}, f32[16,1024]{1,0:T(8,128)}, f32[24,640]{1,0:T(8,128)}, /*index=5*/f32[8,1024]{1,0:T(8,128)}) custom-call(bf16[1024,640]{1,0:T(8,128)(2,1)} %get-tuple-element.167.gate_in, bf16[1024,640]{1,0:T(8,128)(2,1)} %get-tuple-element.168.x_in, ...), custom_call_target="tpu_custom_call" | custom-call | flops 1 | bytes 1 | tf_op jit(solution)/shard_map/pallas_call | solution.py:493
  129.7 1.5 collective-permute-start.24
  131.2 4.6 %shard_map.174 = bf16[2,320,640]{2,1,0:T(8,128)(2,1)} custom-call(s32[40]{0:T(128)} %concatenate.18.idx, bf16[4,640,1024]{2,1,0:T(8,128)(2,1)} %shard_map.171.lhs, bf16[1024,640]{1,0:T(8,128)(2,1)} %get-tuple-element.182.rhs), custom_call_target="tpu_custom_call" | custom-call | flops 1 | bytes 1 | tf_op jit(solution)/shard_map/pallas_call | solution.py:540
  137.1 1.5 collective-permute-start.30
  141.2 2.0 shard_map.176
  143.2 3.4 %shard_map.178 = (bf16[1,320,640]{2,1,0:T(8,128)(2,1)S(1)}, bf16[1,320,640]{2,1,0:T(8,128)(2,1)S(1)}, bf16[1,320,640]{2,1,0:T(8,128)(2,1)S(1)}, bf16[1,320,640]{2,1,0:T(8,128)(2,1)S(1)}) custom-call(s32[40]{0:T(128)S(1)} %copy-done.4, bf16[4,640,1024]{2,1,0:T(8,128)(2,1)S(1)} %bitcast.78, bf16[1024,640]{1,0:T(8,128)(2,1)S(1)} %copy-done.2), custom_call_target="tpu_custom_call" | custom-call | flops 1 | bytes 1 | tf_op jit(solution)/shard_map/pallas_call | solution.py:540
  146.6 1.6 collective-permute-start.32
  148.2 2.2 collective-permute-start.33
  151.2 2.0 shard_map.175
  153.2 2.0 shard_map.177
  155.3 1.5 collective-permute-done.30
  157.3 1.4 collective-permute-start.35
  159.8 1.2 collective-permute-start.36
  161.8 2.6 %collective-permute-start.41 = (bf16[320,640]{1,0:T(8,128)(2,1)}, bf16[320,640]{1,0:T(8,128)(2,1)}, u32[]{:S(2)}, u32[]{:S(2)}) collective-permute-start(bf16[320,640]{1,0:T(8,128)(2,1)} %get-tuple-element.258), channel_id=1, source_target_pairs={{0,24},{4,28},{8,0},{12,4},{16,8},{20,12},{24,16},{28,20},{1,25},{... | collective-permute-start | bytes 1228808 | tf_op jit(solution)/shard_map/ppermute | solution.py:63
  166.2 11.0 %shard_map.179 = bf16[1024,640]{1,0:T(8,128)(2,1)} custom-call(s32[40]{0:T(128)} %concatenate.18.idx, bf16[1024,640]{1,0:T(8,128)(2,1)} %get-tuple-element.198.refs_0_, bf16[1024,640]{1,0:T(8,128)(2,1)} %copy-done.18, bf16[1024,640]{1,0:T(8,128)(2,1)} %collective-permute-done.31.refs_2_, bf16[1024,640]{1,0:T(8,128)(2,1)} %collective-permute-done.38.refs_3_, ...), custom_call_target="tpu_custom_call" | custom-call | flops 1 | bytes 1 | tf_op jit(solution)/shard_map/pallas_call | solution.py:173
  178.2 1.4 collective-permute-start.39
  179.6 2.1 fusion.5
  181.6 1.2 collective-permute-start.40
  182.9 1.8 add_convert_fusion
  186.4 2.5 %copy-done.1 = bf16[4,640,1024]{2,1,0:T(8,128)(2,1)S(1)} copy-done((bf16[4,640,1024]{2,1,0:T(8,128)(2,1)S(1)}, bf16[4,640,1024]{2,1,0:T(8,128)(2,1)}, u32[]{:S(2)}) %copy-start.1) | copy-done | bytes 5242904
  188.9 3.4 %shard_map.180 = (bf16[1,320,640]{2,1,0:T(8,128)(2,1)S(1)}, bf16[1,320,640]{2,1,0:T(8,128)(2,1)S(1)}, bf16[1,320,640]{2,1,0:T(8,128)(2,1)S(1)}, bf16[1,320,640]{2,1,0:T(8,128)(2,1)S(1)}) custom-call(s32[40]{0:T(128)S(1)} %copy-done.5, bf16[4,640,1024]{2,1,0:T(8,128)(2,1)S(1)} %copy-done.1, bf16[1024,640]{1,0:T(8,128)(2,1)S(1)} %fusion.2.rhs), custom_call_target="tpu_custom_call" | custom-call | flops 1 | bytes 1 | tf_op jit(solution)/shard_map/pallas_call | solution.py:540
  194.0 2.1 collective-permute-start.44
  196.2 2.7 %collective-permute-start.45 = (f32[16,640]{1,0:T(8,128)S(1)}, f32[16,640]{1,0:T(8,128)S(1)}, u32[]{:S(2)}, u32[]{:S(2)}) collective-permute-start(f32[16,640]{1,0:T(8,128)S(1)} %fusion.27), channel_id=1, source_target_pairs={{0,24},{4,28},{8,0},{12,4},{16,8},{20,12},{24,16},{28,20},{1,25},{... | collective-permute-start | bytes 122888 | tf_op jit(solution)/shard_map/ppermute | solution.py:63
  199.2 1.3 collective-permute-done.45
  200.6 2.1 collective-permute-start.46
  202.7 2.4 %fusion.9 = (bf16[320,640]{1,0:T(8,128)(2,1)}, bf16[320,640]{1,0:T(8,128)(2,1)}) fusion(bf16[1,320,640]{2,1,0:T(8,128)(2,1)} %copy-done.3, bf16[2,320,640]{2,1,0:T(8,128)(2,1)} %collective-permute-done.39, bf16[1,320,640]{2,1,0:T(8,128)(2,1)S(1)} %get-tuple-element.227), kind=kLoop, calls=%fused_computation.24 | loop fusion | flops 1638400 | bytes 2457600 | tf_op jit(solution)/shard_map/convert_element_type | solution.py:768
  206.0 3.2 %collective-permute-start.48 = (bf16[320,640]{1,0:T(8,128)(2,1)}, bf16[320,640]{1,0:T(8,128)(2,1)}, u32[]{:S(2)}, u32[]{:S(2)}) collective-permute-start(bf16[320,640]{1,0:T(8,128)(2,1)} %get-tuple-element.256), channel_id=1, source_target_pairs={{0,24},{4,28},{8,0},{12,4},{16,8},{20,12},{24,16},{28,20},{1,25},{... | collective-permute-start | bytes 1228808 | tf_op jit(solution)/shard_map/ppermute | solution.py:63
  210.8 2.4 %bitcast_add_fusion.3 = f32[320,640]{1,0:T(8,128)} fusion(bf16[320,640]{1,0:T(8,128)(2,1)} %collective-permute-done.41, bf16[320,640]{1,0:T(8,128)(2,1)} %collective-permute-done.40, bf16[1,320,640]{2,1,0:T(8,128)(2,1)S(1)} %get-tuple-element.205, bf16[2,320,640]{2,1,0:T(8,128)(2,1)} %collective-permute-done.35), kind=kLoop, calls=%fused_computation.15 | loop fusion | flops 1433600 | bytes 2457600 | tf_op jit(solution)/shard_map/add | solution.py:777
  213.2 4.7 %collective-permute-done.49 = f32[16,640]{1,0:T(8,128)S(1)} collective-permute-done((f32[16,640]{1,0:T(8,128)S(1)}, f32[16,640]{1,0:T(8,128)S(1)}, u32[]{:S(2)}, u32[]{:S(2)}) %collective-permute-start.49) | collective-permute-done | bytes 40992 | tf_op jit(solution)/shard_map/ppermute | solution.py:69
  220.4 1.7 collective-permute-done.48
  222.1 1.4 fusion.4
  225.2 2.3 fusion.11
  227.5 8.2 %collective-permute-done.53 = bf16[320,640]{1,0:T(8,128)(2,1)S(1)} collective-permute-done((bf16[320,640]{1,0:T(8,128)(2,1)S(1)}, bf16[320,640]{1,0:T(8,128)(2,1)S(1)}, u32[]{:S(2)}, u32[]{:S(2)}) %collective-permute-start.53) | collective-permute-done | bytes 409632 | tf_op jit(solution)/shard_map/ppermute | solution.py:63
  (192 shorter events, 40.3 us)
Async XLA Ops:
  0.7 8.7 %copy-start.6 = (bf16[1024,640]{1,0:T(8,128)(2,1)S(1)}, bf16[1024,640]{1,0:T(8,128)(2,1)}, u32[]{:S(2)}) copy-start(bf16[1024,640]{1,0:T(8,128)(2,1)} %refs_0_.2) | copy-start | bytes 3932164
  0.7 14.0 %copy-start.42 = (f32[640]{0:T(1024)S(1)}, f32[640]{0:T(1024)}, u32[]{:S(2)}) copy-start(f32[640]{0:T(1024)} %param.15) | copy-start | bytes 7684
  2.0 51.5 %copy-start.14 = (bf16[2,320,640]{2,1,0:T(8,128)(2,1)}, bf16[2,320,640]{2,1,0:T(8,128)(2,1)S(1)}, u32[]{:S(2)}) copy-start(bf16[2,320,640]{2,1,0:T(8,128)(2,1)S(1)} %pad_maximum_fusion.refs_8_) | copy-start | bytes 2457604
  2.0 23.5 %collective-permute-start = (bf16[2,320,640]{2,1,0:T(8,128)(2,1)S(1)}, bf16[2,320,640]{2,1,0:T(8,128)(2,1)}, u32[]{:S(2)}, u32[]{:S(2)}) collective-permute-start(bf16[2,320,640]{2,1,0:T(8,128)(2,1)S(1)} %pad_maximum_fusion.refs_8_), channel_id=1, source_target_pairs={{0,8},{4,12},{8,16},{12,20},{16,24},{20,28},{24,0},{28,4},{1,9},{5... | collective-permute-start | bytes 2457608 | tf_op jit(solution)/shard_map/ppermute | solution.py:63
  5.1 20.4 %collective-permute-start.1 = (bf16[2,320,640]{2,1,0:T(8,128)(2,1)S(1)}, bf16[2,320,640]{2,1,0:T(8,128)(2,1)}, u32[]{:S(2)}, u32[]{:S(2)}) collective-permute-start(bf16[2,320,640]{2,1,0:T(8,128)(2,1)S(1)} %pad_maximum_fusion.refs_8_), channel_id=1, source_target_pairs={{0,4},{4,0},{8,12},{12,8},{16,20},{20,16},{24,28},{28,24},{1,5},{5... | collective-permute-start | bytes 2457608 | tf_op jit(solution)/shard_map/ppermute | solution.py:69
  9.4 11.2 %collective-permute-start.3 = (f32[16,1344]{1,0:T(8,128)}, f32[16,1344]{1,0:T(8,128)}, u32[]{:S(2)}, u32[]{:S(2)}) collective-permute-start(f32[16,1344]{1,0:T(8,128)} %pad_maximum_fusion.2), channel_id=1, source_target_pairs={{0,1},{1,0},{2,3},{3,2},{4,5},{5,4},{6,7},{7,6},{8,9},{9,8},{10,11... | collective-permute-start | bytes 258056 | tf_op jit(solution)/shard_map/ppermute | solution.py:33
  9.4 37.7 %collective-permute-start.8 = (bf16[1024,640]{1,0:T(8,128)(2,1)S(1)}, bf16[1024,640]{1,0:T(8,128)(2,1)S(1)}, u32[]{:S(2)}, u32[]{:S(2)}) collective-permute-start(bf16[1024,640]{1,0:T(8,128)(2,1)S(1)} %copy-done.6), channel_id=1, source_target_pairs={{0,2},{1,3},{2,0},{3,1},{4,6},{5,7},{6,4},{7,5},{8,10},{9,11},{10,... | collective-permute-start | bytes 3932168 | tf_op jit(solution)/shard_map/ppermute | solution.py:33
  11.5 12.8 %collective-permute-start.2 = (bf16[16,640]{1,0:T(8,128)(2,1)}, bf16[16,640]{1,0:T(8,128)(2,1)}, u32[]{:S(2)}, u32[]{:S(2)}) collective-permute-start(bf16[16,640]{1,0:T(8,128)(2,1)} %slice.107), channel_id=1, source_target_pairs={{0,4},{4,8},{8,12},{12,16},{16,20},{20,24},{24,28},{1,5},{5,9},{9,... | collective-permute-start | bytes 61448 | tf_op jit(solution)/shard_map/ppermute | solution.py:74
  25.5 21.6 %collective-permute-start.4 = (bf16[2,320,640]{2,1,0:T(8,128)(2,1)}, bf16[2,320,640]{2,1,0:T(8,128)(2,1)}, u32[]{:S(2)}, u32[]{:S(2)}) collective-permute-start(bf16[2,320,640]{2,1,0:T(8,128)(2,1)} %collective-permute-done.refs_10_), channel_id=1, source_target_pairs={{0,8},{4,12},{8,16},{12,20},{16,24},{20,28},{24,0},{28,4},{1,9},{5... | collective-permute-start | bytes 2457608 | tf_op jit(solution)/shard_map/ppermute | solution.py:63
  26.9 20.2 %collective-permute-start.5 = (bf16[2,320,640]{2,1,0:T(8,128)(2,1)}, bf16[2,320,640]{2,1,0:T(8,128)(2,1)S(1)}, u32[]{:S(2)}, u32[]{:S(2)}) collective-permute-start(bf16[2,320,640]{2,1,0:T(8,128)(2,1)} %collective-permute-done.refs_10_), channel_id=1, source_target_pairs={{0,4},{4,0},{8,12},{12,8},{16,20},{20,16},{24,28},{28,24},{1,5},{5... | collective-permute-start | bytes 2457608 | tf_op jit(solution)/shard_map/ppermute | solution.py:69
  28.5 14.0 %collective-permute-start.6 = (f32[16,1344]{1,0:T(8,128)S(1)}, f32[16,1344]{1,0:T(8,128)S(1)}, u32[]{:S(2)}, u32[]{:S(2)}) collective-permute-start(f32[16,1344]{1,0:T(8,128)S(1)} %fusion.24), channel_id=1, source_target_pairs={{0,2},{1,3},{2,0},{3,1},{4,6},{5,7},{6,4},{7,5},{8,10},{9,11},{10,... | collective-permute-start | bytes 258056 | tf_op jit(solution)/shard_map/ppermute | solution.py:33
  42.5 3.9 %collective-permute-start.7 = (f32[16,320]{1,0:T(8,128)S(1)}, f32[16,320]{1,0:T(8,128)S(1)}, u32[]{:S(2)}, u32[]{:S(2)}) collective-permute-start(f32[16,320]{1,0:T(8,128)S(1)} %slice.141), channel_id=1, source_target_pairs={{0,4},{4,0},{8,12},{12,8},{16,20},{20,16},{24,28},{28,24},{1,5},{5... | collective-permute-start | bytes 61448 | tf_op jit(solution)/shard_map/ppermute | solution.py:69
  43.1 4.0 %collective-permute-start.9 = (bf16[16,640]{1,0:T(8,128)(2,1)}, bf16[16,640]{1,0:T(8,128)(2,1)S(1)}, u32[]{:S(2)}, u32[]{:S(2)}) collective-permute-start(bf16[16,640]{1,0:T(8,128)(2,1)} %collective-permute-done.2.refs_4_.refs_6_), channel_id=1, source_target_pairs={{0,2},{1,3},{2,0},{3,1},{4,6},{5,7},{6,4},{7,5},{8,10},{9,11},{10,... | collective-permute-start | bytes 61448 | tf_op jit(solution)/shard_map/ppermute | solution.py:33
  47.1 6.4 %collective-permute-start.12 = (bf16[1024,640]{1,0:T(8,128)(2,1)S(1)}, bf16[1024,640]{1,0:T(8,128)(2,1)S(1)}, u32[]{:S(2)}, u32[]{:S(2)}) collective-permute-start(bf16[1024,640]{1,0:T(8,128)(2,1)S(1)} %copy-done.6), channel_id=1, source_target_pairs={{0,1},{1,0},{2,3},{3,2},{4,5},{5,4},{6,7},{7,6},{8,9},{9,8},{10,11... | collective-permute-start | bytes 3932168 | tf_op jit(solution)/shard_map/ppermute | solution.py:33
  47.2 6.4 %collective-permute-start.13 = (bf16[1024,640]{1,0:T(8,128)(2,1)S(1)}, bf16[1024,640]{1,0:T(8,128)(2,1)S(1)}, u32[]{:S(2)}, u32[]{:S(2)}) collective-permute-start(bf16[1024,640]{1,0:T(8,128)(2,1)S(1)} %collective-permute-done.8.refs_2_.refs_4_), channel_id=1, source_target_pairs={{0,1},{1,0},{2,3},{3,2},{4,5},{5,4},{6,7},{7,6},{8,9},{9,8},{10,11... | collective-permute-start | bytes 3932168 | tf_op jit(solution)/shard_map/ppermute | solution.py:33
  47.7 22.3 %collective-permute-start.10 = (bf16[2,320,640]{2,1,0:T(8,128)(2,1)}, bf16[2,320,640]{2,1,0:T(8,128)(2,1)}, u32[]{:S(2)}, u32[]{:S(2)}) collective-permute-start(bf16[2,320,640]{2,1,0:T(8,128)(2,1)} %collective-permute-done.4.refs_10_), channel_id=1, source_target_pairs={{0,8},{4,12},{8,16},{12,20},{16,24},{20,28},{24,0},{28,4},{1,9},{5... | collective-permute-start | bytes 2457608 | tf_op jit(solution)/shard_map/ppermute | solution.py:63
  49.3 20.8 %collective-permute-start.11 = (bf16[2,320,640]{2,1,0:T(8,128)(2,1)}, bf16[2,320,640]{2,1,0:T(8,128)(2,1)}, u32[]{:S(2)}, u32[]{:S(2)}) collective-permute-start(bf16[2,320,640]{2,1,0:T(8,128)(2,1)} %collective-permute-done.4.refs_10_), channel_id=1, source_target_pairs={{0,4},{4,0},{8,12},{12,8},{16,20},{20,16},{24,28},{28,24},{1,5},{5... | collective-permute-start | bytes 2457608 | tf_op jit(solution)/shard_map/ppermute | solution.py:69
  50.8 1.5 collective-permute-start.14
  52.4 1.2 collective-permute-start.15
  70.1 24.8 %collective-permute-start.16 = (bf16[2,320,640]{2,1,0:T(8,128)(2,1)}, bf16[2,320,640]{2,1,0:T(8,128)(2,1)S(1)}, u32[]{:S(2)}, u32[]{:S(2)}) collective-permute-start(bf16[2,320,640]{2,1,0:T(8,128)(2,1)} %collective-permute-done.10.refs_8_), channel_id=1, source_target_pairs={{0,4},{4,0},{8,12},{12,8},{16,20},{20,16},{24,28},{28,24},{1,5},{5... | collective-permute-start | bytes 2457608 | tf_op jit(solution)/shard_map/ppermute | solution.py:69
  71.6 20.8 %collective-permute-start.20 = (f32[16,640]{1,0:T(8,128)S(1)}, f32[16,640]{1,0:T(8,128)S(1)}, u32[]{:S(2)}, u32[]{:S(2)}) collective-permute-start(f32[16,640]{1,0:T(8,128)S(1)} %pad_maximum_fusion.3), channel_id=1, source_target_pairs={{0,24},{4,28},{8,0},{12,4},{16,8},{20,12},{24,16},{28,20},{1,25},{... | collective-permute-start | bytes 122888 | tf_op jit(solution)/shard_map/ppermute | solution.py:63
  73.3 20.5 %collective-permute-start.19 = (f32[16,640]{1,0:T(8,128)S(1)}, f32[16,640]{1,0:T(8,128)S(1)}, u32[]{:S(2)}, u32[]{:S(2)}) collective-permute-start(f32[16,640]{1,0:T(8,128)S(1)} %pad_maximum_fusion.3), channel_id=1, source_target_pairs={{0,16},{4,20},{8,24},{12,28},{16,0},{20,4},{24,8},{28,12},{1,17},{... | collective-permute-start | bytes 122888 | tf_op jit(solution)/shard_map/ppermute | solution.py:63
  74.1 19.7 %collective-permute-start.18 = (f32[16,640]{1,0:T(8,128)S(1)}, f32[16,640]{1,0:T(8,128)S(1)}, u32[]{:S(2)}, u32[]{:S(2)}) collective-permute-start(f32[16,640]{1,0:T(8,128)S(1)} %pad_maximum_fusion.3), channel_id=1, source_target_pairs={{0,8},{4,12},{8,16},{12,20},{16,24},{20,28},{24,0},{28,4},{1,9},{5... | collective-permute-start | bytes 122888 | tf_op jit(solution)/shard_map/ppermute | solution.py:63
  74.4 20.3 %collective-permute-start.17 = (bf16[320,640]{1,0:T(8,128)(2,1)}, bf16[320,640]{1,0:T(8,128)(2,1)S(1)}, u32[]{:S(2)}, u32[]{:S(2)}) collective-permute-start(bf16[320,640]{1,0:T(8,128)(2,1)} %param.18), channel_id=1, source_target_pairs={{0,8},{4,12},{8,16},{12,20},{16,24},{20,28},{24,0},{28,4},{1,9},{5... | collective-permute-start | bytes 1228808 | tf_op jit(solution)/shard_map/ppermute | solution.py:63
  92.4 24.1 %collective-permute-start.28 = (bf16[320,640]{1,0:T(8,128)(2,1)S(1)}, bf16[320,640]{1,0:T(8,128)(2,1)S(1)}, u32[]{:S(2)}, u32[]{:S(2)}) collective-permute-start(bf16[320,640]{1,0:T(8,128)(2,1)S(1)} %copy-done.16), channel_id=1, source_target_pairs={{0,24},{4,28},{8,0},{12,4},{16,8},{20,12},{24,16},{28,20},{1,25},{... | collective-permute-start | bytes 1228808 | tf_op jit(solution)/shard_map/ppermute | solution.py:63
  94.8 12.9 %copy-start.13 = (bf16[2,320,640]{2,1,0:T(8,128)(2,1)}, bf16[2,320,640]{2,1,0:T(8,128)(2,1)S(1)}, u32[]{:S(2)}) copy-start(bf16[2,320,640]{2,1,0:T(8,128)(2,1)S(1)} %pad_maximum_fusion.1.refs_4_) | copy-start | bytes 2457604
  94.9 23.1 %collective-permute-start.26 = (bf16[320,640]{1,0:T(8,128)(2,1)S(1)}, bf16[320,640]{1,0:T(8,128)(2,1)S(1)}, u32[]{:S(2)}, u32[]{:S(2)}) collective-permute-start(bf16[320,640]{1,0:T(8,128)(2,1)S(1)} %slice_bitcast_fusion), channel_id=1, source_target_pairs={{0,8},{4,12},{8,16},{12,20},{16,24},{20,28},{24,0},{28,4},{1,9},{5... | collective-permute-start | bytes 1228808 | tf_op jit(solution)/shard_map/ppermute | solution.py:63
  95.6 41.5 %collective-permute-start.25 = (bf16[2,320,640]{2,1,0:T(8,128)(2,1)S(1)}, bf16[2,320,640]{2,1,0:T(8,128)(2,1)S(1)}, u32[]{:S(2)}, u32[]{:S(2)}) collective-permute-start(bf16[2,320,640]{2,1,0:T(8,128)(2,1)S(1)} %pad_maximum_fusion.1.refs_4_), channel_id=1, source_target_pairs={{0,4},{4,0},{8,12},{12,8},{16,20},{20,16},{24,28},{28,24},{1,5},{5... | collective-permute-start | bytes 2457608 | tf_op jit(solution)/shard_map/ppermute | solution.py:69
  107.8 23.4 %copy-start.36 = (f32[4,640]{1,0:T(4,128)S(1)}, f32[4,640]{1,0:T(4,128)}, u32[]{:S(2)}) copy-start(f32[4,640]{1,0:T(4,128)} %param.14) | copy-start | bytes 30724
  107.8 1.6 collective-permute-start.21
  107.9 5.9 %collective-permute-start.22 = (f32[24,1024]{1,0:T(8,128)}, f32[24,1024]{1,0:T(8,128)S(1)}, u32[]{:S(2)}, u32[]{:S(2)}) collective-permute-start(f32[24,1024]{1,0:T(8,128)} %get-tuple-element.171.refs_0_), channel_id=1, source_target_pairs={{0,2},{1,3},{2,0},{3,1},{4,6},{5,7},{6,4},{7,5},{8,10},{9,11},{10,... | collective-permute-start | bytes 294920 | tf_op jit(solution)/shard_map/ppermute | solution.py:33
  109.4 9.0 %copy-start.29 = (f32[24,1024]{1,0:T(8,128)}, f32[24,1024]{1,0:T(8,128)S(1)}, u32[]{:S(2)}) copy-start(f32[24,1024]{1,0:T(8,128)S(1)} %collective-permute-done.21.refs_1_) | copy-start | bytes 294916
  109.4 5.5 %collective-permute-start.23 = (f32[24,1024]{1,0:T(8,128)}, f32[24,1024]{1,0:T(8,128)S(1)}, u32[]{:S(2)}, u32[]{:S(2)}) collective-permute-start(f32[24,1024]{1,0:T(8,128)} %get-tuple-element.171.refs_0_), channel_id=1, source_target_pairs={{0,3},{1,2},{2,1},{3,0},{4,7},{5,6},{6,5},{7,4},{8,11},{9,10},{10,... | collective-permute-start | bytes 294920 | tf_op jit(solution)/shard_map/ppermute | solution.py:33
  115.0 40.3 %collective-permute-start.31 = (bf16[1024,640]{1,0:T(8,128)(2,1)}, bf16[1024,640]{1,0:T(8,128)(2,1)}, u32[]{:S(2)}, u32[]{:S(2)}) collective-permute-start(bf16[1024,640]{1,0:T(8,128)(2,1)} %get-tuple-element.198.refs_0_), channel_id=1, source_target_pairs={{0,2},{1,3},{2,0},{3,1},{4,6},{5,7},{6,4},{7,5},{8,10},{9,11},{10,... | collective-permute-start | bytes 3932168 | tf_op jit(solution)/shard_map/ppermute | solution.py:33
  116.4 19.4 %copy-start.22 = (bf16[320,640]{1,0:T(8,128)(2,1)}, bf16[320,640]{1,0:T(8,128)(2,1)S(1)}, u32[]{:S(2)}) copy-start(bf16[320,640]{1,0:T(8,128)(2,1)S(1)} %collective-permute-done.28) | copy-start | bytes 1228804
  116.4 20.6 %collective-permute-start.29 = (bf16[1,320,640]{2,1,0:T(8,128)(2,1)S(1)}, bf16[1,320,640]{2,1,0:T(8,128)(2,1)S(1)}, u32[]{:S(2)}, u32[]{:S(2)}) collective-permute-start(bf16[1,320,640]{2,1,0:T(8,128)(2,1)S(1)} %bitcast.83), channel_id=1, source_target_pairs={{0,4},{4,0},{8,12},{12,8},{16,20},{20,16},{24,28},{28,24},{1,5},{5... | collective-permute-start | bytes 1228808 | tf_op jit(solution)/shard_map/ppermute | solution.py:69
  118.0 17.8 %copy-start.23 = (bf16[320,640]{1,0:T(8,128)(2,1)}, bf16[320,640]{1,0:T(8,128)(2,1)S(1)}, u32[]{:S(2)}) copy-start(bf16[320,640]{1,0:T(8,128)(2,1)S(1)} %collective-permute-done.26) | copy-start | bytes 1228804
  118.0 19.1 %collective-permute-start.27 = (bf16[1,320,640]{2,1,0:T(8,128)(2,1)S(1)}, bf16[1,320,640]{2,1,0:T(8,128)(2,1)S(1)}, u32[]{:S(2)}, u32[]{:S(2)}) collective-permute-start(bf16[1,320,640]{2,1,0:T(8,128)(2,1)S(1)} %bitcast.85), channel_id=1, source_target_pairs={{0,4},{4,0},{8,12},{12,8},{16,20},{20,16},{24,28},{28,24},{1,5},{5... | collective-permute-start | bytes 1228808 | tf_op jit(solution)/shard_map/ppermute | solution.py:69
  129.7 7.4 %collective-permute-start.24 = (f32[8,640]{1,0:T(8,128)}, f32[8,640]{1,0:T(8,128)S(1)}, u32[]{:S(2)}, u32[]{:S(2)}) collective-permute-start(f32[8,640]{1,0:T(8,128)} %get-tuple-element.175), channel_id=1, source_target_pairs={{4,0},{8,4},{12,8},{16,12},{20,16},{24,20},{28,24},{5,1},{9,5},{13... | collective-permute-start | bytes 61448 | tf_op jit(solution)/shard_map/ppermute | solution.py:74
  137.1 19.7 %collective-permute-start.30 = (bf16[2,320,640]{2,1,0:T(8,128)(2,1)}, bf16[2,320,640]{2,1,0:T(8,128)(2,1)S(1)}, u32[]{:S(2)}, u32[]{:S(2)}) collective-permute-start(bf16[2,320,640]{2,1,0:T(8,128)(2,1)} %shard_map.174), channel_id=1, source_target_pairs={{0,4},{4,0},{8,12},{12,8},{16,20},{20,16},{24,28},{28,24},{1,5},{5... | collective-permute-start | bytes 2457608 | tf_op jit(solution)/shard_map/ppermute | solution.py:69
  146.6 8.6 %collective-permute-start.32 = (f32[24,640]{1,0:T(8,128)S(1)}, f32[24,640]{1,0:T(8,128)S(1)}, u32[]{:S(2)}, u32[]{:S(2)}) collective-permute-start(f32[24,640]{1,0:T(8,128)S(1)} %copy-done.33), channel_id=1, source_target_pairs={{0,8},{4,12},{8,16},{12,20},{16,24},{20,28},{24,0},{28,4},{1,9},{5... | collective-permute-start | bytes 184328 | tf_op jit(solution)/shard_map/ppermute | solution.py:63
  148.2 7.1 %collective-permute-start.33 = (f32[24,640]{1,0:T(8,128)S(1)}, f32[24,640]{1,0:T(8,128)S(1)}, u32[]{:S(2)}, u32[]{:S(2)}) collective-permute-start(f32[24,640]{1,0:T(8,128)S(1)} %copy-done.33), channel_id=1, source_target_pairs={{0,16},{4,20},{8,24},{12,28},{16,0},{20,4},{24,8},{28,12},{1,17},{... | collective-permute-start | bytes 184328 | tf_op jit(solution)/shard_map/ppermute | solution.py:63
  150.4 4.8 %collective-permute-start.34 = (f32[24,640]{1,0:T(8,128)S(1)}, f32[24,640]{1,0:T(8,128)S(1)}, u32[]{:S(2)}, u32[]{:S(2)}) collective-permute-start(f32[24,640]{1,0:T(8,128)S(1)} %copy-done.33), channel_id=1, source_target_pairs={{0,24},{4,28},{8,0},{12,4},{16,8},{20,12},{24,16},{28,20},{1,25},{... | collective-permute-start | bytes 184328 | tf_op jit(solution)/shard_map/ppermute | solution.py:63
  156.8 7.7 %collective-permute-start.37 = (bf16[1024,640]{1,0:T(8,128)(2,1)S(1)}, bf16[1024,640]{1,0:T(8,128)(2,1)S(1)}, u32[]{:S(2)}, u32[]{:S(2)}) collective-permute-start(bf16[1024,640]{1,0:T(8,128)(2,1)S(1)} %copy-done.17), channel_id=1, source_target_pairs={{0,1},{1,0},{2,3},{3,2},{4,5},{5,4},{6,7},{7,6},{8,9},{9,8},{10,11... | collective-permute-start | bytes 3932168 | tf_op jit(solution)/shard_map/ppermute | solution.py:33
  156.8 9.4 %collective-permute-start.38 = (bf16[1024,640]{1,0:T(8,128)(2,1)}, bf16[1024,640]{1,0:T(8,128)(2,1)}, u32[]{:S(2)}, u32[]{:S(2)}) collective-permute-start(bf16[1024,640]{1,0:T(8,128)(2,1)} %collective-permute-done.31.refs_2_), channel_id=1, source_target_pairs={{0,1},{1,0},{2,3},{3,2},{4,5},{5,4},{6,7},{7,6},{8,9},{9,8},{10,11... | collective-permute-start | bytes 3932168 | tf_op jit(solution)/shard_map/ppermute | solution.py:33
  157.3 20.9 %collective-permute-start.35 = (bf16[2,320,640]{2,1,0:T(8,128)(2,1)S(1)}, bf16[2,320,640]{2,1,0:T(8,128)(2,1)}, u32[]{:S(2)}, u32[]{:S(2)}) collective-permute-start(bf16[2,320,640]{2,1,0:T(8,128)(2,1)S(1)} %shard_map.175), channel_id=1, source_target_pairs={{0,4},{4,0},{8,12},{12,8},{16,20},{20,16},{24,28},{28,24},{1,5},{5... | collective-permute-start | bytes 2457608 | tf_op jit(solution)/shard_map/ppermute | solution.py:69
  159.8 17.4 %collective-permute-start.36 = (bf16[320,640]{1,0:T(8,128)(2,1)}, bf16[320,640]{1,0:T(8,128)(2,1)}, u32[]{:S(2)}, u32[]{:S(2)}) collective-permute-start(bf16[320,640]{1,0:T(8,128)(2,1)} %get-tuple-element.259), channel_id=1, source_target_pairs={{0,8},{4,12},{8,16},{12,20},{16,24},{20,28},{24,0},{28,4},{1,9},{5... | collective-permute-start | bytes 1228808 | tf_op jit(solution)/shard_map/ppermute | solution.py:63
  161.8 34.4 %collective-permute-start.41 = (bf16[320,640]{1,0:T(8,128)(2,1)}, bf16[320,640]{1,0:T(8,128)(2,1)}, u32[]{:S(2)}, u32[]{:S(2)}) collective-permute-start(bf16[320,640]{1,0:T(8,128)(2,1)} %get-tuple-element.258), channel_id=1, source_target_pairs={{0,24},{4,28},{8,0},{12,4},{16,8},{20,12},{24,16},{28,20},{1,25},{... | collective-permute-start | bytes 1228808 | tf_op jit(solution)/shard_map/ppermute | solution.py:63
  164.5 18.4 %copy-start.7 = (bf16[1024,640]{1,0:T(8,128)(2,1)S(1)}, bf16[1024,640]{1,0:T(8,128)(2,1)}, u32[]{:S(2)}) copy-start(bf16[1024,640]{1,0:T(8,128)(2,1)} %refs_0_.2) | copy-start | bytes 3932164
  165.5 28.5 %collective-permute-start.42 = (f32[24,640]{1,0:T(8,128)S(1)}, f32[24,640]{1,0:T(8,128)S(1)}, u32[]{:S(2)}, u32[]{:S(2)}) collective-permute-start(f32[24,640]{1,0:T(8,128)S(1)} %add_add_fusion), channel_id=1, source_target_pairs={{0,4},{4,0},{8,12},{12,8},{16,20},{20,16},{24,28},{28,24},{1,5},{5... | collective-permute-start | bytes 184328 | tf_op jit(solution)/shard_map/ppermute | solution.py:69
  178.2 22.4 %collective-permute-start.39 = (bf16[2,320,640]{2,1,0:T(8,128)(2,1)S(1)}, bf16[2,320,640]{2,1,0:T(8,128)(2,1)}, u32[]{:S(2)}, u32[]{:S(2)}) collective-permute-start(bf16[2,320,640]{2,1,0:T(8,128)(2,1)S(1)} %shard_map.176), channel_id=1, source_target_pairs={{0,4},{4,0},{8,12},{12,8},{16,20},{20,16},{24,28},{28,24},{1,5},{5... | collective-permute-start | bytes 2457608 | tf_op jit(solution)/shard_map/ppermute | solution.py:69
  181.6 18.9 %collective-permute-start.40 = (bf16[320,640]{1,0:T(8,128)(2,1)}, bf16[320,640]{1,0:T(8,128)(2,1)}, u32[]{:S(2)}, u32[]{:S(2)}) collective-permute-start(bf16[320,640]{1,0:T(8,128)(2,1)} %fusion.5), channel_id=1, source_target_pairs={{0,8},{4,12},{8,16},{12,20},{16,24},{20,28},{24,0},{28,4},{1,9},{5... | collective-permute-start | bytes 1228808 | tf_op jit(solution)/shard_map/ppermute | solution.py:63
  193.0 5.9 %collective-permute-start.43 = (f32[16,640]{1,0:T(8,128)S(1)}, f32[16,640]{1,0:T(8,128)S(1)}, u32[]{:S(2)}, u32[]{:S(2)}) collective-permute-start(f32[16,640]{1,0:T(8,128)S(1)} %fusion.27), channel_id=1, source_target_pairs={{0,8},{4,12},{8,16},{12,20},{16,24},{20,28},{24,0},{28,4},{1,9},{5... | collective-permute-start | bytes 122888 | tf_op jit(solution)/shard_map/ppermute | solution.py:63
  194.0 5.2 %collective-permute-start.44 = (f32[16,640]{1,0:T(8,128)S(1)}, f32[16,640]{1,0:T(8,128)S(1)}, u32[]{:S(2)}, u32[]{:S(2)}) collective-permute-start(f32[16,640]{1,0:T(8,128)S(1)} %fusion.27), channel_id=1, source_target_pairs={{0,16},{4,20},{8,24},{12,28},{16,0},{20,4},{24,8},{28,12},{1,17},{... | collective-permute-start | bytes 122888 | tf_op jit(solution)/shard_map/ppermute | solution.py:63
  196.2 4.4 %collective-permute-start.45 = (f32[16,640]{1,0:T(8,128)S(1)}, f32[16,640]{1,0:T(8,128)S(1)}, u32[]{:S(2)}, u32[]{:S(2)}) collective-permute-start(f32[16,640]{1,0:T(8,128)S(1)} %fusion.27), channel_id=1, source_target_pairs={{0,24},{4,28},{8,0},{12,4},{16,8},{20,12},{24,16},{28,20},{1,25},{... | collective-permute-start | bytes 122888 | tf_op jit(solution)/shard_map/ppermute | solution.py:63
  198.9 11.3 %copy-start.35 = (f32[24,640]{1,0:T(8,128)S(1)}, f32[24,640]{1,0:T(8,128)}, u32[]{:S(2)}) copy-start(f32[24,640]{1,0:T(8,128)} %copy-done.34) | copy-start | bytes 184324
  200.6 21.5 %collective-permute-start.46 = (bf16[2,320,640]{2,1,0:T(8,128)(2,1)S(1)}, bf16[2,320,640]{2,1,0:T(8,128)(2,1)S(1)}, u32[]{:S(2)}, u32[]{:S(2)}) collective-permute-start(bf16[2,320,640]{2,1,0:T(8,128)(2,1)S(1)} %shard_map.177), channel_id=1, source_target_pairs={{0,4},{4,0},{8,12},{12,8},{16,20},{20,16},{24,28},{28,24},{1,5},{5... | collective-permute-start | bytes 2457608 | tf_op jit(solution)/shard_map/ppermute | solution.py:69
  205.0 15.3 %collective-permute-start.47 = (bf16[320,640]{1,0:T(8,128)(2,1)}, bf16[320,640]{1,0:T(8,128)(2,1)S(1)}, u32[]{:S(2)}, u32[]{:S(2)}) collective-permute-start(bf16[320,640]{1,0:T(8,128)(2,1)} %get-tuple-element.257), channel_id=1, source_target_pairs={{0,8},{4,12},{8,16},{12,20},{16,24},{20,28},{24,0},{28,4},{1,9},{5... | collective-permute-start | bytes 1228808 | tf_op jit(solution)/shard_map/ppermute | solution.py:63
  206.0 16.0 %collective-permute-start.48 = (bf16[320,640]{1,0:T(8,128)(2,1)}, bf16[320,640]{1,0:T(8,128)(2,1)}, u32[]{:S(2)}, u32[]{:S(2)}) collective-permute-start(bf16[320,640]{1,0:T(8,128)(2,1)} %get-tuple-element.256), channel_id=1, source_target_pairs={{0,24},{4,28},{8,0},{12,4},{16,8},{20,12},{24,16},{28,20},{1,25},{... | collective-permute-start | bytes 1228808 | tf_op jit(solution)/shard_map/ppermute | solution.py:63
  210.1 7.8 %collective-permute-start.49 = (f32[16,640]{1,0:T(8,128)S(1)}, f32[16,640]{1,0:T(8,128)S(1)}, u32[]{:S(2)}, u32[]{:S(2)}) collective-permute-start(f32[16,640]{1,0:T(8,128)S(1)} %add_add_fusion.1), channel_id=1, source_target_pairs={{0,4},{4,0},{8,12},{12,8},{16,20},{20,16},{24,28},{28,24},{1,5},{5... | collective-permute-start | bytes 122888 | tf_op jit(solution)/shard_map/ppermute | solution.py:69
  210.2 7.7 %collective-permute-start.51 = (f32[16,640]{1,0:T(8,128)S(1)}, f32[16,640]{1,0:T(8,128)}, u32[]{:S(2)}, u32[]{:S(2)}) collective-permute-start(f32[16,640]{1,0:T(8,128)S(1)} %slice.153), channel_id=1, source_target_pairs={{0,2},{1,3},{2,0},{3,1},{4,6},{5,7},{6,4},{7,5},{8,10},{9,11},{10,... | collective-permute-start | bytes 122888 | tf_op jit(solution)/shard_map/ppermute | solution.py:33
  217.9 2.4 %collective-permute-start.50 = (f32[16,640]{1,0:T(8,128)S(1)}, f32[16,640]{1,0:T(8,128)S(1)}, u32[]{:S(2)}, u32[]{:S(2)}) collective-permute-start(f32[16,640]{1,0:T(8,128)S(1)} %slice.153), channel_id=1, source_target_pairs={{0,1},{1,0},{2,3},{3,2},{4,5},{5,4},{6,7},{7,6},{8,9},{9,8},{10,11... | collective-permute-start | bytes 122888 | tf_op jit(solution)/shard_map/ppermute | solution.py:33
  217.9 2.4 %collective-permute-start.52 = (f32[16,640]{1,0:T(8,128)}, f32[16,640]{1,0:T(8,128)S(1)}, u32[]{:S(2)}, u32[]{:S(2)}) collective-permute-start(f32[16,640]{1,0:T(8,128)} %collective-permute-done.51), channel_id=1, source_target_pairs={{0,1},{1,0},{2,3},{3,2},{4,5},{5,4},{6,7},{7,6},{8,9},{9,8},{10,11... | collective-permute-start | bytes 122888 | tf_op jit(solution)/shard_map/ppermute | solution.py:33
  223.4 12.3 %collective-permute-start.53 = (bf16[320,640]{1,0:T(8,128)(2,1)S(1)}, bf16[320,640]{1,0:T(8,128)(2,1)S(1)}, u32[]{:S(2)}, u32[]{:S(2)}) collective-permute-start(bf16[320,640]{1,0:T(8,128)(2,1)S(1)} %get-tuple-element.254), channel_id=1, source_target_pairs={{0,8},{4,12},{8,16},{12,20},{16,24},{20,28},{24,0},{28,4},{1,9},{5... | collective-permute-start | bytes 1228808 | tf_op jit(solution)/shard_map/ppermute | solution.py:63
  (35 other events, 115.8 us)
